TPU v7x, 128 devices: a whole 4x4x4 slice. The times are simulated.
128 devices in a mesh: dp: 4 (over z), segment: 4 (over x), space: 8 (over y, core).
Axes of the slice: x: 4, y: 4, z: 4, core: 2. Of those that a mesh axis runs over, the one named last changes fastest.
Arguments:
- terrain_in: bfloat16 [8, 2, 64, 256], P('dp', None, 'space'), may hold values from -6 to 6
- meso_in: bfloat16 [8, 4, 32, 32, 128], P('dp', None, None, 'space'), may hold values from -6 to 6
- wind_cot: bfloat16 [8, 3, 32, 128], P('dp', None, 'space'), may hold values from -6 to 6
- patch_weight: bfloat16 [256, 8], replicated, may hold values from -2 to 2
- terrain_weight: bfloat16 [256, 2304], replicated, may hold values from -0.125 to 0.125
- lift_weight: bfloat16 [384, 128], replicated, may hold values from -0.5 to 0.5
- meso_weight: bfloat16 [384, 3456], replicated, may hold values from -0.109375 to 0.109375
- merging_weight: bfloat16 [256, 5760], replicated, may hold values from -0.078125 to 0.078125
- decoder_weight: bfloat16 [256, 2304], replicated, may hold values from -0.125 to 0.125
- head_weight: bfloat16 [3, 256], replicated, may hold values from -0.375 to 0.375
Outputs:
- patch_grad: float32 [256, 8], replicated
- terrain_grad: float32 [256, 2304], replicated
- lift_grad: float32 [384, 128], replicated
- meso_grad: float32 [384, 3456], replicated
- merging_grad: float32 [256, 5760], replicated
- decoder_grad: float32 [256, 2304], replicated
- head_grad: float32 [3, 256], replicated
All inputs are finite; a program needn't handle non-finite values.
Results may differ from a plain program's by a relative error of at most 0.017.
Values may be sent and summed in bfloat16 or wider, within the bound.
No kernel may reach another device: no remote copies, remote signals or barrier semaphores. Data moves between devices by JAX's collectives and lax.ppermute only.
A program may use at most 192 MiB of HBM per device.

v0:
```python
import math

import jax
import jax.numpy as jnp
from jax import lax
from jax.sharding import PartitionSpec as P


def for_sending(shard):
    return jax.tree.map(lambda a: a.astype(jnp.bfloat16) if a.dtype == jnp.float32 else a, shard)


def extended(cells, sides, width):
    for axis, dim in sides:
        count = lax.axis_size(axis)
        ends = count - 1
        head = lax.slice_in_dim(cells, 0, width, axis=dim)
        tail = lax.slice_in_dim(cells, cells.shape[dim] - width, cells.shape[dim], axis=dim)
        cells = jnp.concatenate(
            [
                lax.ppermute(tail, axis, [(i, (i + 1) % count) for i in range(ends)]),
                cells,
                lax.ppermute(head, axis, [((i + 1) % count, i) for i in range(ends)]),
            ],
            axis=dim,
        )
    return cells


def shifted(shard, axis, by):
    devices = lax.axis_size(axis)
    pairs = [(i, i + by) for i in range(devices) if 0 <= i + by < devices]
    return lax.ppermute(shard, axis, pairs)


def depth_stack(terrain):
    fields, padded_rows, columns = terrain.shape
    split = terrain.reshape(fields, padded_rows // 2, 2, columns // 2, 2)
    return split.transpose(0, 2, 4, 1, 3).reshape(fields * 4, padded_rows // 2 * (columns // 2))


def silu_slope(pre_act):
    sigma = jax.nn.sigmoid(pre_act)
    return sigma * (1.0 + pre_act * (1.0 - sigma))


def conv_forward(weight, haloed):
    channels, padded_rows, breadth = haloed.shape
    height = padded_rows - 2
    padded = jnp.pad(haloed, ((0, 0), (0, 0), (1, 1)))
    result = jnp.zeros((weight.shape[0], height * breadth), jnp.float32)
    for tap_index in range(9):
        row_shift = tap_index // 3
        column_shift = tap_index % 3
        window = padded[
            :, row_shift : row_shift + height, column_shift : column_shift + breadth
        ].reshape(channels, height * breadth)
        result = result + jnp.dot(
            weight[:, tap_index * channels : (tap_index + 1) * channels],
            window,
            preferred_element_type=jnp.float32,
        )
    return result.reshape(weight.shape[0], height, breadth)


def conv_input_grad(weight, haloed_delta):
    outputs, padded_rows, breadth = haloed_delta.shape
    height = padded_rows - 2
    channels = weight.shape[1] // 9
    padded = jnp.pad(haloed_delta, ((0, 0), (0, 0), (1, 1)))
    result = jnp.zeros((channels, height * breadth), jnp.float32)
    for tap_index in range(9):
        row_shift = 2 - tap_index // 3
        column_shift = 2 - tap_index % 3
        window = padded[
            :, row_shift : row_shift + height, column_shift : column_shift + breadth
        ].reshape(outputs, height * breadth)
        result = result + lax.dot_general(
            weight[:, tap_index * channels : (tap_index + 1) * channels],
            window,
            (((0,), (0,)), ((), ())),
            preferred_element_type=jnp.float32,
        )
    return result.reshape(channels, height, breadth)


def conv_weight_grad(back_delta, haloed_source):
    outputs, height, breadth = back_delta.shape
    channels = haloed_source.shape[0]
    padded = jnp.pad(haloed_source, ((0, 0), (0, 0), (1, 1)))
    delta_flat = back_delta.reshape(outputs, height * breadth)
    pieces = []
    for tap_index in range(9):
        row_shift = tap_index // 3
        column_shift = tap_index % 3
        window = padded[
            :, row_shift : row_shift + height, column_shift : column_shift + breadth
        ].reshape(channels, height * breadth)
        pieces.append(
            lax.dot_general(
                delta_flat, window, (((1,), (1,)), ((), ())), preferred_element_type=jnp.float32
            )
        )
    return jnp.concatenate(pieces, axis=1)


def local(
    terrain_in,
    meso_in,
    wind_cot,
    patch_weight,
    terrain_weight,
    lift_weight,
    meso_weight,
    merging_weight,
    decoder_weight,
    head_weight,
):
    micro_count = terrain_in.shape[0]
    height = meso_in.shape[3]
    breadth = meso_in.shape[4]
    cell_count = height * breadth
    level_chans = meso_in.shape[1] * meso_in.shape[2]
    terr_chans = patch_weight.shape[0]
    meso_chans = lift_weight.shape[0]
    mix_chans = merging_weight.shape[0]
    joint_chans = terr_chans + meso_chans
    wind_chans = head_weight.shape[0]
    grad_scale = 1.0 / math.sqrt(
        micro_count * lax.axis_size("dp") * height * lax.axis_size("space") * breadth
    )
    segment_index = lax.axis_index("segment")
    bf16 = jnp.bfloat16
    tick_count = micro_count + 3

    def blank_field(channels, dtype):
        return jnp.zeros((channels, height, breadth), dtype)

    def blank_slots():
        return (
            blank_field(terr_chans, bf16),
            blank_field(meso_chans, bf16),
            blank_field(mix_chans, bf16),
        )

    def widen_pre(pre_act):
        return jnp.concatenate(
            [pre_act, blank_field(meso_chans - pre_act.shape[0], jnp.float32)], axis=0
        )

    def widen_delta(back_delta):
        if back_delta.shape[0] < meso_chans:
            return jnp.concatenate(
                [back_delta, blank_field(meso_chans - back_delta.shape[0], bf16)], axis=0
            )
        return back_delta

    received = blank_slots()
    saved_front = []
    saved_pre = []
    for tick in range(tick_count):

        def front_terrain(slots):
            if tick < micro_count:
                terrain_act = jnp.dot(
                    patch_weight, depth_stack(terrain_in[tick]), preferred_element_type=jnp.float32
                ).astype(bf16)
                return jnp.concatenate(
                    [
                        terrain_act.reshape(terr_chans, height, breadth),
                        blank_field(meso_chans, bf16),
                    ],
                    axis=0,
                )
            return blank_field(joint_chans, bf16)

        def front_meso(slots):
            if 1 <= tick <= micro_count:
                meso_flat = meso_in[tick - 1].reshape(level_chans, cell_count)
                meso_act = jnp.dot(
                    lift_weight, meso_flat, preferred_element_type=jnp.float32
                ).astype(bf16)
                return jnp.concatenate(
                    [meso_act.reshape(meso_chans, height, breadth), blank_field(terr_chans, bf16)],
                    axis=0,
                )
            return blank_field(joint_chans, bf16)

        def front_merging(slots):
            if 2 <= tick <= micro_count + 1:
                return jnp.concatenate([slots[0], slots[1]], axis=0)
            return blank_field(joint_chans, bf16)

        def front_decoder(slots):
            if 3 <= tick <= micro_count + 2:
                return jnp.concatenate(
                    [slots[2], blank_field(joint_chans - mix_chans, bf16)], axis=0
                )
            return blank_field(joint_chans, bf16)

        front = lax.switch(
            segment_index, [front_terrain, front_meso, front_merging, front_decoder], received
        )
        haloed = extended(for_sending(front), (("space", 1),), 1).astype(front.dtype)

        def empty_outputs():
            return (blank_field(meso_chans, jnp.float32), blank_slots())

        def apply_terrain(operands):
            source, slots = operands
            if tick < micro_count:
                pre_act = conv_forward(terrain_weight, source[:terr_chans])
                return (
                    widen_pre(pre_act),
                    (
                        jax.nn.silu(pre_act).astype(bf16),
                        blank_field(meso_chans, bf16),
                        blank_field(mix_chans, bf16),
                    ),
                )
            return empty_outputs()

        def apply_meso(operands):
            source, slots = operands
            if 1 <= tick <= micro_count:
                pre_act = conv_forward(meso_weight, source[:meso_chans])
                return (
                    pre_act,
                    (slots[0], jax.nn.silu(pre_act).astype(bf16), blank_field(mix_chans, bf16)),
                )
            return empty_outputs()

        def apply_merging(operands):
            source, slots = operands
            if 2 <= tick <= micro_count + 1:
                pre_act = conv_forward(merging_weight, source)
                return (
                    widen_pre(pre_act),
                    (
                        blank_field(terr_chans, bf16),
                        blank_field(meso_chans, bf16),
                        jax.nn.silu(pre_act).astype(bf16),
                    ),
                )
            return empty_outputs()

        def apply_decoder(operands):
            source, slots = operands
            if 3 <= tick <= micro_count + 2:
                pre_act = conv_forward(decoder_weight, source[:mix_chans])
                return (widen_pre(pre_act), blank_slots())
            return empty_outputs()

        pre_act, outgoing = lax.switch(
            segment_index,
            [apply_terrain, apply_meso, apply_merging, apply_decoder],
            (haloed, received),
        )
        saved_front.append(haloed)
        saved_pre.append(pre_act)
        if tick < micro_count + 2:
            received = shifted(
                (for_sending(outgoing[0]), for_sending(outgoing[1]), for_sending(outgoing[2])),
                "segment",
                1,
            )
    grad_sums = tuple(
        (
            jnp.zeros(weight.shape, jnp.float32)
            for weight in (
                patch_weight,
                terrain_weight,
                lift_weight,
                meso_weight,
                merging_weight,
                decoder_weight,
                head_weight,
            )
        )
    )
    head_blank = jnp.zeros(head_weight.shape, jnp.float32)
    received = blank_slots()
    for tick in range(tick_count):

        def delta_terrain(slots):
            if 3 <= tick <= micro_count + 2:
                pre_act = saved_pre[tick - 3][:terr_chans]
                return (widen_delta((silu_slope(pre_act) * slots[0]).astype(bf16)), head_blank)
            return (blank_field(meso_chans, bf16), head_blank)

        def delta_meso(slots):
            if 2 <= tick <= micro_count + 1:
                pre_act = saved_pre[tick - 1]
                return ((silu_slope(pre_act) * slots[1]).astype(bf16), head_blank)
            return (blank_field(meso_chans, bf16), head_blank)

        def delta_merging(slots):
            if 1 <= tick <= micro_count:
                pre_act = saved_pre[tick + 1][:mix_chans]
                return (widen_delta((silu_slope(pre_act) * slots[2]).astype(bf16)), head_blank)
            return (blank_field(meso_chans, bf16), head_blank)

        def delta_decoder(slots):
            if tick < micro_count:
                pre_act = saved_pre[tick + 3][:mix_chans]
                decoder_out = jax.nn.silu(pre_act).astype(bf16)
                cot_flat = wind_cot[tick].reshape(wind_chans, cell_count)
                head_part = grad_scale * lax.dot_general(
                    cot_flat,
                    decoder_out.reshape(mix_chans, cell_count),
                    (((1,), (1,)), ((), ())),
                    preferred_element_type=jnp.float32,
                )
                decoder_back = grad_scale * lax.dot_general(
                    head_weight,
                    cot_flat,
                    (((0,), (0,)), ((), ())),
                    preferred_element_type=jnp.float32,
                )
                back_delta = (
                    silu_slope(pre_act) * decoder_back.reshape(mix_chans, height, breadth)
                ).astype(bf16)
                return (widen_delta(back_delta), head_part)
            return (blank_field(meso_chans, bf16), head_blank)

        back_field, head_part = lax.switch(
            segment_index, [delta_terrain, delta_meso, delta_merging, delta_decoder], received
        )
        grad_sums = grad_sums[:6] + (grad_sums[6] + head_part,)
        haloed_back = extended(for_sending(back_field), (("space", 1),), 1).astype(back_field.dtype)

        def spare_outputs(operands):
            return (operands[0], blank_slots())

        def grads_terrain(operands):
            if 3 <= tick <= micro_count + 2:
                sums, halo_delta, slots = operands
                sample = tick - 3
                delta_part = halo_delta[:terr_chans]
                terrain_part = conv_weight_grad(
                    delta_part[:, 1:-1], saved_front[tick - 3][:terr_chans]
                )
                terrain_back = conv_input_grad(terrain_weight, delta_part).astype(bf16)
                patch_part = lax.dot_general(
                    terrain_back.reshape(terr_chans, cell_count),
                    depth_stack(terrain_in[sample]),
                    (((1,), (1,)), ((), ())),
                    preferred_element_type=jnp.float32,
                )
                sums = (sums[0] + patch_part, sums[1] + terrain_part) + sums[2:]
                return (sums, blank_slots())
            return spare_outputs(operands)

        def grads_meso(operands):
            if 2 <= tick <= micro_count + 1:
                sums, halo_delta, slots = operands
                sample = tick - 2
                meso_part = conv_weight_grad(
                    halo_delta[:, 1:-1], saved_front[tick - 1][:meso_chans]
                )
                meso_back = conv_input_grad(meso_weight, halo_delta).astype(bf16)
                meso_flat = meso_in[sample].reshape(level_chans, cell_count)
                lift_part = lax.dot_general(
                    meso_back.reshape(meso_chans, cell_count),
                    meso_flat,
                    (((1,), (1,)), ((), ())),
                    preferred_element_type=jnp.float32,
                )
                sums = sums[:2] + (sums[2] + lift_part, sums[3] + meso_part) + sums[4:]
                return (
                    sums,
                    (slots[0], blank_field(meso_chans, bf16), blank_field(mix_chans, bf16)),
                )
            return spare_outputs(operands)

        def grads_merging(operands):
            if 1 <= tick <= micro_count:
                sums, halo_delta, slots = operands
                delta_part = halo_delta[:mix_chans]
                merging_part = conv_weight_grad(delta_part[:, 1:-1], saved_front[tick + 1])
                joined_back = conv_input_grad(merging_weight, delta_part).astype(bf16)
                sums = sums[:4] + (sums[4] + merging_part,) + sums[5:]
                return (
                    sums,
                    (
                        joined_back[:terr_chans],
                        joined_back[terr_chans:],
                        blank_field(mix_chans, bf16),
                    ),
                )
            return spare_outputs(operands)

        def grads_decoder(operands):
            if tick < micro_count:
                sums, halo_delta, slots = operands
                delta_part = halo_delta[:mix_chans]
                decoder_part = conv_weight_grad(
                    delta_part[:, 1:-1], saved_front[tick + 3][:mix_chans]
                )
                merging_back = conv_input_grad(decoder_weight, delta_part).astype(bf16)
                sums = sums[:5] + (sums[5] + decoder_part, sums[6])
                return (
                    sums,
                    (blank_field(terr_chans, bf16), blank_field(meso_chans, bf16), merging_back),
                )
            return spare_outputs(operands)

        grad_sums, outgoing = lax.switch(
            segment_index,
            [grads_terrain, grads_meso, grads_merging, grads_decoder],
            (grad_sums, haloed_back, received),
        )
        if tick < micro_count + 2:
            received = shifted(
                (for_sending(outgoing[0]), for_sending(outgoing[1]), for_sending(outgoing[2])),
                "segment",
                -1,
            )
    summed = lax.psum(grad_sums, ("dp", "segment", "space"))
    return tuple(summed)


def solution(mesh):
    placed = (
        P("dp", None, "space", None),
        P("dp", None, None, "space", None),
        P("dp", None, "space", None),
        P(),
        P(),
        P(),
        P(),
        P(),
        P(),
        P(),
    )
    return jax.shard_map(
        local,
        mesh=mesh,
        in_specs=placed,
        out_specs=(P(), P(), P(), P(), P(), P(), P()),
        check_vma=False,
    )
```

profile of v0, /device:TPU:1, one launch (start us, length us, event | category | flops | bytes accessed | tf_op | source)
XLA Modules:
  0.0 742.3 jit_solution(4936908705955048565)
XLA Ops:
  11.8 4.6 collective-permute-start.2
  32.0 6.9 conditional.22
  45.3 8.0 %conditional.23 = (f32[384,4,128]{0,2,1:T(8,128)}, bf16[256,4,128]{0,2,1:T(8,128)(2,1)S(1)}, bf16[384,4,128]{2,1,0:T(4,128)(2,1)S(1)}) conditional(s32[]{:T(128)} %clamp.2, (bf16[640,6,128]{2,0,1:T(8,128)(2,1)}, bf16[256,2304]{1,0:T(8,128)(2,1)S(1)}) %tuple.663, (bf16[640,6,128]{2,0,1:T(8,128)(2,1)}, ...), branch_computations={%region_12.13_spmd, %region_13.14_spmd, %region_14.15_spmd, %regio... | conditional | flops 1361510400 | bytes 41910324 | solution.py:254
  53.3 7.5 %collective-permute-start.6 = (bf16[384,4,128]{2,1,0:T(4,128)(2,1)S(1)}, bf16[384,4,128]{2,1,0:T(4,128)(2,1)S(1)}, u32[]{:S(2)}, u32[]{:S(2)}) collective-permute-start(bf16[384,4,128]{2,1,0:T(4,128)(2,1)S(1)} %get-tuple-element.390), channel_id=1, source_target_pairs={{0,8},{8,16},{16,24},{1,9},{9,17},{17,25},{2,10},{10,18},{18,26},{... | collective-permute-start | bytes 1179656 | tf_op jit(solution)/shard_map/ppermute | solution.py:33
  62.9 12.3 %collective-permute-done.5 = bf16[256,4,128]{2,1,0:T(4,128)(2,1)S(1)} collective-permute-done((bf16[256,4,128]{2,1,0:T(4,128)(2,1)S(1)}, bf16[256,4,128]{2,1,0:T(4,128)(2,1)S(1)}, u32[]{:S(2)}, u32[]{:S(2)}) %collective-permute-start.5) | collective-permute-done | bytes 262176 | tf_op jit(solution)/shard_map/ppermute | solution.py:33
  87.0 10.0 %conditional.25 = (f32[384,4,128]{0,2,1:T(8,128)}, bf16[256,4,128]{2,1,0:T(4,128)(2,1)S(1)}, bf16[384,4,128]{2,1,0:T(4,128)(2,1)S(1)}, bf16[256,4,128]{2,1,0:T(4,128)(2,1)S(1)}) conditional(s32[]{:T(128)} %clamp.2, () %tuple.309, (bf16[640,6,128]{2,0,1:T(8,128)(2,1)S(1)}, bf16[384,3456]{1,0:T(8,128)(2,1)S(1)}, ...), branch_computations={%region_20.21_spmd, %region_21.22_spmd, %region_22.23_spmd, %regio... | conditional | flops 1511653376 | bytes 43974720 | solution.py:254
  97.0 13.0 %collective-permute-start.10 = (bf16[384,4,128]{2,1,0:T(4,128)(2,1)S(1)}, bf16[384,4,128]{2,1,0:T(4,128)(2,1)S(1)}, u32[]{:S(2)}, u32[]{:S(2)}) collective-permute-start(bf16[384,4,128]{2,1,0:T(4,128)(2,1)S(1)} %get-tuple-element.392), channel_id=1, source_target_pairs={{0,8},{8,16},{16,24},{1,9},{9,17},{17,25},{2,10},{10,18},{18,26},{... | collective-permute-start | bytes 1179656 | tf_op jit(solution)/shard_map/ppermute | solution.py:33
  113.8 10.6 %collective-permute-done.9 = bf16[256,4,128]{2,1,0:T(4,128)(2,1)S(1)} collective-permute-done((bf16[256,4,128]{2,1,0:T(4,128)(2,1)S(1)}, bf16[256,4,128]{2,1,0:T(4,128)(2,1)S(1)}, u32[]{:S(2)}, u32[]{:S(2)}) %collective-permute-start.9) | collective-permute-done | bytes 262176 | tf_op jit(solution)/shard_map/ppermute | solution.py:33
  128.0 5.5 collective-permute-start.12
  142.1 4.8 collective-permute-start.17
  174.7 4.8 collective-permute-start.20
  185.5 15.2 %conditional.33 = (f32[256,5760]{1,0:T(8,128)}, f32[256,2304]{0,1:T(8,128)}, bf16[384,4,128]{2,1,0:T(4,128)(2,1)}, f32[256,5760]{0,1:T(8,128)}, bf16[256,4,128]{...) conditional(s32[]{:T(128)} %clamp.2, ...), branch_computations={%region_52.53_spmd, %region_53.54_spmd, %region_54.55_spmd, %regio... | conditional | flops 3022848000 | bytes 74121320 | solution.py:408
  203.2 16.5 %collective-permute-done.23 = bf16[256,4,128]{2,1,0:T(4,128)(2,1)S(1)} collective-permute-done((bf16[256,4,128]{2,1,0:T(4,128)(2,1)S(1)}, bf16[256,4,128]{2,1,0:T(4,128)(2,1)S(1)}, u32[]{:S(2)}, u32[]{:S(2)}) %collective-permute-start.23) | collective-permute-done | bytes 262176 | tf_op jit(solution)/shard_map/ppermute | solution.py:33
  220.2 4.7 collective-permute-start.24
  232.2 70.3 %collective-permute-done.26 = bf16[256,4,128]{0,2,1:T(8,128)(2,1)S(1)} collective-permute-done((bf16[256,4,128]{0,2,1:T(8,128)(2,1)}, bf16[256,4,128]{0,2,1:T(8,128)(2,1)S(1)}, u32[]{:S(2)}, u32[]{:S(2)}) %collective-permute-start.26) | collective-permute-done | bytes 262176 | tf_op jit(solution)/shard_map/ppermute | solution.py:33
  302.5 10.7 %conditional.35 = (f32[384,128]{1,0:T(8,128)}, f32[384,3456]{1,0:T(8,128)}, f32[256,5760]{0,1:T(8,128)}, bf16[256,4,128]{0,2,1:T(8,128)(2,1)S(1)}, bf16[384,4,128]{0,2,1:T(8,128)(2,1)S(1)}) conditional(s32[]{:T(128)} %clamp.2, f32[256,5760]{0,1:T(8,128)} %get-tuple-element.641, (bf16[384,6,128]{2,0,1:T(8,128)(2,1)S(1)}, ...), branch_computations={%region_60.61_spmd, %region_61.62_spmd, %region_62.63_spmd, %regio... | conditional | flops 3024322560 | bytes 120782944 | solution.py:408
  316.3 48.1 %collective-permute-done.27 = bf16[256,4,128]{2,1,0:T(4,128)(2,1)S(1)} collective-permute-done((bf16[256,4,128]{2,1,0:T(4,128)(2,1)S(1)}, bf16[256,4,128]{2,1,0:T(4,128)(2,1)S(1)}, u32[]{:S(2)}, u32[]{:S(2)}) %collective-permute-start.27) | collective-permute-done | bytes 262176 | tf_op jit(solution)/shard_map/ppermute | solution.py:33
  378.4 60.0 %conditional.37 = (f32[256,8]{1,0:T(8,128)S(1)}, f32[256,2304]{1,0:T(8,128)S(1)}, f32[384,128]{1,0:T(8,128)}, bf16[256,4,128]{2,1,0:T(4,128)(2,1)S(1)}, f32[384,3456]{1,0:T(8,128)}) conditional(s32[]{:T(128)} %clamp.2, (bf16[384,6,128]{2,1,0:T(8,128)(2,1)S(1)}, bf16[256,2304]{1,0:T(8,128)(2,1)}, ...), branch_computations={%region_68.69_spmd, %region_69.70_spmd, %region_70.71_spmd, %regio... | conditional | flops 2771386368 | bytes 117481664 | solution.py:408
  439.7 5.8 collective-permute-done.31
  457.4 6.4 copy.303
  465.4 36.0 %conditional.39 = (f32[256,8]{0,1:T(8,128)S(1)}, f32[256,2304]{1,0:T(8,128)S(1)}) conditional(s32[]{:T(128)} %clamp.2, (bf16[384,6,128]{2,0,1:T(8,128)(2,1)S(1)}, bf16[256,2304]{1,0:T(8,128)(2,1)}, bf16[2,2,8,256]{3,2,1,0:T(8,128)(2,1)S(1)}, f32[256,8]{1,0:T(8,128)S(1)}, bf16[640,6,128]{2,0,1:T(8,128)(2,1)}, ...), branch_computations={%region_76.77_spmd, %region_77.78_spmd, %region_78.79_spmd, %regio... | conditional | flops 1211828224 | bytes 61825152 | solution.py:408
  502.9 66.4 %all-reduce.42 = (f32[256,8]{0,1:T(8,128)}, f32[3,256]{1,0:T(4,128)}) all-reduce(f32[256,8]{0,1:T(8,128)S(1)} %get-tuple-element.412, f32[3,256]{1,0:T(4,128)S(1)} %add.573), channel_id=1, replica_groups=mesh['dp'=4,'segment'=4,'space'=8] {'dp','segment','space'}, use_global_device_ids=true, to_apply=%region_80.81 | all-reduce | flops 2816 | bytes 22528 | tf_op jit(solution)/shard_map/psum | solution.py:419
  569.3 151.4 %all-reduce.46.cloned.1.call-done = (f32[256,2304]{1,0:T(8,128)}, f32[384,128]{1,0:T(8,128)}, f32[384,3456]{1,0:T(8,128)}, f32[256,5760]{1,0:T(8,128)}, f32[256,2304]{1,0:T(8,128)}) async-done(((f32[256,2304]{1,0:T(8,128)}, f32[384,128]{1,0:T(8,128)}, f32[384,3456]{1,0:T(8,128)}, f32[256,5760]{1,0:T(8,128)}, f32[256,2304]{1,0:T(8,128)}), (f32[256,2304]{1,0:T(8,128)}, f32[384,128]{1,0:T(8,128)}, ...) | async-done | bytes 16121872 | tf_op jit(solution)/shard_map/psum | solution.py:419
  724.6 5.6 copy.1213
  (333 shorter events, 272.2 us)
Async XLA Ops:
  7.2 713.5 %all-reduce.46.cloned.1.call-start = ((), (), s32[]{:S(2)}) async-start(), calls=%async_computation | async-start | bytes 32243712 | tf_op jit(solution)/shard_map/psum | solution.py:419
  11.8 17.9 %collective-permute-start.2 = (bf16[640,1,128]{2,0,1:T(8,128)(2,1)}, bf16[640,1,128]{2,0,1:T(8,128)(2,1)S(1)}, u32[]{:S(2)}, u32[]{:S(2)}) collective-permute-start(bf16[640,1,128]{2,0,1:T(8,128)(2,1)} %copy.942), channel_id=1, source_target_pairs={{0,1},{1,2},{2,3},{3,4},{4,5},{5,6},{6,7},{8,9},{9,10},{10,11},{11... | collective-permute-start | bytes 491528 | tf_op jit(solution)/shard_map/ppermute | solution.py:21
  17.0 14.3 %collective-permute-start.3 = (bf16[640,1,128]{2,0,1:T(8,128)(2,1)}, bf16[640,1,128]{2,0,1:T(8,128)(2,1)S(1)}, u32[]{:S(2)}, u32[]{:S(2)}) collective-permute-start(bf16[640,1,128]{2,0,1:T(8,128)(2,1)} %copy.943), channel_id=1, source_target_pairs={{1,0},{2,1},{3,2},{4,3},{5,4},{6,5},{7,6},{9,8},{10,9},{11,10},{12... | collective-permute-start | bytes 491528 | tf_op jit(solution)/shard_map/ppermute | solution.py:23
  23.5 16.8 %collective-permute-start = (bf16[640,1,128]{2,0,1:T(8,128)(2,1)}, bf16[640,1,128]{2,0,1:T(8,128)(2,1)}, u32[]{:S(2)}, u32[]{:S(2)}) collective-permute-start(bf16[640,1,128]{2,0,1:T(8,128)(2,1)} %copy.940), channel_id=1, source_target_pairs={{0,1},{1,2},{2,3},{3,4},{4,5},{5,6},{6,7},{8,9},{9,10},{10,11},{11... | collective-permute-start | bytes 491528 | tf_op jit(solution)/shard_map/ppermute | solution.py:21
  27.8 15.0 %collective-permute-start.1 = (bf16[640,1,128]{2,0,1:T(8,128)(2,1)}, bf16[640,1,128]{2,0,1:T(8,128)(2,1)S(1)}, u32[]{:S(2)}, u32[]{:S(2)}) collective-permute-start(bf16[640,1,128]{2,0,1:T(8,128)(2,1)} %copy.941), channel_id=1, source_target_pairs={{1,0},{2,1},{3,2},{4,3},{5,4},{6,5},{7,6},{9,8},{10,9},{11,10},{12... | collective-permute-start | bytes 491528 | tf_op jit(solution)/shard_map/ppermute | solution.py:23
  53.3 21.9 %collective-permute-start.6 = (bf16[384,4,128]{2,1,0:T(4,128)(2,1)S(1)}, bf16[384,4,128]{2,1,0:T(4,128)(2,1)S(1)}, u32[]{:S(2)}, u32[]{:S(2)}) collective-permute-start(bf16[384,4,128]{2,1,0:T(4,128)(2,1)S(1)} %get-tuple-element.390), channel_id=1, source_target_pairs={{0,8},{8,16},{16,24},{1,9},{9,17},{17,25},{2,10},{10,18},{18,26},{... | collective-permute-start | bytes 1179656 | tf_op jit(solution)/shard_map/ppermute | solution.py:33
  61.0 14.2 %collective-permute-start.5 = (bf16[256,4,128]{2,1,0:T(4,128)(2,1)S(1)}, bf16[256,4,128]{2,1,0:T(4,128)(2,1)S(1)}, u32[]{:S(2)}, u32[]{:S(2)}) collective-permute-start(bf16[256,4,128]{2,1,0:T(4,128)(2,1)S(1)} %copy.239), channel_id=1, source_target_pairs={{0,8},{8,16},{16,24},{1,9},{9,17},{17,25},{2,10},{10,18},{18,26},{... | collective-permute-start | bytes 786440 | tf_op jit(solution)/shard_map/ppermute | solution.py:33
  97.0 27.5 %collective-permute-start.10 = (bf16[384,4,128]{2,1,0:T(4,128)(2,1)S(1)}, bf16[384,4,128]{2,1,0:T(4,128)(2,1)S(1)}, u32[]{:S(2)}, u32[]{:S(2)}) collective-permute-start(bf16[384,4,128]{2,1,0:T(4,128)(2,1)S(1)} %get-tuple-element.392), channel_id=1, source_target_pairs={{0,8},{8,16},{16,24},{1,9},{9,17},{17,25},{2,10},{10,18},{18,26},{... | collective-permute-start | bytes 1179656 | tf_op jit(solution)/shard_map/ppermute | solution.py:33
  110.0 14.5 %collective-permute-start.9 = (bf16[256,4,128]{2,1,0:T(4,128)(2,1)S(1)}, bf16[256,4,128]{2,1,0:T(4,128)(2,1)S(1)}, u32[]{:S(2)}, u32[]{:S(2)}) collective-permute-start(bf16[256,4,128]{2,1,0:T(4,128)(2,1)S(1)} %get-tuple-element.391), channel_id=1, source_target_pairs={{0,8},{8,16},{16,24},{1,9},{9,17},{17,25},{2,10},{10,18},{18,26},{... | collective-permute-start | bytes 786440 | tf_op jit(solution)/shard_map/ppermute | solution.py:33
  111.9 15.3 %collective-permute-start.11 = (bf16[256,4,128]{2,1,0:T(4,128)(2,1)S(1)}, bf16[256,4,128]{2,1,0:T(4,128)(2,1)S(1)}, u32[]{:S(2)}, u32[]{:S(2)}) collective-permute-start(bf16[256,4,128]{2,1,0:T(4,128)(2,1)S(1)} %get-tuple-element.640), channel_id=1, source_target_pairs={{0,8},{8,16},{16,24},{1,9},{9,17},{17,25},{2,10},{10,18},{18,26},{... | collective-permute-start | bytes 786440 | tf_op jit(solution)/shard_map/ppermute | solution.py:33
  128.0 7.7 %collective-permute-start.12 = (bf16[640,1,128]{2,0,1:T(8,128)(2,1)S(1)}, bf16[640,1,128]{2,0,1:T(8,128)(2,1)S(1)}, u32[]{:S(2)}, u32[]{:S(2)}) collective-permute-start(bf16[640,1,128]{2,0,1:T(8,128)(2,1)S(1)} %copy.946), channel_id=1, source_target_pairs={{0,1},{1,2},{2,3},{3,4},{4,5},{5,6},{6,7},{8,9},{9,10},{10,11},{11... | collective-permute-start | bytes 491528 | tf_op jit(solution)/shard_map/ppermute | solution.py:21
  142.1 18.9 %collective-permute-start.17 = (bf16[256,4,128]{2,1,0:T(4,128)(2,1)}, bf16[256,4,128]{2,1,0:T(4,128)(2,1)}, u32[]{:S(2)}, u32[]{:S(2)}) collective-permute-start(bf16[256,4,128]{2,1,0:T(4,128)(2,1)} %copy.256), channel_id=1, source_target_pairs={{0,8},{8,16},{16,24},{1,9},{9,17},{17,25},{2,10},{10,18},{18,26},{... | collective-permute-start | bytes 786440 | tf_op jit(solution)/shard_map/ppermute | solution.py:33
  159.7 13.0 %collective-permute-start.16 = (bf16[256,4,128]{2,1,0:T(4,128)(2,1)S(1)}, bf16[256,4,128]{2,1,0:T(4,128)(2,1)}, u32[]{:S(2)}, u32[]{:S(2)}) collective-permute-start(bf16[256,4,128]{2,1,0:T(4,128)(2,1)S(1)} %copy.255), channel_id=1, source_target_pairs={{8,0},{16,8},{24,16},{9,1},{17,9},{25,17},{10,2},{18,10},{26,18},{... | collective-permute-start | bytes 786440 | tf_op jit(solution)/shard_map/ppermute | solution.py:33
  164.0 8.7 %collective-permute-start.18 = (bf16[640,1,128]{2,0,1:T(8,128)(2,1)S(1)}, bf16[640,1,128]{2,0,1:T(8,128)(2,1)S(1)}, u32[]{:S(2)}, u32[]{:S(2)}) collective-permute-start(bf16[640,1,128]{2,0,1:T(8,128)(2,1)S(1)} %copy.948), channel_id=1, source_target_pairs={{0,1},{1,2},{2,3},{3,4},{4,5},{5,6},{6,7},{8,9},{9,10},{10,11},{11... | collective-permute-start | bytes 491528 | tf_op jit(solution)/shard_map/ppermute | solution.py:21
  200.6 19.1 %collective-permute-start.22 = (bf16[384,4,128]{2,1,0:T(4,128)(2,1)}, bf16[384,4,128]{2,1,0:T(4,128)(2,1)S(1)}, u32[]{:S(2)}, u32[]{:S(2)}) collective-permute-start(bf16[384,4,128]{2,1,0:T(4,128)(2,1)} %get-tuple-element.402), channel_id=1, source_target_pairs={{8,0},{16,8},{24,16},{9,1},{17,9},{25,17},{10,2},{18,10},{26,18},{... | collective-permute-start | bytes 1179656 | tf_op jit(solution)/shard_map/ppermute | solution.py:33
  201.9 17.8 %collective-permute-start.23 = (bf16[256,4,128]{2,1,0:T(4,128)(2,1)S(1)}, bf16[256,4,128]{2,1,0:T(4,128)(2,1)S(1)}, u32[]{:S(2)}, u32[]{:S(2)}) collective-permute-start(bf16[256,4,128]{2,1,0:T(4,128)(2,1)S(1)} %get-tuple-element.642), channel_id=1, source_target_pairs={{8,0},{16,8},{24,16},{9,1},{17,9},{25,17},{10,2},{18,10},{26,18},{... | collective-permute-start | bytes 786440 | tf_op jit(solution)/shard_map/ppermute | solution.py:33
  220.2 8.0 %collective-permute-start.24 = (bf16[384,1,128]{2,0,1:T(8,128)(2,1)S(1)}, bf16[384,1,128]{2,0,1:T(8,128)(2,1)S(1)}, u32[]{:S(2)}, u32[]{:S(2)}) collective-permute-start(bf16[384,1,128]{2,0,1:T(8,128)(2,1)S(1)} %copy.950), channel_id=1, source_target_pairs={{0,1},{1,2},{2,3},{3,4},{4,5},{5,6},{6,7},{8,9},{9,10},{10,11},{11... | collective-permute-start | bytes 294920 | tf_op jit(solution)/shard_map/ppermute | solution.py:21
  224.9 77.6 %collective-permute-start.26 = (bf16[256,4,128]{0,2,1:T(8,128)(2,1)}, bf16[256,4,128]{0,2,1:T(8,128)(2,1)S(1)}, u32[]{:S(2)}, u32[]{:S(2)}) collective-permute-start(bf16[256,4,128]{0,2,1:T(8,128)(2,1)} %copy-done.40), channel_id=1, source_target_pairs={{8,0},{16,8},{24,16},{9,1},{17,9},{25,17},{10,2},{18,10},{26,18},{... | collective-permute-start | bytes 786440 | tf_op jit(solution)/shard_map/ppermute | solution.py:33
  313.5 50.9 %collective-permute-start.28 = (bf16[384,4,128]{2,1,0:T(4,128)(2,1)S(1)}, bf16[384,4,128]{2,1,0:T(4,128)(2,1)S(1)}, u32[]{:S(2)}, u32[]{:S(2)}) collective-permute-start(bf16[384,4,128]{2,1,0:T(4,128)(2,1)S(1)} %copy.280), channel_id=1, source_target_pairs={{8,0},{16,8},{24,16},{9,1},{17,9},{25,17},{10,2},{18,10},{26,18},{... | collective-permute-start | bytes 1179656 | tf_op jit(solution)/shard_map/ppermute | solution.py:33
  315.0 49.4 %collective-permute-start.27 = (bf16[256,4,128]{2,1,0:T(4,128)(2,1)S(1)}, bf16[256,4,128]{2,1,0:T(4,128)(2,1)S(1)}, u32[]{:S(2)}, u32[]{:S(2)}) collective-permute-start(bf16[256,4,128]{2,1,0:T(4,128)(2,1)S(1)} %copy.279), channel_id=1, source_target_pairs={{8,0},{16,8},{24,16},{9,1},{17,9},{25,17},{10,2},{18,10},{26,18},{... | collective-permute-start | bytes 786440 | tf_op jit(solution)/shard_map/ppermute | solution.py:33
  370.7 7.0 collective-permute-start.30
  438.4 7.1 collective-permute-start.31
  449.2 14.5 %collective-permute-start.32 = (bf16[384,1,128]{2,0,1:T(8,128)(2,1)S(1)}, bf16[384,1,128]{2,0,1:T(8,128)(2,1)S(1)}, u32[]{:S(2)}, u32[]{:S(2)}) collective-permute-start(bf16[384,1,128]{2,0,1:T(8,128)(2,1)S(1)} %get-tuple-element.807), channel_id=1, source_target_pairs={{0,1},{1,2},{2,3},{3,4},{4,5},{5,6},{6,7},{8,9},{9,10},{10,11},{11... | collective-permute-start | bytes 294920 | tf_op jit(solution)/shard_map/ppermute | solution.py:21
  452.4 12.0 %collective-permute-start.33 = (bf16[384,1,128]{2,0,1:T(8,128)(2,1)S(1)}, bf16[384,1,128]{2,0,1:T(8,128)(2,1)}, u32[]{:S(2)}, u32[]{:S(2)}) collective-permute-start(bf16[384,1,128]{2,0,1:T(8,128)(2,1)S(1)} %get-tuple-element.808), channel_id=1, source_target_pairs={{1,0},{2,1},{3,2},{4,3},{5,4},{6,5},{7,6},{9,8},{10,9},{11,10},{12... | collective-permute-start | bytes 294920 | tf_op jit(solution)/shard_map/ppermute | solution.py:23
  (40 other events, 278.0 us)
Sparse Core Ops, SparseCore 0:
  503.0 217.6 all-reduce.45
where the time goes:
time: 752 us; the launch traced here: 742 us
  waiting for transfers between devices  349 us (46%)
  local copies, waits for them, and re-layouts  114 us (15%)
  starting transfers between devices  100 us (13%)
  blocking collectives  66.4 us (9%)
  matrix products  54.4 us (7%)
  loops' own time  34.5 us (5%)
  between operations  15.4 us (2%)
  other arithmetic  8.69 us (1%)
    ppermute x14, waiting for transfers between devices, shifted(): return lax.ppermute(shard, axis, pairs)  173 us
    psum x1, waiting for transfers between devices, local(): summed = lax.psum(grad_sums, ('dp', 'segment', 'space'))  151 us
    psum x1, blocking collectives, local(): summed = lax.psum(grad_sums, ('dp', 'segment', 'space'))  66.4 us
    ppermute x14, starting transfers between devices, shifted(): return lax.ppermute(shard, axis, pairs)  41.4 us
    ppermute x10, starting transfers between devices, extended(): lax.ppermute(tail, axis, [(i, (i + 1) % count) for i in range(ends)])  38.7 us
    unnamed x73, local copies, waits for them, and re-layouts  26.3 us
    dot_general x16, matrix products, conv_input_grad(): lax.dot_general(weight[:, tap_index * channels:(tap_index + 1) * channels...  25 us
    another operation x5, loops' own time, local(): lax.switch(segment_index, [grads_terrain, grads_meso, grads_merging, grad...  23.5 us
  transfers between devices with their start and end apart: 35, of which 19 were waited for; matrix products, arithmetic and copies ran while one was open for 5% of the time, Pallas kernels for 0%

commit v1 on v0

v1 whole, which is shorter than its diff:
```python
import math

import jax
import jax.numpy as jnp
from jax import lax
from jax.experimental import pallas as pl
from jax.experimental.pallas import tpu as pltpu
from jax.sharding import PartitionSpec as P

BF = jnp.bfloat16
F32 = jnp.float32
TERR, MESO, MIX = 256, 384, 256
JOINT = TERR + MESO
LEV = 128
SLAB = 16
PACK = LEV + SLAB
ROWS, COLS = 4, 128
HALO = 5
CHUNK = 2 * COLS
OQ, MQ = MIX // 4, MESO // 4
WIDE = 1280
PIECES = 32
NT = (((1,), (1,)), ((), ()))


def dot(a, b):
    return jnp.dot(a, b, preferred_element_type=F32)


def dot_nt(a, b):
    return lax.dot_general(a, b, NT, preferred_element_type=F32)


def params(mib):
    return pltpu.CompilerParams(vmem_limit_bytes=mib * 1024 * 1024)


def prep_kernel(mw, lw, tw, pw, gw, dw, wm, wt, gt, dt):
    for tap in range(9):
        wm[:, tap * LEV : (tap + 1) * LEV] = dot(
            mw[:, tap * MESO : (tap + 1) * MESO], lw[...]
        ).astype(BF)
    wt[...] = jnp.concatenate(
        [dot(tw[:, tap * TERR : (tap + 1) * TERR], pw[...]).astype(BF) for tap in range(9)], axis=1
    )
    for tap in range(9):
        gt[:, tap * MIX : (tap + 1) * MIX] = gw[:, tap * JOINT : (tap + 1) * JOINT].T
        dt[:, tap * MIX : (tap + 1) * MIX] = dw[:, tap * MIX : (tap + 1) * MIX].T


def prep(meso_weight, lift_weight, terrain_weight, patch16, merging_weight, decoder_weight):
    return pl.pallas_call(
        prep_kernel,
        out_shape=(
            jax.ShapeDtypeStruct((MESO, 9 * LEV), BF),
            jax.ShapeDtypeStruct((TERR, 9 * SLAB), BF),
            jax.ShapeDtypeStruct((JOINT, 9 * MIX), BF),
            jax.ShapeDtypeStruct((MIX, 9 * MIX), BF),
        ),
        compiler_params=params(40),
        cost_estimate=pl.CostEstimate(
            flops=2 * 9 * 384 * 384 * 128, bytes_accessed=17_000_000, transcendentals=0
        ),
        name="prep",
    )(meso_weight, lift_weight, terrain_weight, patch16, merging_weight, decoder_weight)


def neighbours(v):
    width = v.shape[1]
    lane = lax.broadcasted_iota(jnp.int32, (1, width), 1) % COLS
    left, right = [], []
    for r in range(width // COLS):
        piece = v[:, r * COLS : (r + 1) * COLS]
        left.append(pltpu.roll(piece, 1, 1))
        right.append(pltpu.roll(piece, COLS - 1, 1))
    left = jnp.where(lane == 0, 0.0, jnp.concatenate(left, axis=1))
    right = jnp.where(lane == COLS - 1, 0.0, jnp.concatenate(right, axis=1))
    return left, right


def logistic(v):
    return 0.5 * (1.0 + jnp.tanh(0.5 * v))


def main_kernel(
    place, x, wm, wt, gw, dw, gt, dt, hw, out, x3, p9, j3, jslope, m3, mslope, dout, d3, e3
):
    segment, first_row = place[0], place[1] * ROWS

    def lanes(row):
        return pl.ds(pl.multiple_of(row * COLS, COLS), CHUNK)

    def inside(row):
        at = lax.broadcasted_iota(jnp.int32, (1, CHUNK), 1) // COLS + row + first_row
        return jnp.logical_and(at >= 0, at < 8 * ROWS)

    n_in, n_join, n_mix, n_dec, n_back = (
        ROWS + 2 * HALO,
        ROWS + 8,
        ROWS + 6,
        ROWS + 4,
        ROWS + 2,
    )

    def load(i, carry):
        s, r = i // n_in, i % n_in
        v = x[s, r].astype(F32)
        left, right = neighbours(v)
        at = pl.ds(pl.multiple_of(r * COLS, COLS), COLS)
        for b, u in enumerate((left, v, right)):
            u = u.astype(BF)
            x3[s, b * LEV : (b + 1) * LEV, at] = u[:LEV]
            for a in range(3):

                @pl.when(jnp.logical_and(r >= a, r < n_join + a))
                def _(a=a, b=b, u=u):
                    to = pl.ds(pl.multiple_of((r - a) * COLS, COLS), COLS)
                    tap = 3 * a + b
                    p9[s, tap * SLAB : (tap + 1) * SLAB, to] = u[LEV:]

        return carry

    lax.fori_loop(0, 2 * n_in, load, 0)

    def first(i, carry):
        s, k = i // (n_join // 2), i % (n_join // 2)
        row = 2 * k
        pre_t = dot(wt[...], p9[s, :, lanes(row)])
        pre_m = sum(
            dot(wm[:, a * 3 * LEV : (a + 1) * 3 * LEV], x3[s, :, lanes(row + a)]) for a in range(3)
        )
        valid = inside(row - 4)
        for at, pre in ((0, pre_t), (TERR, pre_m)):
            size = pre.shape[0]
            sigma = logistic(pre)
            v = jnp.where(valid, pre * sigma, 0.0)
            left, right = neighbours(v)
            for b, u in enumerate((left, v, right)):
                j3[s, b * JOINT + at : b * JOINT + at + size, lanes(row)] = u.astype(BF)

            @pl.when(jnp.logical_and(row >= 4, row < 8))
            def _(at=at, size=size, sigma=sigma, pre=pre):
                jslope[s, at : at + size, lanes(row - 4)] = sigma * (1.0 + pre * (1.0 - sigma))

        return carry

    lax.fori_loop(0, n_join, first, 0)

    def merge(i, carry):
        s, k = i // (n_mix // 2), i % (n_mix // 2)
        row = 2 * k
        pre = sum(
            dot(gw[:, a * 3 * JOINT : (a + 1) * 3 * JOINT], j3[s, :, lanes(row + a)])
            for a in range(3)
        )
        sigma = logistic(pre)
        v = jnp.where(inside(row - 3), pre * sigma, 0.0)
        left, right = neighbours(v)
        for b, u in enumerate((left, v, right)):
            m3[s, b * MIX : (b + 1) * MIX, lanes(row)] = u.astype(BF)
        mslope[s, :, lanes(row)] = sigma * (1.0 + pre * (1.0 - sigma))
        return carry

    lax.fori_loop(0, n_mix, merge, 0)

    scale = 1.0 / math.sqrt(8 * 32 * 128)

    def decode(i, carry):
        s, k = i // (n_dec // 2), i % (n_dec // 2)
        row = 2 * k
        pre = sum(
            dot(dw[:, a * 3 * MIX : (a + 1) * 3 * MIX], m3[s, :, lanes(row + a)]) for a in range(3)
        )
        sigma = logistic(pre)
        cot = jnp.concatenate([x[s, row + 3, LEV:], x[s, row + 4, LEV:]], axis=1)
        back = scale * dot(hw[...], cot)
        v = sigma * (1.0 + pre * (1.0 - sigma)) * back
        left, right = neighbours(v)
        for b, u in enumerate((right, v, left)):
            d3[s, b * MIX : (b + 1) * MIX, lanes(row)] = u.astype(BF)

        @pl.when(jnp.logical_and(row >= 2, row < 6))
        def _():
            dout[s, :, lanes(row - 2)] = (pre * sigma).astype(BF)

        return carry

    lax.fori_loop(0, n_dec, decode, 0)

    def back_decoder(i, carry):
        s, k = i // (n_back // 2), i % (n_back // 2)
        row = 2 * k
        back = sum(
            dot(dt[:, a * 3 * MIX : (a + 1) * 3 * MIX], d3[s, :, lanes(row + 2 - a)])
            for a in range(3)
        )
        v = jnp.where(inside(row - 1), mslope[s, :, lanes(row + 2)] * back, 0.0)
        left, right = neighbours(v)
        for b, u in enumerate((right, v, left)):
            e3[s, b * MIX : (b + 1) * MIX, lanes(row)] = u.astype(BF)
        return carry

    lax.fori_loop(0, n_back, back_decoder, 0)

    def back_merging(i, carry):
        s, k = i // (ROWS // 2), i % (ROWS // 2)
        row = 2 * k
        back = sum(
            dot(gt[:, a * 3 * MIX : (a + 1) * 3 * MIX], e3[s, :, lanes(row + 2 - a)])
            for a in range(3)
        )
        jslope[s, :, lanes(row)] = jslope[s, :, lanes(row)] * back
        return carry

    lax.fori_loop(0, ROWS, back_merging, 0)

    def put(rows, column, value):
        value = value.astype(BF)
        width = value.shape[1]
        done = 0
        while done < width:
            group, offset = divmod(column + done, WIDE)
            take = min(width - done, WIDE - offset)
            for t in range(value.shape[0] // 16):
                out[(rows // 16 + t) * 8 + group, :, offset : offset + take] = value[
                    t * 16 : (t + 1) * 16, done : done + take
                ]
            done += take

    own = ROWS * COLS
    q = pl.ds(pl.multiple_of(segment * OQ, OQ), OQ)
    qd = pl.ds(pl.multiple_of(MIX + segment * OQ, OQ), OQ)
    qm = pl.ds(pl.multiple_of(TERR + segment * MQ, 32), MQ)
    e_own = [e3[s, qd, COLS : COLS + own] for s in range(2)]
    for tap in range(9):
        a, b = divmod(tap, 3)
        put(
            0,
            tap * JOINT,
            sum(
                dot_nt(e_own[s], j3[s, b * JOINT : (b + 1) * JOINT, (3 + a) * COLS : (3 + a) * COLS + own])
                for s in range(2)
            ),
        )
    column = 9 * JOINT
    d_own = [d3[s, qd, 2 * COLS : 2 * COLS + own] for s in range(2)]
    for a in range(3):
        put(
            0,
            column + a * 3 * MIX,
            sum(
                dot_nt(d_own[s], m3[s, :, (2 + a) * COLS : (2 + a) * COLS + own]) for s in range(2)
            ),
        )
    column += 9 * MIX
    h_own = [jslope[s, qm, :].astype(BF) for s in range(2)]
    for a in range(3):
        h = sum(
            dot_nt(h_own[s], x3[s, :, (4 + a) * COLS : (4 + a) * COLS + own]) for s in range(2)
        )
        put(0, column + a * 3 * LEV, h[:64])
        spare = column + 9 * LEV
        for c in range(3):
            at = a * 3 * LEV + c * LEV
            piece = h[64:, c * LEV : (c + 1) * LEV]
            if at < 640:
                put(0, spare + at, piece)
            else:
                put(32, spare + at - 640, piece)
    put(32, column + 9 * LEV + 512, jnp.zeros((32, 128), F32))
    column += 9 * LEV + 640
    t_own = [jslope[s, q, :].astype(BF) for s in range(2)]
    g = sum(dot_nt(t_own[s], p9[s, :, 4 * COLS : 4 * COLS + own]) for s in range(2))
    head = scale * sum(
        dot_nt(
            dout[s, q, :],
            jnp.concatenate([x[s, HALO + r, LEV:] for r in range(ROWS)], axis=1),
        )
        for s in range(2)
    )
    tail = 8 * WIDE - column
    put(0, column, jnp.concatenate([g, head, jnp.zeros((OQ, tail - 10 * SLAB), F32)], axis=1))


def main(place, x, wm, wt, gw, dw, gt, dt, hw):
    vmem = pl.BlockSpec(memory_space=pltpu.VMEM)
    return pl.pallas_call(
        main_kernel,
        out_shape=jax.ShapeDtypeStruct((PIECES, 16, WIDE), BF),
        in_specs=[pl.BlockSpec(memory_space=pltpu.SMEM)] + [vmem] * 8,
        out_specs=vmem,
        scratch_shapes=[
            pltpu.VMEM((2, 3 * LEV, (ROWS + 2 * HALO) * COLS), BF),
            pltpu.VMEM((2, 9 * SLAB, (ROWS + 8) * COLS), BF),
            pltpu.VMEM((2, 3 * JOINT, (ROWS + 8) * COLS), BF),
            pltpu.VMEM((2, JOINT, ROWS * COLS), F32),
            pltpu.VMEM((2, 3 * MIX, (ROWS + 6) * COLS), BF),
            pltpu.VMEM((2, MIX, (ROWS + 6) * COLS), F32),
            pltpu.VMEM((2, MIX, ROWS * COLS), BF),
            pltpu.VMEM((2, 3 * MIX, (ROWS + 4) * COLS), BF),
            pltpu.VMEM((2, 3 * MIX, (ROWS + 2) * COLS), BF),
        ],
        compiler_params=params(56),
        cost_estimate=pl.CostEstimate(
            flops=19_000_000_000, bytes_accessed=14_000_000, transcendentals=3_000_000
        ),
        name="sections",
    )(place, x, wm, wt, gw, dw, gt, dt, hw)


def finish_kernel(got, mw, lw, tw, pw, patch, terrain, lift, meso, merging, decoder, head, ht, gt):
    for seg in range(4):
        for t in range(4):
            lo = seg * OQ + t * 16

            def take(column, width):
                pieces = []
                done = 0
                while done < width:
                    group, offset = divmod(column + done, WIDE)
                    n = min(width - done, WIDE - offset)
                    pieces.append(got[seg * PIECES + t * 8 + group, :, offset : offset + n])
                    done += n
                return pieces[0] if len(pieces) == 1 else jnp.concatenate(pieces, axis=1)

            merging[lo : lo + 16, :] = take(0, 9 * JOINT).astype(F32)
            decoder[lo : lo + 16, :] = take(9 * JOINT, 9 * MIX).astype(F32)
            column = 9 * JOINT + 9 * MIX
            mlo = seg * MQ + t * 16
            ht[mlo : mlo + 16, :] = take(column, 9 * LEV)
            mlo = seg * MQ + 64 + (t % 2) * 16
            if t < 2:
                ht[mlo : mlo + 16, :640] = take(column + 9 * LEV, 640)
            else:
                ht[mlo : mlo + 16, 640:] = take(column + 9 * LEV, 512)
            gt[lo : lo + 16, :] = take(column + 9 * LEV + 640, 256)
    h = ht[...]
    for tap in range(9):
        meso[:, tap * MESO : (tap + 1) * MESO] = dot_nt(h[:, tap * LEV : (tap + 1) * LEV], lw[...])
    turned = h.astype(F32).T.astype(BF)
    lift[...] = sum(
        dot(turned[tap * LEV : (tap + 1) * LEV, :], mw[:, tap * MESO : (tap + 1) * MESO])
        for tap in range(9)
    ).T
    g = gt[...]
    for tap in range(9):
        terrain[:, tap * TERR : (tap + 1) * TERR] = dot_nt(
            g[:, tap * SLAB : (tap + 1) * SLAB], pw[...]
        )
    turned = g.astype(F32).T
    patch[...] = sum(
        dot(
            turned[tap * SLAB : (tap + 1) * SLAB, :].astype(BF),
            tw[:, tap * TERR : (tap + 1) * TERR],
        )
        for tap in range(9)
    ).T[:, :8]
    head[...] = turned[9 * SLAB + 8 : 9 * SLAB + 11, :]


def finish(got, meso_weight, lift_weight, terrain_weight, patch16):
    return pl.pallas_call(
        finish_kernel,
        out_shape=(
            jax.ShapeDtypeStruct((TERR, 8), F32),
            jax.ShapeDtypeStruct((TERR, 9 * TERR), F32),
            jax.ShapeDtypeStruct((MESO, LEV), F32),
            jax.ShapeDtypeStruct((MESO, 9 * MESO), F32),
            jax.ShapeDtypeStruct((MIX, 9 * JOINT), F32),
            jax.ShapeDtypeStruct((MIX, 9 * MIX), F32),
            jax.ShapeDtypeStruct((3, MIX), F32),
        ),
        scratch_shapes=[pltpu.VMEM((MESO, 9 * LEV), BF), pltpu.VMEM((MIX, 256), BF)],
        compiler_params=params(52),
        name="finish",
    )(got, meso_weight, lift_weight, terrain_weight, patch16)


def packed(terrain_in, meso_in, wind_cot):
    samples = terrain_in.shape[0]
    source = lax.broadcasted_iota(jnp.int32, (2 * COLS, 2 * COLS), 0)
    target = lax.broadcasted_iota(jnp.int32, (2 * COLS, 2 * COLS), 1)
    pick = (source == 2 * (target % COLS) + target // COLS).astype(BF)
    split = dot(terrain_in.reshape(samples * 4 * ROWS, 2 * COLS), pick).astype(BF)
    patches = (
        split.reshape(samples, 2, ROWS, 2, 2, COLS)
        .transpose(0, 2, 1, 3, 4, 5)
        .reshape(samples, ROWS, 8, COLS)
    )
    levels = meso_in.reshape(samples, LEV, ROWS, COLS).transpose(0, 2, 1, 3)
    cot = wind_cot.transpose(0, 2, 1, 3)
    rest = jnp.zeros((samples, ROWS, PACK - LEV - 11, COLS), BF)
    return jnp.concatenate([levels, patches, cot, rest], axis=2)


def shifted(v, by):
    count = lax.axis_size("space")
    return lax.ppermute(
        v, "space", [(i, i + by) for i in range(count) if 0 <= i + by < count]
    )


def local(
    terrain_in,
    meso_in,
    wind_cot,
    patch_weight,
    terrain_weight,
    lift_weight,
    meso_weight,
    merging_weight,
    decoder_weight,
    head_weight,
):
    own = packed(terrain_in, meso_in, wind_cot)
    haloed = jnp.concatenate(
        [shifted(own[:, 3:], 2), shifted(own, 1), own, shifted(own, -1), shifted(own[:, :1], -2)],
        axis=1,
    )
    patch16 = jnp.pad(patch_weight, ((0, 0), (0, SLAB - 8)))
    head16 = jnp.pad(head_weight.T, ((0, 0), (8, SLAB - 11)))
    wm, wt, gt, dt = prep(
        meso_weight, lift_weight, terrain_weight, patch16, merging_weight, decoder_weight
    )
    place = jnp.stack([lax.axis_index("segment"), lax.axis_index("space")]).astype(jnp.int32)
    parts = main(place, haloed, wm, wt, merging_weight, decoder_weight, gt, dt, head16)
    parts = lax.all_to_all(parts, ("dp", "space"), 0, 0, tiled=True)
    mine = jnp.sum(parts.astype(F32), axis=0).astype(BF)
    got = lax.all_gather(mine, ("segment", "dp", "space"))
    return finish(got, meso_weight, lift_weight, terrain_weight, patch16)


def solution(mesh):
    placed = (
        P("dp", None, "space", None),
        P("dp", None, None, "space", None),
        P("dp", None, "space", None),
        P(),
        P(),
        P(),
        P(),
        P(),
        P(),
        P(),
    )
    return jax.shard_map(
        local,
        mesh=mesh,
        in_specs=placed,
        out_specs=(P(), P(), P(), P(), P(), P(), P()),
        check_vma=False,
    )
```

time: 752 us -> 201 us (0.27); the launches traced: 742 us -> 200 us
  waiting for transfers between devices: 349 us -> 65.4 us
  local copies, waits for them, and re-layouts: 114 us -> 16.3 us
  starting transfers between devices: 100 us -> 11.8 us
  Pallas kernels: 0 us -> 60.5 us
  matrix products: 54.4 us -> 0.16 us
  blocking collectives: 66.4 us -> 28.5 us
  loops' own time: 34.5 us -> 0 us
    ppermute x34 -> x4, waiting for transfers between devices: 197 us -> 0.01 us  [shifted(): lax.ppermute(v, 'space', [(i, i + by) for i in range(count) if 0 <= i + b...]
    psum x1 -> x0, waiting for transfers between devices: 151 us -> none  [local(): summed = lax.psum(grad_sums, ('dp', 'segment', 'space'))]
    ppermute x34 -> x4, starting transfers between devices: 100 us -> 11.8 us  [shifted(): lax.ppermute(v, 'space', [(i, i + by) for i in range(count) if 0 <= i + b...]
    psum x1 -> x0, blocking collectives: 66.4 us -> none  [local(): summed = lax.psum(grad_sums, ('dp', 'segment', 'space'))]
    all_gather x0 -> x1, waiting for transfers between devices: none -> 65.4 us  [local(): got = lax.all_gather(mine, ('segment', 'dp', 'space'))]
    pallas_call x0 -> x3, Pallas kernels: none -> 60.5 us  [the longest x1 48 us: main(): pl.pallas_call(main_kernel, out_shape=jax.ShapeDtypeStruct((PIECES, 16, W...]
    dot_general x56 -> x1, matrix products: 54.4 us -> 0.16 us  [dot(): return jnp.dot(a, b, preferred_element_type=F32)]
    another operation x20 -> x0, loops' own time: 34.5 us -> none  [the longest x5 23.5 us: local(): lax.switch(segment_index, [grads_terrain, grads_meso, grads_merging, grad...]
  transfers between devices with their start and end apart: 35 -> 5, of which waited for: 19 -> 1; matrix products, arithmetic and copies ran while one was open for 5% -> 2% of each run, Pallas kernels for 0% -> 1%
where the time goes in v1:
time: 201 us; the launch traced here: 200 us
  waiting for transfers between devices  65.4 us (33%)
  Pallas kernels  60.5 us (30%)
  blocking collectives  28.5 us (14%)
  local copies, waits for them, and re-layouts  16.3 us (8%)
  between operations  14.2 us (7%)
  starting transfers between devices  11.8 us (6%)
  other arithmetic  3.09 us (2%)
    all_gather x1, waiting for transfers between devices, local(): got = lax.all_gather(mine, ('segment', 'dp', 'space'))  65.4 us
    pallas_call x1, Pallas kernels, main(): pl.pallas_call(main_kernel, out_shape=jax.ShapeDtypeStruct((PIECES, 16, W...  48 us
    all_to_all x1, blocking collectives, local(): parts = lax.all_to_all(parts, ('dp', 'space'), 0, 0, tiled=True)  28.5 us
    unnamed x31, local copies, waits for them, and re-layouts  14.2 us
    ppermute x4, starting transfers between devices, shifted(): lax.ppermute(v, 'space', [(i, i + by) for i in range(count) if 0 <= i + b...  11.8 us
    pallas_call x1, Pallas kernels, finish(): pl.pallas_call(finish_kernel, out_shape=(jax.ShapeDtypeStruct((TERR, 8),...  11.1 us
  transfers between devices with their start and end apart: 5, of which 1 were waited for; matrix products, arithmetic and copies ran while one was open for 2% of the time, Pallas kernels for 1%

profile of v1, /device:TPU:1, one launch (start us, length us, event | category | flops | bytes accessed | tf_op | source)
XLA Modules:
  0.0 200.1 jit_solution(5418022288383149500)
XLA Ops:
  7.3 0.8 copy.24
  8.3 1.0 copy.17
  9.6 3.3 %collective-permute-start.2 = (bf16[2,4,144,128]{3,2,1,0:T(8,128)(2,1)S(1)}, bf16[2,4,144,128]{3,2,1,0:T(8,128)(2,1)S(1)}, u32[]{:S(2)}, u32[]{:S(2)}) collective-permute-start(bf16[2,4,144,128]{3,2,1,0:T(8,128)(2,1)S(1)} %maximum_maximum_fusion), channel_id=1, source_target_pairs={{1,0},{2,1},{3,2},{4,3},{5,4},{6,5},{7,6},{9,8},{10,9},{11,10},{12... | collective-permute-start | bytes 884744 | tf_op jit(solution)/shard_map/ppermute | solution.py:398
  12.9 3.2 %collective-permute-start.1 = (bf16[2,4,144,128]{3,2,1,0:T(8,128)(2,1)S(1)}, bf16[2,4,144,128]{3,2,1,0:T(8,128)(2,1)}, u32[]{:S(2)}, u32[]{:S(2)}) collective-permute-start(bf16[2,4,144,128]{3,2,1,0:T(8,128)(2,1)S(1)} %maximum_maximum_fusion), channel_id=1, source_target_pairs={{0,1},{1,2},{2,3},{3,4},{4,5},{5,6},{6,7},{8,9},{9,10},{10,11},{11... | collective-permute-start | bytes 884744 | tf_op jit(solution)/shard_map/ppermute | solution.py:398
  16.1 0.7 fusion.11
  16.8 1.3 collective-permute-start.3
  18.0 4.0 %collective-permute-start = (bf16[2,1,144,128]{3,2,1,0:T(8,128)(2,1)}, bf16[2,1,144,128]{3,2,1,0:T(8,128)(2,1)S(1)}, u32[]{:S(2)}, u32[]{:S(2)}) collective-permute-start(bf16[2,1,144,128]{3,2,1,0:T(8,128)(2,1)} %get-tuple-element.23), channel_id=1, source_target_pairs={{0,2},{1,3},{2,4},{3,5},{4,6},{5,7},{8,10},{9,11},{10,12},{11,13},... | collective-permute-start | bytes 221192 | tf_op jit(solution)/shard_map/ppermute | solution.py:398
  22.0 0.8 copy.20
  22.9 0.8 copy.21
  23.7 0.7 pad.9.hw
  24.4 1.7 copy-done.1
  26.2 1.8 copy-done.3
  28.0 0.9 copy-done.5
  28.9 1.3 prep.1
  30.2 1.6 copy-done.7
  31.8 1.0 copy-done.8
  32.8 0.9 copy-done.9
  35.1 1.0 constant_dynamic-update-slice_fusion.3
  36.3 1.0 copy-done.11
  37.3 48.0 %sections.1 = bf16[32,16,1280]{2,1,0:T(8,128)(2,1)} custom-call(s32[2]{0:T(128)} %pad_add_fusion.place, bf16[2,14,144,128]{3,2,1,0:T(8,128)(2,1)} %copy-done.11, bf16[384,1152]{1,0:T(8,128)(2,1)} %copy-done.9, bf16[256,144]{1,0:T(8,128)(2,1)} %copy-done.10, bf16[256,5760]{1,0:T(8,128)(2,1)} %gw.3, bf16[256,2304]{1,0:T(8,128)(2,1)} %dw.3, ...), custom_call_target="tpu_custom_call" | custom-call | flops 19000000512 | bytes 14000000 | tf_op jit(solution)/shard_map/sections/pallas_call | solution.py:287
  85.4 28.5 %all_to_all.5 = bf16[32,16,1280]{2,1,0:T(8,128)(2,1)} all-to-all(bf16[32,16,1280]{2,1,0:T(8,128)(2,1)} %sections.1), channel_id=1, replica_groups=mesh['dp'=4,'segment'=4,'space'=8] {'dp','space'}, dimensions={0} | all-to-all | bytes 2621440 | tf_op jit(solution)/shard_map/all_to_all | solution.py:427
  113.9 2.1 %reduce_sum.12 = bf16[16,1280]{1,0:T(8,128)(2,1)} reduce(bf16[32,16,1280]{2,1,0:T(8,128)(2,1)} %all_to_all.5, bf16[]{:T(256)} %constant.46.clone.1), dimensions={0}, to_apply=%region_0.1 | reduce | flops 634880 | bytes 1351682 | tf_op jit(solution)/shard_map/reduce_sum | solution.py:428
  116.0 65.4 %all-gather.3.cloned.1.call-done = bf16[2048,1280]{1,0:T(8,128)(2,1)} async-done(((bf16[16,1280]{1,0:T(8,128)(2,1)}), bf16[2048,1280]{1,0:T(8,128)(2,1)}) %all-gather.3.cloned.1.call-update) | async-done | bytes 5242896 | tf_op jit(solution)/shard_map/all_gather | solution.py:429
  181.4 11.1 %finish.1 = (f32[256,8]{1,0:T(8,128)S(1)}, f32[256,2304]{1,0:T(8,128)}, f32[384,128]{1,0:T(8,128)}, f32[384,3456]{1,0:T(8,128)}, f32[256,5760]{1,0:T(8,128)}, /*index=5*/f32[256,2304]{1,0:T(8,128)}, f32[3,256]{1,0:T(4,128)}) custom-call(bf16[128,16,1280]{2,1,0:T(8,128)(2,1)} %bitcast.18, bf16[384,3456]{1,0:T(8,128)(2,1)} %mw.3, ...), custom_call_target="tpu_custom_call" | custom-call | tf_op jit(solution)/shard_map/finish/pallas_call | solution.py:362
  (39 shorter events, 2.7 us)
Async XLA Ops:
  7.2 1.0 copy-start
  7.2 17.2 %copy-start.4 = (bf16[256,2304]{1,0:T(8,128)(2,1)S(1)}, bf16[256,2304]{1,0:T(8,128)(2,1)}, u32[]{:S(2)}) copy-start(bf16[256,2304]{1,0:T(8,128)(2,1)} %dw.3) | copy-start | bytes 3538948
  7.2 17.2 %copy-start.2 = (bf16[256,2304]{1,0:T(8,128)(2,1)S(1)}, bf16[256,2304]{1,0:T(8,128)(2,1)}, u32[]{:S(2)}) copy-start(bf16[256,2304]{1,0:T(8,128)(2,1)} %tw.3) | copy-start | bytes 3538948
  7.2 174.2 %all-gather.3.cloned.1.call-start = ((), (), s32[]{:S(2)}) async-start(), calls=%async_computation.1 | async-start | bytes 5283840 | tf_op jit(solution)/shard_map/all_gather | solution.py:429
  9.6 26.7 %collective-permute-start.2 = (bf16[2,4,144,128]{3,2,1,0:T(8,128)(2,1)S(1)}, bf16[2,4,144,128]{3,2,1,0:T(8,128)(2,1)S(1)}, u32[]{:S(2)}, u32[]{:S(2)}) collective-permute-start(bf16[2,4,144,128]{3,2,1,0:T(8,128)(2,1)S(1)} %maximum_maximum_fusion), channel_id=1, source_target_pairs={{1,0},{2,1},{3,2},{4,3},{5,4},{6,5},{7,6},{9,8},{10,9},{11,10},{12... | collective-permute-start | bytes 884744 | tf_op jit(solution)/shard_map/ppermute | solution.py:398
  12.9 22.2 %collective-permute-start.1 = (bf16[2,4,144,128]{3,2,1,0:T(8,128)(2,1)S(1)}, bf16[2,4,144,128]{3,2,1,0:T(8,128)(2,1)}, u32[]{:S(2)}, u32[]{:S(2)}) collective-permute-start(bf16[2,4,144,128]{3,2,1,0:T(8,128)(2,1)S(1)} %maximum_maximum_fusion), channel_id=1, source_target_pairs={{0,1},{1,2},{2,3},{3,4},{4,5},{5,6},{6,7},{8,9},{9,10},{10,11},{11... | collective-permute-start | bytes 884744 | tf_op jit(solution)/shard_map/ppermute | solution.py:398
  16.8 19.6 %collective-permute-start.3 = (bf16[2,1,144,128]{3,2,1,0:T(8,128)(2,1)}, bf16[2,1,144,128]{3,2,1,0:T(8,128)(2,1)S(1)}, u32[]{:S(2)}, u32[]{:S(2)}) collective-permute-start(bf16[2,1,144,128]{3,2,1,0:T(8,128)(2,1)} %get-tuple-element.22), channel_id=1, source_target_pairs={{2,0},{3,1},{4,2},{5,3},{6,4},{7,5},{10,8},{11,9},{12,10},{13,11},... | collective-permute-start | bytes 221192 | tf_op jit(solution)/shard_map/ppermute | solution.py:398
  18.0 17.0 %collective-permute-start = (bf16[2,1,144,128]{3,2,1,0:T(8,128)(2,1)}, bf16[2,1,144,128]{3,2,1,0:T(8,128)(2,1)S(1)}, u32[]{:S(2)}, u32[]{:S(2)}) collective-permute-start(bf16[2,1,144,128]{3,2,1,0:T(8,128)(2,1)} %get-tuple-element.23), channel_id=1, source_target_pairs={{0,2},{1,3},{2,4},{3,5},{4,6},{5,7},{8,10},{9,11},{10,12},{11,13},... | collective-permute-start | bytes 221192 | tf_op jit(solution)/shard_map/ppermute | solution.py:398
  24.4 1.8 copy-start.1
  26.2 1.8 copy-start.3
  28.0 0.9 copy-start.5
  30.2 1.6 copy-start.7
  31.8 1.0 copy-start.8
  32.8 0.9 copy-start.9
  33.8 0.7 copy-start.10
  36.3 1.0 copy-start.11
  85.4 96.1 %copy-start.6 = (bf16[384,128]{1,0:T(8,128)(2,1)S(1)}, bf16[384,128]{1,0:T(8,128)(2,1)}, u32[]{:S(2)}) copy-start(bf16[384,128]{1,0:T(8,128)(2,1)} %lw.3) | copy-start | bytes 294916
Sparse Core Ops, SparseCore 0:
  116.1 65.2 all-gather.2

commit v2 on v1

v2 whole, which is shorter than its diff:
```python
import math

import jax
import jax.numpy as jnp
from jax import lax
from jax.experimental import pallas as pl
from jax.experimental.pallas import tpu as pltpu
from jax.sharding import PartitionSpec as P

BF = jnp.bfloat16
F32 = jnp.float32
TERR, MESO, MIX = 256, 384, 256
JOINT = TERR + MESO
LEV = 128
SLAB = 16
PACK = LEV + SLAB
ROWS, COLS = 4, 128
HALO = 5
OQ, MQ = MIX // 4, MESO // 4
WIDE = 1280
NT = (((1,), (1,)), ((), ()))


def dot(a, b):
    return jnp.dot(a, b, preferred_element_type=F32)


def dot_nt(a, b):
    return lax.dot_general(a, b, NT, preferred_element_type=F32)


def params(mib):
    return pltpu.CompilerParams(vmem_limit_bytes=mib * 1024 * 1024)


def sixteen(v, above):
    rows, width = v.shape
    parts = [v.astype(F32)]
    if above:
        parts.insert(0, jnp.zeros((above, width), F32))
    if above + rows < SLAB:
        parts.append(jnp.zeros((SLAB - above - rows, width), F32))
    return jnp.concatenate(parts, axis=0)


def neighbours(v):
    width = v.shape[1]
    lane = lax.broadcasted_iota(jnp.int32, (1, width), 1) % COLS
    left, right = [], []
    for r in range(width // COLS):
        piece = v[:, r * COLS : (r + 1) * COLS]
        left.append(pltpu.roll(piece, 1, 1))
        right.append(pltpu.roll(piece, COLS - 1, 1))
    left = jnp.where(lane == 0, 0.0, jnp.concatenate(left, axis=1))
    right = jnp.where(lane == COLS - 1, 0.0, jnp.concatenate(right, axis=1))
    return left, right


def logistic(v):
    return 0.5 * (1.0 + jnp.tanh(0.5 * v))


def main_kernel(place, far_up, up, mid, down, far_down, lw, pw, hw, *refs):
    mw_hbm, tw_hbm, gw_hbm, dw_hbm, keep, send, out = refs[:7]
    mw, tw, gw, dw, wm, wt, gt, dt, sems = refs[7:16]
    x3, p9, j3, jslope, jdelta, m3, mslope, dout, d3, e3 = refs[16:]
    pairs = ((mw_hbm, mw), (tw_hbm, tw), (gw_hbm, gw), (dw_hbm, dw))
    copies = [pltpu.make_async_copy(u, v, sems.at[i]) for i, (u, v) in enumerate(pairs)]
    for copy in copies:
        copy.start()
    segment, first_row = place[0], place[1] * ROWS
    chip, core = place[1] // 2, place[1] % 2

    def cut(row, rows):
        return slice(row * COLS, (row + rows) * COLS)

    def inside(row, rows):
        at = lax.broadcasted_iota(jnp.int32, (1, rows * COLS), 1) // COLS + row + first_row
        return jnp.logical_and(at >= 0, at < 8 * ROWS)

    n_in, n_join, n_mix, n_dec, n_back = (
        ROWS + 2 * HALO,
        ROWS + 8,
        ROWS + 6,
        ROWS + 4,
        ROWS + 2,
    )

    def slab(s, r):
        for ref, rows in ((far_up, 1), (up, ROWS), (mid, ROWS), (down, ROWS), (far_down, 1)):
            if r < rows:
                return ref[s, r]
            r -= rows

    for r in range(n_in):
        for s in range(2):
            v = slab(s, r).astype(F32)
            left, right = neighbours(v)
            for b, u in enumerate((left, v, right)):
                u = u.astype(BF)
                x3[s, b * LEV : (b + 1) * LEV, cut(r, 1)] = u[:LEV]
                for a in range(3):
                    if a <= r < n_join + a:
                        tap = 3 * a + b
                        p9[s, tap * SLAB : (tap + 1) * SLAB, cut(r - a, 1)] = u[LEV:]

    pw16 = sixteen(pw[...], 0).astype(BF)
    head_turned = sixteen(hw[...], 8).T.astype(BF)
    copies[0].wait()
    for tap in range(9):
        wm[:, tap * LEV : (tap + 1) * LEV] = dot(
            mw[:, tap * MESO : (tap + 1) * MESO], lw[...]
        ).astype(BF)
    copies[1].wait()
    wt[...] = jnp.concatenate(
        [dot_nt(tw[:, tap * TERR : (tap + 1) * TERR], pw16).astype(BF) for tap in range(9)], axis=1
    )

    def first(row, rows):
        for s in range(2):
            pre_t = dot(wt[...], p9[s, :, cut(row, rows)])
            pre_m = sum(
                dot(wm[:, a * 3 * LEV : (a + 1) * 3 * LEV], x3[s, :, cut(row + a, rows)])
                for a in range(3)
            )
            for at, pre in ((0, pre_t), (TERR, pre_m)):
                size = pre.shape[0]
                sigma = logistic(pre)
                v = jnp.where(inside(row - 4, rows), pre * sigma, 0.0)
                left, right = neighbours(v)
                for b, u in enumerate((left, v, right)):
                    j3[s, b * JOINT + at : b * JOINT + at + size, cut(row, rows)] = u.astype(BF)
                if row == 4:
                    jslope[s, at : at + size, :] = sigma * (1.0 + pre * (1.0 - sigma))

    for row in (0, 4, 8):
        first(row, 4)

    copies[2].wait()
    copies[3].wait()
    for tap in range(9):
        gt[:, tap * MIX : (tap + 1) * MIX] = gw[:, tap * JOINT : (tap + 1) * JOINT].T
        dt[:, tap * MIX : (tap + 1) * MIX] = dw[:, tap * MIX : (tap + 1) * MIX].T

    for row in (0, 5):
        for s in range(2):
            pre = sum(
                dot(gw[:, a * 3 * JOINT : (a + 1) * 3 * JOINT], j3[s, :, cut(row + a, 5)])
                for a in range(3)
            )
            sigma = logistic(pre)
            v = jnp.where(inside(row - 3, 5), pre * sigma, 0.0)
            left, right = neighbours(v)
            for b, u in enumerate((left, v, right)):
                m3[s, b * MIX : (b + 1) * MIX, cut(row, 5)] = u.astype(BF)
            mslope[s, :, cut(row, 5)] = sigma * (1.0 + pre * (1.0 - sigma))

    scale = 1.0 / math.sqrt(8 * 32 * 128)

    for row in (0, 4):
        for s in range(2):
            pre = sum(
                dot(dw[:, a * 3 * MIX : (a + 1) * 3 * MIX], m3[s, :, cut(row + a, 4)])
                for a in range(3)
            )
            sigma = logistic(pre)
            cot = jnp.concatenate([slab(s, row + 3 + r)[LEV:] for r in range(4)], axis=1)
            back = scale * dot(head_turned, cot)
            v = sigma * (1.0 + pre * (1.0 - sigma)) * back
            left, right = neighbours(v)
            for b, u in enumerate((right, v, left)):
                d3[s, b * MIX : (b + 1) * MIX, cut(row, 4)] = u.astype(BF)
            half = slice(2 * COLS, 4 * COLS) if row == 0 else slice(0, 2 * COLS)
            dout[s, :, cut(row // 2, 2)] = (pre * sigma)[:, half].astype(BF)

    for row in (0, 3):
        for s in range(2):
            back = sum(
                dot(dt[:, a * 3 * MIX : (a + 1) * 3 * MIX], d3[s, :, cut(row + 2 - a, 3)])
                for a in range(3)
            )
            v = jnp.where(inside(row - 1, 3), mslope[s, :, cut(row + 2, 3)] * back, 0.0)
            left, right = neighbours(v)
            for b, u in enumerate((right, v, left)):
                e3[s, b * MIX : (b + 1) * MIX, cut(row, 3)] = u.astype(BF)

    for s in range(2):
        back = sum(
            dot(gt[:, a * 3 * MIX : (a + 1) * 3 * MIX], e3[s, :, cut(2 - a, 4)]) for a in range(3)
        )
        jdelta[s] = (jslope[s] * back).astype(BF)

    def put(rows, column, value):
        value = value.astype(BF)
        width = value.shape[1]
        done = 0
        while done < width:
            group, offset = divmod(column + done, WIDE)
            take = min(width - done, WIDE - offset)
            slot = 4 * lax.rem(core + group // 4, 2) + lax.rem(group % 4 + 4 - chip, 4)
            out[slot, rows : rows + value.shape[0], offset : offset + take] = value[
                :, done : done + take
            ]
            done += take

    def stacked(delta):
        def zero(rows):
            return jnp.zeros((delta.shape[0], rows * COLS), BF)

        return jnp.concatenate(
            [
                jnp.concatenate([delta, zero(2)], axis=1),
                jnp.concatenate([zero(1), delta, zero(1)], axis=1),
                jnp.concatenate([zero(2), delta], axis=1),
            ],
            axis=0,
        )

    q = pl.ds(pl.multiple_of(segment * OQ, OQ), OQ)
    qd = pl.ds(pl.multiple_of(MIX + segment * OQ, OQ), OQ)
    qm = pl.ds(pl.multiple_of(TERR + segment * MQ, 32), MQ)
    d_own = [stacked(d3[s, qd, cut(2, ROWS)]) for s in range(2)]
    e_own = [stacked(e3[s, qd, cut(1, ROWS)]) for s in range(2)]
    h_own = [stacked(jdelta[s, qm, :]) for s in range(2)]
    for b in range(3):
        part = sum(
            dot_nt(e_own[s], j3[s, b * JOINT : (b + 1) * JOINT, cut(3, ROWS + 2)])
            for s in range(2)
        )
        for a in range(3):
            put(0, (3 * a + b) * JOINT, part[a * OQ : (a + 1) * OQ])
    column = 9 * JOINT
    part = sum(dot_nt(d_own[s], m3[s, :, cut(2, ROWS + 2)]) for s in range(2))
    for a in range(3):
        put(0, column + a * 3 * MIX, part[a * OQ : (a + 1) * OQ])
    column += 9 * MIX
    part = sum(dot_nt(h_own[s], x3[s, :, cut(4, ROWS + 2)]) for s in range(2))
    for a in range(3):
        h = part[a * MQ : (a + 1) * MQ]
        put(0, column + a * 3 * LEV, h[:64])
        spare = column + 9 * LEV
        for c in range(3):
            at = a * 3 * LEV + c * LEV
            piece = h[64:, c * LEV : (c + 1) * LEV]
            if at < 640:
                put(0, spare + at, piece)
            else:
                put(32, spare + at - 640, piece)
    put(32, column + 9 * LEV + 512, jnp.zeros((32, 128), F32))
    column += 9 * LEV + 640
    g = sum(dot_nt(jdelta[s, q, :], p9[s, :, cut(4, ROWS)]) for s in range(2))
    head = scale * sum(
        dot_nt(
            dout[s, q, :],
            jnp.concatenate([mid[s, r, LEV:] for r in range(ROWS)], axis=1),
        )
        for s in range(2)
    )
    tail = 8 * WIDE - column
    put(0, column, jnp.concatenate([g, head, jnp.zeros((OQ, tail - 10 * SLAB), F32)], axis=1))
    keep[...] = out[:4]
    send[...] = out[4:]


def main(place, pieces, lift_weight, patch_turned, head_weight, *weights):
    smem = pl.BlockSpec(memory_space=pltpu.SMEM)
    vmem = pl.BlockSpec(memory_space=pltpu.VMEM)
    hbm = pl.BlockSpec(memory_space=pl.ANY)
    return pl.pallas_call(
        main_kernel,
        out_shape=(jax.ShapeDtypeStruct((4, OQ, WIDE), BF),) * 2,
        in_specs=[smem] + [vmem] * 8 + [hbm] * 4,
        out_specs=(vmem, vmem),
        scratch_shapes=[
            pltpu.VMEM((8, OQ, WIDE), BF),
            pltpu.VMEM((MESO, 9 * MESO), BF),
            pltpu.VMEM((TERR, 9 * TERR), BF),
            pltpu.VMEM((MIX, 9 * JOINT), BF),
            pltpu.VMEM((MIX, 9 * MIX), BF),
            pltpu.VMEM((MESO, 9 * LEV), BF),
            pltpu.VMEM((TERR, 9 * SLAB), BF),
            pltpu.VMEM((JOINT, 9 * MIX), BF),
            pltpu.VMEM((MIX, 9 * MIX), BF),
            pltpu.SemaphoreType.DMA((4,)),
            pltpu.VMEM((2, 3 * LEV, (ROWS + 2 * HALO) * COLS), BF),
            pltpu.VMEM((2, 9 * SLAB, (ROWS + 8) * COLS), BF),
            pltpu.VMEM((2, 3 * JOINT, (ROWS + 8) * COLS), BF),
            pltpu.VMEM((2, JOINT, ROWS * COLS), F32),
            pltpu.VMEM((2, JOINT, ROWS * COLS), BF),
            pltpu.VMEM((2, 3 * MIX, (ROWS + 6) * COLS), BF),
            pltpu.VMEM((2, MIX, (ROWS + 6) * COLS), F32),
            pltpu.VMEM((2, MIX, ROWS * COLS), BF),
            pltpu.VMEM((2, 3 * MIX, (ROWS + 4) * COLS), BF),
            pltpu.VMEM((2, 3 * MIX, (ROWS + 2) * COLS), BF),
        ],
        compiler_params=params(56),
        cost_estimate=pl.CostEstimate(
            flops=19_000_000_000, bytes_accessed=14_000_000, transcendentals=3_000_000
        ),
        name="sections",
    )(place, *pieces, lift_weight, patch_turned, head_weight, *weights)


def split_kernel(keep, came, own, next1, next2, next3):
    own[...] = keep[0].astype(F32) + came[0].astype(F32)
    for j, to in enumerate((next1, next2, next3), 1):
        to[...] = (keep[j].astype(F32) + came[j].astype(F32)).astype(BF)


def total_kernel(own, one, two, three, out):
    out[...] = (
        (own[...].astype(F32) + two[...].astype(F32))
        + (one[...].astype(F32) + three[...].astype(F32))
    ).astype(BF)


def stack_kernel(own, one, two, three, out):
    for j, v in enumerate((own, one, two, three)):
        out[j] = v[...]


def small(kernel, out_shape, *operands):
    return pl.pallas_call(
        kernel, out_shape=out_shape, compiler_params=params(16), name=kernel.__name__[:-7]
    )(*operands)


def by_space(v, by):
    return lax.ppermute(v, "space", [(i, (i + 2 * by) % 8) for i in range(8)])


def to_partner(v):
    return lax.ppermute(v, "space", [(i, i ^ 1) for i in range(8)])


def by_depth(v, by):
    return lax.ppermute(v, "dp", [(i, (i + by) % 4) for i in range(4)])


def across(v, by, chip_core):
    pairs = []
    for seg in range(4):
        for place in range(8):
            if place % 2 == chip_core:
                to = (seg, (place + 2 * by) % 8)
            else:
                to = ((seg + by) % 4, place)
            pairs.append((seg * 8 + place, to[0] * 8 + to[1]))
    return lax.ppermute(v, ("segment", "space"), pairs)


STEPS = (0, -1, 1, -2)


def summed_everywhere(keep, send):
    piece = jax.ShapeDtypeStruct((OQ, WIDE), BF)
    wide = jax.ShapeDtypeStruct((OQ, WIDE), F32)
    own, *parts = small(split_kernel, (wide, piece, piece, piece), keep, to_partner(send))
    own = small(total_kernel, piece, own, *[by_space(p, j) for j, p in enumerate(parts, 1)])
    own = small(total_kernel, piece, own, *[by_depth(own, j) for j in (1, 2, 3)])
    four = jax.ShapeDtypeStruct((4, OQ, WIDE), BF)
    block = small(stack_kernel, four, own, *[across(own, j, 0) for j in (1, 2, 3)])
    behind, ahead = across(block, 1, 1), across(block, -1, 1)
    mine = (block, behind, ahead, across(behind, 1, 1))
    return mine + tuple(to_partner(v) for v in mine)


def finish_kernel(place, *refs):
    blocks, (lw, pw, mw_hbm, tw_hbm) = refs[:8], refs[8:12]
    patch, lift, head, terrain, meso, merging, decoder = refs[12:19]
    mw, tw, stage, wide_m, wide_t, ht, gt, sems = refs[19:]
    reads = [
        pltpu.make_async_copy(mw_hbm, mw, sems.at[0]),
        pltpu.make_async_copy(tw_hbm, tw, sems.at[1]),
    ]
    for copy in reads:
        copy.start()
    segment, chip, core = place[0], place[1] // 2, place[1] % 2
    for i, block in enumerate(blocks):
        kind = core if i < 4 else 1 - core
        for j in range(4):
            along_space = jnp.where(kind == 0, -j, STEPS[i % 4])
            along_segment = jnp.where(kind == 0, STEPS[i % 4], -j)
            group = 4 * kind + lax.rem(chip + along_space + 4, 4)
            row = lax.rem(segment + along_segment + 4, 4) * OQ
            stage[
                pl.ds(pl.multiple_of(row, OQ), OQ), pl.ds(pl.multiple_of(group * WIDE, WIDE), WIDE)
            ] = block[j].astype(F32)
    column = 9 * JOINT + 9 * MIX
    writes = [
        pltpu.make_async_copy(stage.at[:, : 9 * JOINT], merging, sems.at[2]),
        pltpu.make_async_copy(stage.at[:, 9 * JOINT : column], decoder, sems.at[3]),
    ]
    for copy in writes:
        copy.start()
    for seg in range(4):
        lo = seg * OQ
        at = seg * MQ
        ht[at : at + 64, :] = stage[lo : lo + OQ, column : column + 9 * LEV].astype(BF)
        spare = column + 9 * LEV
        ht[at + 64 : at + MQ, :640] = stage[lo : lo + 32, spare : spare + 640].astype(BF)
        ht[at + 64 : at + MQ, 640:] = stage[lo + 32 : lo + OQ, spare : spare + 512].astype(BF)
        gt[lo : lo + OQ, :] = stage[lo : lo + OQ, spare + 640 : spare + 896]
    for a in range(3):
        for tap in range(3 * a, 3 * a + 3):
            wide_m[:, tap * MESO : (tap + 1) * MESO] = dot_nt(
                ht[:, tap * LEV : (tap + 1) * LEV], lw[...]
            )
        part = slice(3 * a * MESO, 3 * (a + 1) * MESO)
        writes.append(pltpu.make_async_copy(wide_m.at[:, part], meso.at[:, part], sems.at[4 + a]))
        writes[-1].start()
    pw16 = sixteen(pw[...], 0).astype(BF)
    g = gt[...]
    for tap in range(9):
        wide_t[:, tap * TERR : (tap + 1) * TERR] = dot(
            g[:, tap * SLAB : (tap + 1) * SLAB].astype(BF), pw16
        )
    writes.append(pltpu.make_async_copy(wide_t, terrain, sems.at[7]))
    writes[-1].start()
    turned = g.T
    head[...] = turned[9 * SLAB + 8 : 9 * SLAB + 11, :]
    reads[1].wait()
    patch[...] = sum(
        dot(
            turned[tap * SLAB : (tap + 1) * SLAB, :].astype(BF),
            tw[:, tap * TERR : (tap + 1) * TERR],
        )
        for tap in range(9)
    )[:8]
    turned = ht[...].astype(F32).T.astype(BF)
    reads[0].wait()
    lift[...] = sum(
        dot(turned[tap * LEV : (tap + 1) * LEV, :], mw[:, tap * MESO : (tap + 1) * MESO])
        for tap in range(9)
    ).T
    for copy in writes:
        copy.wait()


def finish(place, blocks, lift_weight, patch_turned, meso_weight, terrain_weight):
    smem = pl.BlockSpec(memory_space=pltpu.SMEM)
    vmem = pl.BlockSpec(memory_space=pltpu.VMEM)
    hbm = pl.BlockSpec(memory_space=pl.ANY)
    patch, lift, head, terrain, meso, merging, decoder = pl.pallas_call(
        finish_kernel,
        out_shape=(
            jax.ShapeDtypeStruct((8, TERR), F32),
            jax.ShapeDtypeStruct((MESO, LEV), F32),
            jax.ShapeDtypeStruct((3, MIX), F32),
            jax.ShapeDtypeStruct((TERR, 9 * TERR), F32),
            jax.ShapeDtypeStruct((MESO, 9 * MESO), F32),
            jax.ShapeDtypeStruct((MIX, 9 * JOINT), F32),
            jax.ShapeDtypeStruct((MIX, 9 * MIX), F32),
        ),
        in_specs=[smem] + [vmem] * 10 + [hbm] * 2,
        out_specs=(vmem,) * 3 + (hbm,) * 4,
        scratch_shapes=[
            pltpu.VMEM((MESO, 9 * MESO), BF),
            pltpu.VMEM((TERR, 9 * TERR), BF),
            pltpu.VMEM((MIX, 8 * WIDE), F32),
            pltpu.VMEM((MESO, 9 * MESO), F32),
            pltpu.VMEM((TERR, 9 * TERR), F32),
            pltpu.VMEM((MESO, 9 * LEV), BF),
            pltpu.VMEM((MIX, 256), F32),
            pltpu.SemaphoreType.DMA((8,)),
        ],
        compiler_params=params(40),
        name="finish",
    )(place, *blocks, lift_weight, patch_turned, meso_weight, terrain_weight)
    return patch.T, terrain, lift, meso, merging, decoder, head


def packed(terrain_in, meso_in, wind_cot):
    samples = terrain_in.shape[0]
    source = lax.broadcasted_iota(jnp.int32, (2 * COLS, 2 * COLS), 0)
    target = lax.broadcasted_iota(jnp.int32, (2 * COLS, 2 * COLS), 1)
    pick = (source == 2 * (target % COLS) + target // COLS).astype(BF)
    split = dot(terrain_in.reshape(samples * 4 * ROWS, 2 * COLS), pick).astype(BF)
    patches = (
        split.reshape(samples, 2, ROWS, 2, 2, COLS)
        .transpose(0, 2, 1, 3, 4, 5)
        .reshape(samples, ROWS, 8, COLS)
    )
    levels = meso_in.reshape(samples, LEV, ROWS, COLS).transpose(0, 2, 1, 3)
    cot = wind_cot.transpose(0, 2, 1, 3)
    rest = jnp.zeros((samples, ROWS, PACK - LEV - 11, COLS), BF)
    return jnp.concatenate([levels, patches, cot, rest], axis=2)


def shifted(v, by):
    count = lax.axis_size("space")
    return lax.ppermute(
        v, "space", [(i, i + by) for i in range(count) if 0 <= i + by < count]
    )


def local(
    terrain_in,
    meso_in,
    wind_cot,
    patch_weight,
    terrain_weight,
    lift_weight,
    meso_weight,
    merging_weight,
    decoder_weight,
    head_weight,
):
    own = packed(terrain_in, meso_in, wind_cot)
    up, down = shifted(own, 1), shifted(own, -1)
    far_up, far_down = shifted(own[:, 3:], 2), shifted(own[:, :1], -2)
    place = jnp.stack([lax.axis_index("segment"), lax.axis_index("space")]).astype(jnp.int32)
    keep, send = main(
        place,
        (far_up, up, own, down, far_down),
        lift_weight,
        patch_weight.T,
        head_weight,
        meso_weight,
        terrain_weight,
        merging_weight,
        decoder_weight,
    )
    blocks = summed_everywhere(keep, send)
    return finish(place, blocks, lift_weight, patch_weight.T, meso_weight, terrain_weight)


def solution(mesh):
    placed = (
        P("dp", None, "space", None),
        P("dp", None, None, "space", None),
        P("dp", None, "space", None),
        P(),
        P(),
        P(),
        P(),
        P(),
        P(),
        P(),
    )
    return jax.shard_map(
        local,
        mesh=mesh,
        in_specs=placed,
        out_specs=(P(), P(), P(), P(), P(), P(), P()),
        check_vma=False,
    )
```

time: 201 us -> 127 us (0.63)
  blocking collectives: 28.5 us -> 0 us
  starting transfers between devices: 11.8 us -> 36.5 us
  waiting for transfers between devices: 65.4 us -> 43.6 us
  Pallas kernels: 60.5 us -> 41.3 us
  between operations: 14.2 us -> 1.02 us
  local copies, waits for them, and re-layouts: 16.3 us -> 3.74 us
  other arithmetic: 3.09 us -> 0.81 us
    all_gather x1 -> x0, waiting for transfers between devices: 65.4 us -> none  [local(): got = lax.all_gather(mine, ('segment', 'dp', 'space'))]
    ppermute x0 -> x17, waiting for transfers between devices: none -> 42.2 us  [the longest x6 22.2 us: across(): return lax.ppermute(v, ('segment', 'space'), pairs)]
    all_to_all x1 -> x0, blocking collectives: 28.5 us -> none  [local(): parts = lax.all_to_all(parts, ('dp', 'space'), 0, 0, tiled=True)]
    ppermute x0 -> x17, starting transfers between devices: none -> 24.7 us  [the longest x5 7.78 us: to_partner(): return lax.ppermute(v, 'space', [(i, i ^ 1) for i in range(8)])]
    pallas_call x3 -> x6, Pallas kernels: 60.5 us -> 41.3 us  [the longest x1 32.8 us: main(): pl.pallas_call(main_kernel, out_shape=(jax.ShapeDtypeStruct((4, OQ, WIDE)...]
    unnamed x31 -> x26, local copies, waits for them, and re-layouts: 14.2 us -> 3.61 us
    reduce_sum x1 -> x0, other arithmetic: 2.13 us -> none  [local(): mine = jnp.sum(parts.astype(F32), axis=0).astype(BF)]
  transfers between devices with their start and end apart: 5 -> 21, of which waited for: 1 -> 12; matrix products, arithmetic and copies ran while one was open for 2% -> 1% of each run, Pallas kernels for 1% -> 0%
where the time goes in v2:
time: 127 us
  waiting for transfers between devices  43.6 us (34%)
  Pallas kernels  41.3 us (33%)
  starting transfers between devices  36.5 us (29%)
  local copies, waits for them, and re-layouts  3.74 us (3%)
    pallas_call x1, Pallas kernels, main(): pl.pallas_call(main_kernel, out_shape=(jax.ShapeDtypeStruct((4, OQ, WIDE)...  32.8 us
    ppermute x6, waiting for transfers between devices, across(): return lax.ppermute(v, ('segment', 'space'), pairs)  22.2 us
    ppermute x4, starting transfers between devices, shifted(): lax.ppermute(v, 'space', [(i, i + by) for i in range(count) if 0 <= i + b...  11.8 us
    ppermute x3, waiting for transfers between devices, by_depth(): return lax.ppermute(v, 'dp', [(i, (i + by) % 4) for i in range(4)])  9.79 us
    pallas_call x1, Pallas kernels, finish(): pl.pallas_call(finish_kernel, out_shape=(jax.ShapeDtypeStruct((8, TERR),...  8.14 us
    ppermute x5, starting transfers between devices, to_partner(): return lax.ppermute(v, 'space', [(i, i ^ 1) for i in range(8)])  7.78 us
    ppermute x3, waiting for transfers between devices, by_space(): return lax.ppermute(v, 'space', [(i, (i + 2 * by) % 8) for i in range(8)])  6.56 us
    ppermute x6, starting transfers between devices, across(): return lax.ppermute(v, ('segment', 'space'), pairs)  6.42 us
  transfers between devices with their start and end apart: 21, of which 12 were waited for; matrix products, arithmetic and copies ran while one was open for 1% of the time, Pallas kernels for 0%

profile of v2, /device:TPU:1, one launch (start us, length us, event | category | flops | bytes accessed | tf_op | source)
XLA Modules:
  0.0 127.1 jit_solution(14877259325132668572)
XLA Ops:
  2.8 3.3 %collective-permute-start.2 = (bf16[2,4,144,128]{3,2,1,0:T(8,128)(2,1)S(1)}, bf16[2,4,144,128]{3,2,1,0:T(8,128)(2,1)S(1)}, u32[]{:S(2)}, u32[]{:S(2)}) collective-permute-start(bf16[2,4,144,128]{3,2,1,0:T(8,128)(2,1)S(1)} %maximum_maximum_fusion.mid), channel_id=1, source_target_pairs={{1,0},{2,1},{3,2},{4,3},{5,4},{6,5},{7,6},{9,8},{10,9},{11,10},{12... | collective-permute-start | bytes 884744 | tf_op jit(solution)/shard_map/ppermute | solution.py:492
  6.2 3.2 %collective-permute-start.1 = (bf16[2,4,144,128]{3,2,1,0:T(8,128)(2,1)S(1)}, bf16[2,4,144,128]{3,2,1,0:T(8,128)(2,1)S(1)}, u32[]{:S(2)}, u32[]{:S(2)}) collective-permute-start(bf16[2,4,144,128]{3,2,1,0:T(8,128)(2,1)S(1)} %maximum_maximum_fusion.mid), channel_id=1, source_target_pairs={{0,1},{1,2},{2,3},{3,4},{4,5},{5,6},{6,7},{8,9},{9,10},{10,11},{11... | collective-permute-start | bytes 884744 | tf_op jit(solution)/shard_map/ppermute | solution.py:492
  10.7 4.0 %collective-permute-start = (bf16[2,1,144,128]{3,2,1,0:T(8,128)(2,1)S(1)}, bf16[2,1,144,128]{3,2,1,0:T(8,128)(2,1)S(1)}, u32[]{:S(2)}, u32[]{:S(2)}) collective-permute-start(bf16[2,1,144,128]{3,2,1,0:T(8,128)(2,1)S(1)} %get-tuple-element.34), channel_id=1, source_target_pairs={{0,2},{1,3},{2,4},{3,5},{4,6},{5,7},{8,10},{9,11},{10,12},{11,13},... | collective-permute-start | bytes 221192 | tf_op jit(solution)/shard_map/ppermute | solution.py:492
  15.3 1.4 %collective-permute-done.far_up = bf16[2,1,144,128]{3,2,1,0:T(8,128)(2,1)S(1)} collective-permute-done((bf16[2,1,144,128]{3,2,1,0:T(8,128)(2,1)S(1)}, bf16[2,1,144,128]{3,2,1,0:T(8,128)(2,1)S(1)}, u32[]{:S(2)}, u32[]{:S(2)}) %collective-permute-start) | collective-permute-done | bytes 73760 | tf_op jit(solution)/shard_map/ppermute | solution.py:492
  17.6 32.8 %sections.1 = (bf16[4,64,1280]{2,1,0:T(8,128)(2,1)}, bf16[4,64,1280]{2,1,0:T(8,128)(2,1)}) custom-call(s32[2]{0:T(128)} %pad_add_fusion.place, bf16[2,1,144,128]{3,2,1,0:T(8,128)(2,1)} %copy-done.11, bf16[2,4,144,128]{3,2,1,0:T(8,128)(2,1)} %copy-done.9, bf16[2,4,144,128]{3,2,1,0:T(8,128)(2,1)} %copy-done.7, bf16[2,4,144,128]{3,2,1,0:T(8,128)(2,1)} %copy-done.8, ...), custom_call_target="tpu_custom_call" | custom-call | flops 19000000512 | bytes 14000000 | tf_op jit(solution)/shard_map/sections/pallas_call | solution.py:269
  50.9 1.9 %collective-permute-done.4.came = bf16[4,64,1280]{2,1,0:T(8,128)(2,1)S(1)} collective-permute-done((bf16[4,64,1280]{2,1,0:T(8,128)(2,1)}, bf16[4,64,1280]{2,1,0:T(8,128)(2,1)S(1)}, u32[]{:S(2)}, u32[]{:S(2)}) %collective-permute-start.4) | collective-permute-done | bytes 655392 | tf_op jit(solution)/shard_map/ppermute | solution.py:333
  54.0 2.3 %collective-permute-start.5 = (bf16[64,1280]{1,0:T(8,128)(2,1)S(1)}, bf16[64,1280]{1,0:T(8,128)(2,1)S(1)}, u32[]{:S(2)}, u32[]{:S(2)}) collective-permute-start(bf16[64,1280]{1,0:T(8,128)(2,1)S(1)} %get-tuple-element.23), channel_id=1, source_target_pairs={{0,2},{1,3},{2,4},{3,5},{4,6},{5,7},{6,0},{7,1},{8,10},{9,11},{10,... | collective-permute-start | bytes 491528 | tf_op jit(solution)/shard_map/ppermute | solution.py:329
  56.3 2.8 %collective-permute-start.6 = (bf16[64,1280]{1,0:T(8,128)(2,1)S(1)}, bf16[64,1280]{1,0:T(8,128)(2,1)S(1)}, u32[]{:S(2)}, u32[]{:S(2)}) collective-permute-start(bf16[64,1280]{1,0:T(8,128)(2,1)S(1)} %get-tuple-element.24), channel_id=1, source_target_pairs={{0,4},{1,5},{2,6},{3,7},{4,0},{5,1},{6,2},{7,3},{8,12},{9,13},{10,... | collective-permute-start | bytes 491528 | tf_op jit(solution)/shard_map/ppermute | solution.py:329
  60.0 2.2 %collective-permute-done.5.one = bf16[64,1280]{1,0:T(8,128)(2,1)S(1)} collective-permute-done((bf16[64,1280]{1,0:T(8,128)(2,1)S(1)}, bf16[64,1280]{1,0:T(8,128)(2,1)S(1)}, u32[]{:S(2)}, u32[]{:S(2)}) %collective-permute-start.5) | collective-permute-done | bytes 163872 | tf_op jit(solution)/shard_map/ppermute | solution.py:329
  62.2 4.4 %collective-permute-done.6.two = bf16[64,1280]{1,0:T(8,128)(2,1)S(1)} collective-permute-done((bf16[64,1280]{1,0:T(8,128)(2,1)S(1)}, bf16[64,1280]{1,0:T(8,128)(2,1)S(1)}, u32[]{:S(2)}, u32[]{:S(2)}) %collective-permute-start.6) | collective-permute-done | bytes 163872 | tf_op jit(solution)/shard_map/ppermute | solution.py:329
  66.7 3.8 %collective-permute-start.10 = (bf16[64,1280]{1,0:T(8,128)(2,1)S(1)}, bf16[64,1280]{1,0:T(8,128)(2,1)S(1)}, u32[]{:S(2)}, u32[]{:S(2)}) collective-permute-start(bf16[64,1280]{1,0:T(8,128)(2,1)S(1)} %total.2.own), channel_id=1, source_target_pairs={{0,96},{32,0},{64,32},{96,64},{1,97},{33,1},{65,33},{97,65},{2,98}... | collective-permute-start | bytes 491528 | tf_op jit(solution)/shard_map/ppermute | solution.py:337
  71.2 5.6 %collective-permute-done.10.three = bf16[64,1280]{1,0:T(8,128)(2,1)S(1)} collective-permute-done((bf16[64,1280]{1,0:T(8,128)(2,1)S(1)}, bf16[64,1280]{1,0:T(8,128)(2,1)S(1)}, u32[]{:S(2)}, u32[]{:S(2)}) %collective-permute-start.10) | collective-permute-done | bytes 163872 | tf_op jit(solution)/shard_map/ppermute | solution.py:337
  76.8 4.2 %collective-permute-done.8.one = bf16[64,1280]{1,0:T(8,128)(2,1)S(1)} collective-permute-done((bf16[64,1280]{1,0:T(8,128)(2,1)S(1)}, bf16[64,1280]{1,0:T(8,128)(2,1)S(1)}, u32[]{:S(2)}, u32[]{:S(2)}) %collective-permute-start.8) | collective-permute-done | bytes 163872 | tf_op jit(solution)/shard_map/ppermute | solution.py:337
  81.1 2.5 %collective-permute-start.13 = (bf16[64,1280]{1,0:T(8,128)(2,1)S(1)}, bf16[64,1280]{1,0:T(8,128)(2,1)S(1)}, u32[]{:S(2)}, u32[]{:S(2)}) collective-permute-start(bf16[64,1280]{1,0:T(8,128)(2,1)S(1)} %total.3.own), channel_id=1, source_target_pairs={{0,6},{1,25},{2,0},{3,27},{4,2},{5,29},{6,4},{7,31},{8,14},{9,1},{... | collective-permute-start | bytes 491528 | tf_op jit(solution)/shard_map/ppermute | solution.py:349
  84.7 2.9 %collective-permute-done.13.three = bf16[64,1280]{1,0:T(8,128)(2,1)S(1)} collective-permute-done((bf16[64,1280]{1,0:T(8,128)(2,1)S(1)}, bf16[64,1280]{1,0:T(8,128)(2,1)S(1)}, u32[]{:S(2)}, u32[]{:S(2)}) %collective-permute-start.13) | collective-permute-done | bytes 163872 | tf_op jit(solution)/shard_map/ppermute | solution.py:349
  87.6 2.0 %collective-permute-done.12.two = bf16[64,1280]{1,0:T(8,128)(2,1)S(1)} collective-permute-done((bf16[64,1280]{1,0:T(8,128)(2,1)S(1)}, bf16[64,1280]{1,0:T(8,128)(2,1)S(1)}, u32[]{:S(2)}, u32[]{:S(2)}) %collective-permute-start.12) | collective-permute-done | bytes 163872 | tf_op jit(solution)/shard_map/ppermute | solution.py:349
  89.6 1.8 %collective-permute-done.11.one = bf16[64,1280]{1,0:T(8,128)(2,1)S(1)} collective-permute-done((bf16[64,1280]{1,0:T(8,128)(2,1)S(1)}, bf16[64,1280]{1,0:T(8,128)(2,1)S(1)}, u32[]{:S(2)}, u32[]{:S(2)}) %collective-permute-start.11) | collective-permute-done | bytes 163872 | tf_op jit(solution)/shard_map/ppermute | solution.py:349
  92.3 1.8 %collective-permute-start.15 = (bf16[4,64,1280]{2,1,0:T(8,128)(2,1)S(1)}, bf16[4,64,1280]{2,1,0:T(8,128)(2,1)S(1)}, u32[]{:S(2)}, u32[]{:S(2)}) collective-permute-start(bf16[4,64,1280]{2,1,0:T(8,128)(2,1)S(1)} %stack.13.refs_0_), channel_id=1, source_target_pairs={{0,24},{1,7},{2,26},{3,1},{4,28},{5,3},{6,30},{7,5},{8,0},{9,15},{... | collective-permute-start | bytes 1966088 | tf_op jit(solution)/shard_map/ppermute | solution.py:349
  94.1 8.3 %collective-permute-done.14.refs_1_ = bf16[4,64,1280]{2,1,0:T(8,128)(2,1)S(1)} collective-permute-done((bf16[4,64,1280]{2,1,0:T(8,128)(2,1)S(1)}, bf16[4,64,1280]{2,1,0:T(8,128)(2,1)S(1)}, u32[]{:S(2)}, u32[]{:S(2)}) %collective-permute-start.14) | collective-permute-done | bytes 655392 | tf_op jit(solution)/shard_map/ppermute | solution.py:349
  102.4 3.1 %collective-permute-start.17 = (bf16[4,64,1280]{2,1,0:T(8,128)(2,1)S(1)}, bf16[4,64,1280]{2,1,0:T(8,128)(2,1)S(1)}, u32[]{:S(2)}, u32[]{:S(2)}) collective-permute-start(bf16[4,64,1280]{2,1,0:T(8,128)(2,1)S(1)} %stack.13.refs_0_), channel_id=1, source_target_pairs={{0,1},{1,0},{2,3},{3,2},{4,5},{5,4},{6,7},{7,6},{8,9},{9,8},{10,11... | collective-permute-start | bytes 1966088 | tf_op jit(solution)/shard_map/ppermute | solution.py:333
  106.0 7.3 %collective-permute-done.16.refs_3_ = bf16[4,64,1280]{2,1,0:T(8,128)(2,1)S(1)} collective-permute-done((bf16[4,64,1280]{2,1,0:T(8,128)(2,1)S(1)}, bf16[4,64,1280]{2,1,0:T(8,128)(2,1)S(1)}, u32[]{:S(2)}, u32[]{:S(2)}) %collective-permute-start.16) | collective-permute-done | bytes 655392 | tf_op jit(solution)/shard_map/ppermute | solution.py:349
  113.4 3.7 %collective-permute-start.20 = (bf16[4,64,1280]{2,1,0:T(8,128)(2,1)S(1)}, bf16[4,64,1280]{2,1,0:T(8,128)(2,1)S(1)}, u32[]{:S(2)}, u32[]{:S(2)}) collective-permute-start(bf16[4,64,1280]{2,1,0:T(8,128)(2,1)S(1)} %collective-permute-done.16.refs_3_), channel_id=1, source_target_pairs={{0,1},{1,0},{2,3},{3,2},{4,5},{5,4},{6,7},{7,6},{8,9},{9,8},{10,11... | collective-permute-start | bytes 1966088 | tf_op jit(solution)/shard_map/ppermute | solution.py:333
  117.1 1.7 %collective-permute-done.20.refs_7_ = bf16[4,64,1280]{2,1,0:T(8,128)(2,1)S(1)} collective-permute-done((bf16[4,64,1280]{2,1,0:T(8,128)(2,1)S(1)}, bf16[4,64,1280]{2,1,0:T(8,128)(2,1)S(1)}, u32[]{:S(2)}, u32[]{:S(2)}) %collective-permute-start.20) | collective-permute-done | bytes 655392 | tf_op jit(solution)/shard_map/ppermute | solution.py:333
  118.8 8.1 %finish.1 = (f32[8,256]{1,0:T(8,128)}, f32[384,128]{1,0:T(8,128)}, f32[3,256]{1,0:T(4,128)}, f32[256,2304]{1,0:T(8,128)}, f32[384,3456]{1,0:T(8,128)}, /*index=5*/f32[256,5760]{1,0:T(8,128)}, f32[256,2304]{1,0:T(8,128)}) custom-call(s32[2]{0:T(128)S(1)} %copy-done.6, bf16[4,64,1280]{2,1,0:T(8,128)(2,1)S(1)} %stack.13.refs_0_, ...), custom_call_target="tpu_custom_call" | custom-call | tf_op jit(solution)/shard_map/finish/pallas_call | solution.py:444
  (61 shorter events, 11.0 us)
Async XLA Ops:
  2.8 13.9 %collective-permute-start.2 = (bf16[2,4,144,128]{3,2,1,0:T(8,128)(2,1)S(1)}, bf16[2,4,144,128]{3,2,1,0:T(8,128)(2,1)S(1)}, u32[]{:S(2)}, u32[]{:S(2)}) collective-permute-start(bf16[2,4,144,128]{3,2,1,0:T(8,128)(2,1)S(1)} %maximum_maximum_fusion.mid), channel_id=1, source_target_pairs={{1,0},{2,1},{3,2},{4,3},{5,4},{6,5},{7,6},{9,8},{10,9},{11,10},{12... | collective-permute-start | bytes 884744 | tf_op jit(solution)/shard_map/ppermute | solution.py:492
  6.2 10.6 %collective-permute-start.1 = (bf16[2,4,144,128]{3,2,1,0:T(8,128)(2,1)S(1)}, bf16[2,4,144,128]{3,2,1,0:T(8,128)(2,1)S(1)}, u32[]{:S(2)}, u32[]{:S(2)}) collective-permute-start(bf16[2,4,144,128]{3,2,1,0:T(8,128)(2,1)S(1)} %maximum_maximum_fusion.mid), channel_id=1, source_target_pairs={{0,1},{1,2},{2,3},{3,4},{4,5},{5,6},{6,7},{8,9},{9,10},{10,11},{11... | collective-permute-start | bytes 884744 | tf_op jit(solution)/shard_map/ppermute | solution.py:492
  9.4 6.0 %collective-permute-start.3 = (bf16[2,1,144,128]{3,2,1,0:T(8,128)(2,1)S(1)}, bf16[2,1,144,128]{3,2,1,0:T(8,128)(2,1)S(1)}, u32[]{:S(2)}, u32[]{:S(2)}) collective-permute-start(bf16[2,1,144,128]{3,2,1,0:T(8,128)(2,1)S(1)} %get-tuple-element.33), channel_id=1, source_target_pairs={{2,0},{3,1},{4,2},{5,3},{6,4},{7,5},{10,8},{11,9},{12,10},{13,11},... | collective-permute-start | bytes 221192 | tf_op jit(solution)/shard_map/ppermute | solution.py:492
  10.7 6.1 %collective-permute-start = (bf16[2,1,144,128]{3,2,1,0:T(8,128)(2,1)S(1)}, bf16[2,1,144,128]{3,2,1,0:T(8,128)(2,1)S(1)}, u32[]{:S(2)}, u32[]{:S(2)}) collective-permute-start(bf16[2,1,144,128]{3,2,1,0:T(8,128)(2,1)S(1)} %get-tuple-element.34), channel_id=1, source_target_pairs={{0,2},{1,3},{2,4},{3,5},{4,6},{5,7},{8,10},{9,11},{10,12},{11,13},... | collective-permute-start | bytes 221192 | tf_op jit(solution)/shard_map/ppermute | solution.py:492
  17.6 101.2 %copy-start.4 = (bf16[384,128]{1,0:T(8,128)(2,1)S(1)}, bf16[384,128]{1,0:T(8,128)(2,1)}, u32[]{:S(2)}) copy-start(bf16[384,128]{1,0:T(8,128)(2,1)} %refs_8_.1) | copy-start | bytes 294916
  17.6 101.2 %copy-start.5 = (bf16[256,8]{0,1:T(8,128)(2,1)S(1)}, bf16[256,8]{0,1:T(8,128)(2,1)}, u32[]{:S(2)}) copy-start(bf16[256,8]{0,1:T(8,128)(2,1)} %param.13) | copy-start | bytes 12292
  17.6 101.2 %copy-start.6 = (s32[2]{0:T(128)S(1)}, s32[2]{0:T(128)}, u32[]{:S(2)}) copy-start(s32[2]{0:T(128)} %pad_add_fusion.place) | copy-start | bytes 28
  50.4 2.4 %collective-permute-start.4 = (bf16[4,64,1280]{2,1,0:T(8,128)(2,1)}, bf16[4,64,1280]{2,1,0:T(8,128)(2,1)S(1)}, u32[]{:S(2)}, u32[]{:S(2)}) collective-permute-start(bf16[4,64,1280]{2,1,0:T(8,128)(2,1)} %get-tuple-element.21), channel_id=1, source_target_pairs={{0,1},{1,0},{2,3},{3,2},{4,5},{5,4},{6,7},{7,6},{8,9},{9,8},{10,11... | collective-permute-start | bytes 1966088 | tf_op jit(solution)/shard_map/ppermute | solution.py:333
  54.0 8.2 %collective-permute-start.5 = (bf16[64,1280]{1,0:T(8,128)(2,1)S(1)}, bf16[64,1280]{1,0:T(8,128)(2,1)S(1)}, u32[]{:S(2)}, u32[]{:S(2)}) collective-permute-start(bf16[64,1280]{1,0:T(8,128)(2,1)S(1)} %get-tuple-element.23), channel_id=1, source_target_pairs={{0,2},{1,3},{2,4},{3,5},{4,6},{5,7},{6,0},{7,1},{8,10},{9,11},{10,... | collective-permute-start | bytes 491528 | tf_op jit(solution)/shard_map/ppermute | solution.py:329
  56.3 10.3 %collective-permute-start.6 = (bf16[64,1280]{1,0:T(8,128)(2,1)S(1)}, bf16[64,1280]{1,0:T(8,128)(2,1)S(1)}, u32[]{:S(2)}, u32[]{:S(2)}) collective-permute-start(bf16[64,1280]{1,0:T(8,128)(2,1)S(1)} %get-tuple-element.24), channel_id=1, source_target_pairs={{0,4},{1,5},{2,6},{3,7},{4,0},{5,1},{6,2},{7,3},{8,12},{9,13},{10,... | collective-permute-start | bytes 491528 | tf_op jit(solution)/shard_map/ppermute | solution.py:329
  59.1 7.5 %collective-permute-start.7 = (bf16[64,1280]{1,0:T(8,128)(2,1)S(1)}, bf16[64,1280]{1,0:T(8,128)(2,1)S(1)}, u32[]{:S(2)}, u32[]{:S(2)}) collective-permute-start(bf16[64,1280]{1,0:T(8,128)(2,1)S(1)} %get-tuple-element.25), channel_id=1, source_target_pairs={{0,6},{1,7},{2,0},{3,1},{4,2},{5,3},{6,4},{7,5},{8,14},{9,15},{10,... | collective-permute-start | bytes 491528 | tf_op jit(solution)/shard_map/ppermute | solution.py:329
  66.7 10.1 %collective-permute-start.10 = (bf16[64,1280]{1,0:T(8,128)(2,1)S(1)}, bf16[64,1280]{1,0:T(8,128)(2,1)S(1)}, u32[]{:S(2)}, u32[]{:S(2)}) collective-permute-start(bf16[64,1280]{1,0:T(8,128)(2,1)S(1)} %total.2.own), channel_id=1, source_target_pairs={{0,96},{32,0},{64,32},{96,64},{1,97},{33,1},{65,33},{97,65},{2,98}... | collective-permute-start | bytes 491528 | tf_op jit(solution)/shard_map/ppermute | solution.py:337
  70.5 6.3 %collective-permute-start.9 = (bf16[64,1280]{1,0:T(8,128)(2,1)S(1)}, bf16[64,1280]{1,0:T(8,128)(2,1)S(1)}, u32[]{:S(2)}, u32[]{:S(2)}) collective-permute-start(bf16[64,1280]{1,0:T(8,128)(2,1)S(1)} %total.2.own), channel_id=1, source_target_pairs={{0,64},{32,96},{64,0},{96,32},{1,65},{33,97},{65,1},{97,33},{2,66}... | collective-permute-start | bytes 491528 | tf_op jit(solution)/shard_map/ppermute | solution.py:337
  70.5 10.5 %collective-permute-start.8 = (bf16[64,1280]{1,0:T(8,128)(2,1)S(1)}, bf16[64,1280]{1,0:T(8,128)(2,1)S(1)}, u32[]{:S(2)}, u32[]{:S(2)}) collective-permute-start(bf16[64,1280]{1,0:T(8,128)(2,1)S(1)} %total.2.own), channel_id=1, source_target_pairs={{0,32},{32,64},{64,96},{96,0},{1,33},{33,65},{65,97},{97,1},{2,34}... | collective-permute-start | bytes 491528 | tf_op jit(solution)/shard_map/ppermute | solution.py:337
  81.1 6.6 %collective-permute-start.13 = (bf16[64,1280]{1,0:T(8,128)(2,1)S(1)}, bf16[64,1280]{1,0:T(8,128)(2,1)S(1)}, u32[]{:S(2)}, u32[]{:S(2)}) collective-permute-start(bf16[64,1280]{1,0:T(8,128)(2,1)S(1)} %total.3.own), channel_id=1, source_target_pairs={{0,6},{1,25},{2,0},{3,27},{4,2},{5,29},{6,4},{7,31},{8,14},{9,1},{... | collective-permute-start | bytes 491528 | tf_op jit(solution)/shard_map/ppermute | solution.py:349
  83.6 6.0 %collective-permute-start.12 = (bf16[64,1280]{1,0:T(8,128)(2,1)S(1)}, bf16[64,1280]{1,0:T(8,128)(2,1)S(1)}, u32[]{:S(2)}, u32[]{:S(2)}) collective-permute-start(bf16[64,1280]{1,0:T(8,128)(2,1)S(1)} %total.3.own), channel_id=1, source_target_pairs={{0,4},{1,17},{2,6},{3,19},{4,0},{5,21},{6,2},{7,23},{8,12},{9,25},... | collective-permute-start | bytes 491528 | tf_op jit(solution)/shard_map/ppermute | solution.py:349
  84.1 7.2 %collective-permute-start.11 = (bf16[64,1280]{1,0:T(8,128)(2,1)S(1)}, bf16[64,1280]{1,0:T(8,128)(2,1)S(1)}, u32[]{:S(2)}, u32[]{:S(2)}) collective-permute-start(bf16[64,1280]{1,0:T(8,128)(2,1)S(1)} %total.3.own), channel_id=1, source_target_pairs={{0,2},{1,9},{2,4},{3,11},{4,6},{5,13},{6,0},{7,15},{8,10},{9,17},{... | collective-permute-start | bytes 491528 | tf_op jit(solution)/shard_map/ppermute | solution.py:349
  91.4 11.0 %collective-permute-start.14 = (bf16[4,64,1280]{2,1,0:T(8,128)(2,1)S(1)}, bf16[4,64,1280]{2,1,0:T(8,128)(2,1)S(1)}, u32[]{:S(2)}, u32[]{:S(2)}) collective-permute-start(bf16[4,64,1280]{2,1,0:T(8,128)(2,1)S(1)} %stack.13.refs_0_), channel_id=1, source_target_pairs={{0,8},{1,3},{2,10},{3,5},{4,12},{5,7},{6,14},{7,1},{8,16},{9,11},{... | collective-permute-start | bytes 1966088 | tf_op jit(solution)/shard_map/ppermute | solution.py:349
  92.3 13.2 %collective-permute-start.15 = (bf16[4,64,1280]{2,1,0:T(8,128)(2,1)S(1)}, bf16[4,64,1280]{2,1,0:T(8,128)(2,1)S(1)}, u32[]{:S(2)}, u32[]{:S(2)}) collective-permute-start(bf16[4,64,1280]{2,1,0:T(8,128)(2,1)S(1)} %stack.13.refs_0_), channel_id=1, source_target_pairs={{0,24},{1,7},{2,26},{3,1},{4,28},{5,3},{6,30},{7,5},{8,0},{9,15},{... | collective-permute-start | bytes 1966088 | tf_op jit(solution)/shard_map/ppermute | solution.py:349
  102.4 10.9 %collective-permute-start.16 = (bf16[4,64,1280]{2,1,0:T(8,128)(2,1)S(1)}, bf16[4,64,1280]{2,1,0:T(8,128)(2,1)S(1)}, u32[]{:S(2)}, u32[]{:S(2)}) collective-permute-start(bf16[4,64,1280]{2,1,0:T(8,128)(2,1)S(1)} %collective-permute-done.14.refs_1_), channel_id=1, source_target_pairs={{0,8},{1,3},{2,10},{3,5},{4,12},{5,7},{6,14},{7,1},{8,16},{9,11},{... | collective-permute-start | bytes 1966088 | tf_op jit(solution)/shard_map/ppermute | solution.py:349
  102.4 14.6 %collective-permute-start.17 = (bf16[4,64,1280]{2,1,0:T(8,128)(2,1)S(1)}, bf16[4,64,1280]{2,1,0:T(8,128)(2,1)S(1)}, u32[]{:S(2)}, u32[]{:S(2)}) collective-permute-start(bf16[4,64,1280]{2,1,0:T(8,128)(2,1)S(1)} %stack.13.refs_0_), channel_id=1, source_target_pairs={{0,1},{1,0},{2,3},{3,2},{4,5},{5,4},{6,7},{7,6},{8,9},{9,8},{10,11... | collective-permute-start | bytes 1966088 | tf_op jit(solution)/shard_map/ppermute | solution.py:333
  105.5 11.6 %collective-permute-start.18 = (bf16[4,64,1280]{2,1,0:T(8,128)(2,1)S(1)}, bf16[4,64,1280]{2,1,0:T(8,128)(2,1)S(1)}, u32[]{:S(2)}, u32[]{:S(2)}) collective-permute-start(bf16[4,64,1280]{2,1,0:T(8,128)(2,1)S(1)} %collective-permute-done.14.refs_1_), channel_id=1, source_target_pairs={{0,1},{1,0},{2,3},{3,2},{4,5},{5,4},{6,7},{7,6},{8,9},{9,8},{10,11... | collective-permute-start | bytes 1966088 | tf_op jit(solution)/shard_map/ppermute | solution.py:333
  105.5 11.5 %collective-permute-start.19 = (bf16[4,64,1280]{2,1,0:T(8,128)(2,1)S(1)}, bf16[4,64,1280]{2,1,0:T(8,128)(2,1)S(1)}, u32[]{:S(2)}, u32[]{:S(2)}) collective-permute-start(bf16[4,64,1280]{2,1,0:T(8,128)(2,1)S(1)} %collective-permute-done.15.refs_2_), channel_id=1, source_target_pairs={{0,1},{1,0},{2,3},{3,2},{4,5},{5,4},{6,7},{7,6},{8,9},{9,8},{10,11... | collective-permute-start | bytes 1966088 | tf_op jit(solution)/shard_map/ppermute | solution.py:333
  113.4 5.4 %collective-permute-start.20 = (bf16[4,64,1280]{2,1,0:T(8,128)(2,1)S(1)}, bf16[4,64,1280]{2,1,0:T(8,128)(2,1)S(1)}, u32[]{:S(2)}, u32[]{:S(2)}) collective-permute-start(bf16[4,64,1280]{2,1,0:T(8,128)(2,1)S(1)} %collective-permute-done.16.refs_3_), channel_id=1, source_target_pairs={{0,1},{1,0},{2,3},{3,2},{4,5},{5,4},{6,7},{7,6},{8,9},{9,8},{10,11... | collective-permute-start | bytes 1966088 | tf_op jit(solution)/shard_map/ppermute | solution.py:333
  (9 other events, 156.2 us)

commit v3 on v2

v3 whole, which is shorter than its diff:
```python
import math

import jax
import jax.numpy as jnp
from jax import lax
from jax.experimental import pallas as pl
from jax.experimental.pallas import tpu as pltpu
from jax.sharding import PartitionSpec as P

BF = jnp.bfloat16
F32 = jnp.float32
TERR, MESO, MIX = 256, 384, 256
JOINT = TERR + MESO
LEV = 128
SLAB = 16
PACK = LEV + SLAB
ROWS, COLS = 8, 128
HALO = 5
OQ, MQ = MIX // 4, MESO // 4
WIDE = 1280
NT = (((1,), (1,)), ((), ()))


def dot(a, b):
    return jnp.dot(a, b, preferred_element_type=F32)


def dot_nt(a, b):
    return lax.dot_general(a, b, NT, preferred_element_type=F32)


def params(mib):
    return pltpu.CompilerParams(vmem_limit_bytes=mib * 1024 * 1024)


def sixteen(v, above):
    rows, width = v.shape
    parts = [v.astype(F32)]
    if above:
        parts.insert(0, jnp.zeros((above, width), F32))
    if above + rows < SLAB:
        parts.append(jnp.zeros((SLAB - above - rows, width), F32))
    return jnp.concatenate(parts, axis=0)


def prep_kernel(mw, lw, tw, pw, gw, dw, wm, wt, gt, dt):
    for tap in range(9):
        wm[:, tap * LEV : (tap + 1) * LEV] = dot(
            mw[:, tap * MESO : (tap + 1) * MESO], lw[...]
        ).astype(BF)
    pw16 = sixteen(pw[...], 0).astype(BF)
    wt[...] = jnp.concatenate(
        [dot_nt(tw[:, tap * TERR : (tap + 1) * TERR], pw16).astype(BF) for tap in range(9)], axis=1
    )
    for tap in range(9):
        gt[:, tap * MIX : (tap + 1) * MIX] = gw[:, tap * JOINT : (tap + 1) * JOINT].T
        dt[:, tap * MIX : (tap + 1) * MIX] = dw[:, tap * MIX : (tap + 1) * MIX].T


def prep(meso_weight, lift_weight, terrain_weight, patch_turned, merging_weight, decoder_weight):
    return pl.pallas_call(
        prep_kernel,
        out_shape=(
            jax.ShapeDtypeStruct((MESO, 9 * LEV), BF),
            jax.ShapeDtypeStruct((TERR, 9 * SLAB), BF),
            jax.ShapeDtypeStruct((JOINT, 9 * MIX), BF),
            jax.ShapeDtypeStruct((MIX, 9 * MIX), BF),
        ),
        compiler_params=params(24),
        cost_estimate=pl.CostEstimate(
            flops=2 * 9 * 384 * 384 * 128, bytes_accessed=17_000_000, transcendentals=0
        ),
        name="prep",
    )(meso_weight, lift_weight, terrain_weight, patch_turned, merging_weight, decoder_weight)


def rows_kernel(place, own, partner, eight, first, last):
    core = place[1] % 2
    for c in range(2):

        @pl.when(core == c)
        def _(c=c):
            halves = (own, partner) if c == 0 else (partner, own)
            for r in range(ROWS):
                v = halves[r // 4][c, r % 4]
                eight[r] = v
                if r < HALO:
                    first[r] = v
                if r >= ROWS - HALO:
                    last[r - (ROWS - HALO)] = v


def chip_rows(place, own, partner):
    smem = pl.BlockSpec(memory_space=pltpu.SMEM)
    vmem = pl.BlockSpec(memory_space=pltpu.VMEM)
    return pl.pallas_call(
        rows_kernel,
        out_shape=tuple(
            jax.ShapeDtypeStruct((n, PACK, COLS), BF) for n in (ROWS, HALO, HALO)
        ),
        in_specs=[smem, vmem, vmem],
        out_specs=(vmem,) * 3,
        compiler_params=params(16),
        name="rows",
    )(place, own, partner)


def neighbours(v):
    width = v.shape[1]
    lane = lax.broadcasted_iota(jnp.int32, (1, width), 1) % COLS
    left, right = [], []
    for r in range(width // COLS):
        piece = v[:, r * COLS : (r + 1) * COLS]
        left.append(pltpu.roll(piece, 1, 1))
        right.append(pltpu.roll(piece, COLS - 1, 1))
    left = jnp.where(lane == 0, 0.0, jnp.concatenate(left, axis=1))
    right = jnp.where(lane == COLS - 1, 0.0, jnp.concatenate(right, axis=1))
    return left, right


def logistic(v):
    return 0.5 * (1.0 + jnp.tanh(0.5 * v))


def main_kernel(place, above, eight, below, hw, *refs):
    n_w = 6
    weights_hbm, keep, send, out = refs[:n_w], *refs[n_w : n_w + 3]
    wm, wt, gw, dw, dt, gt = weights = refs[n_w + 3 : 2 * n_w + 3]
    sems, x3, p9, j3, jslope, jdelta, m3, mslope, dout, d3, e3 = refs[2 * n_w + 3 :]
    copies = [
        pltpu.make_async_copy(u, v, sems.at[i]) for i, (u, v) in enumerate(zip(weights_hbm, weights))
    ]
    for copy in copies:
        copy.start()
    segment, depth = place[0], place[2]
    chip, core = place[1] // 2, place[1] % 2
    first_row = chip * ROWS

    def cut(row, rows):
        return slice(row * COLS, (row + rows) * COLS)

    def inside(row, rows):
        at = lax.broadcasted_iota(jnp.int32, (1, rows * COLS), 1) // COLS + row + first_row
        return jnp.logical_and(at >= 0, at < 4 * ROWS)

    def slab(r):
        for ref, rows in ((above, HALO), (eight, ROWS), (below, HALO)):
            if r < rows:
                return ref[r]
            r -= rows

    n_in, n_join = ROWS + 2 * HALO, ROWS + 8

    for r in range(n_in):
        v = slab(r).astype(F32)
        left, right = neighbours(v)
        for b, u in enumerate((left, v, right)):
            u = u.astype(BF)
            x3[b * LEV : (b + 1) * LEV, cut(r, 1)] = u[:LEV]
            for a in range(3):
                if a <= r < n_join + a:
                    tap = 3 * a + b
                    p9[tap * SLAB : (tap + 1) * SLAB, cut(r - a, 1)] = u[LEV:]

    head_turned = sixteen(hw[...], 8).T.astype(BF)
    copies[0].wait()
    copies[1].wait()

    for row in (0, 4, 8, 12):
        pre_t = dot(wt[...], p9[:, cut(row, 4)])
        pre_m = sum(
            dot(wm[:, a * 3 * LEV : (a + 1) * 3 * LEV], x3[:, cut(row + a, 4)]) for a in range(3)
        )
        for at, pre in ((0, pre_t), (TERR, pre_m)):
            size = pre.shape[0]
            sigma = logistic(pre)
            v = jnp.where(inside(row - 4, 4), pre * sigma, 0.0)
            left, right = neighbours(v)
            for b, u in enumerate((left, v, right)):
                j3[b * JOINT + at : b * JOINT + at + size, cut(row, 4)] = u.astype(BF)
            if row in (4, 8):
                jslope[at : at + size, cut(row - 4, 4)] = sigma * (1.0 + pre * (1.0 - sigma))

    copies[2].wait()
    for row, rows in ((0, 4), (4, 5), (9, 5)):
        pre = sum(
            dot(gw[:, a * 3 * JOINT : (a + 1) * 3 * JOINT], j3[:, cut(row + a, rows)])
            for a in range(3)
        )
        sigma = logistic(pre)
        v = jnp.where(inside(row - 3, rows), pre * sigma, 0.0)
        left, right = neighbours(v)
        for b, u in enumerate((left, v, right)):
            m3[b * MIX : (b + 1) * MIX, cut(row, rows)] = u.astype(BF)
        mslope[:, cut(row, rows)] = sigma * (1.0 + pre * (1.0 - sigma))

    scale = 1.0 / math.sqrt(8 * 32 * 128)

    copies[3].wait()
    for row in (0, 4, 8):
        pre = sum(
            dot(dw[:, a * 3 * MIX : (a + 1) * 3 * MIX], m3[:, cut(row + a, 4)]) for a in range(3)
        )
        sigma = logistic(pre)
        cot = jnp.concatenate([slab(row + 3 + r)[LEV:] for r in range(4)], axis=1)
        back = scale * dot(head_turned, cot)
        v = sigma * (1.0 + pre * (1.0 - sigma)) * back
        left, right = neighbours(v)
        for b, u in enumerate((right, v, left)):
            d3[b * MIX : (b + 1) * MIX, cut(row, 4)] = u.astype(BF)
        lo, hi = max(row, 2), min(row + 4, 10)
        dout[:, cut(lo - 2, hi - lo)] = (pre * sigma)[:, cut(lo - row, hi - lo)].astype(BF)

    copies[4].wait()
    for row in (0, 5):
        back = sum(
            dot(dt[:, a * 3 * MIX : (a + 1) * 3 * MIX], d3[:, cut(row + 2 - a, 5)])
            for a in range(3)
        )
        v = jnp.where(inside(row - 1, 5), mslope[:, cut(row + 2, 5)] * back, 0.0)
        left, right = neighbours(v)
        for b, u in enumerate((right, v, left)):
            e3[b * MIX : (b + 1) * MIX, cut(row, 5)] = u.astype(BF)

    copies[5].wait()
    for row in (0, 4):
        back = sum(
            dot(gt[:, a * 3 * MIX : (a + 1) * 3 * MIX], e3[:, cut(row + 2 - a, 4)])
            for a in range(3)
        )
        jdelta[:, cut(row, 4)] = (jslope[:, cut(row, 4)] * back).astype(BF)

    def put(rows, column, value):
        value = value.astype(BF)
        width = value.shape[1]
        done = 0
        while done < width:
            group, offset = divmod(column + done, WIDE)
            take = min(width - done, WIDE - offset)
            along = chip if group < 4 else depth
            slot = 4 * lax.rem(core + group // 4, 2) + lax.rem(group % 4 + 4 - along, 4)
            out[slot, rows : rows + value.shape[0], offset : offset + take] = value[
                :, done : done + take
            ]
            done += take

    def stacked(delta):
        def zero(rows):
            return jnp.zeros((delta.shape[0], rows * COLS), BF)

        return jnp.concatenate(
            [
                jnp.concatenate([delta, zero(2)], axis=1),
                jnp.concatenate([zero(1), delta, zero(1)], axis=1),
                jnp.concatenate([zero(2), delta], axis=1),
            ],
            axis=0,
        )

    q = pl.ds(pl.multiple_of(segment * OQ, OQ), OQ)
    qd = pl.ds(pl.multiple_of(MIX + segment * OQ, OQ), OQ)
    qm = pl.ds(pl.multiple_of(TERR + segment * MQ, 32), MQ)
    d_own = stacked(d3[qd, cut(2, ROWS)])
    e_own = stacked(e3[qd, cut(1, ROWS)])
    h_own = stacked(jdelta[qm, :])
    for b in range(3):
        part = dot_nt(e_own, j3[b * JOINT : (b + 1) * JOINT, cut(3, ROWS + 2)])
        for a in range(3):
            put(0, (3 * a + b) * JOINT, part[a * OQ : (a + 1) * OQ])
    column = 9 * JOINT
    part = dot_nt(d_own, m3[:, cut(2, ROWS + 2)])
    for a in range(3):
        put(0, column + a * 3 * MIX, part[a * OQ : (a + 1) * OQ])
    column += 9 * MIX
    part = dot_nt(h_own, x3[:, cut(4, ROWS + 2)])
    for a in range(3):
        h = part[a * MQ : (a + 1) * MQ]
        put(0, column + a * 3 * LEV, h[:64])
        spare = column + 9 * LEV
        for c in range(3):
            at = a * 3 * LEV + c * LEV
            piece = h[64:, c * LEV : (c + 1) * LEV]
            if at < 640:
                put(0, spare + at, piece)
            else:
                put(32, spare + at - 640, piece)
    put(32, column + 9 * LEV + 512, jnp.zeros((32, 128), F32))
    column += 9 * LEV + 640
    g = dot_nt(jdelta[q, :], p9[:, cut(4, ROWS)])
    head = scale * dot_nt(
        dout[q, :], jnp.concatenate([eight[r, LEV:] for r in range(ROWS)], axis=1)
    )
    tail = 8 * WIDE - column
    put(0, column, jnp.concatenate([g, head, jnp.zeros((OQ, tail - 10 * SLAB), F32)], axis=1))
    keep[...] = out[:4]
    send[...] = out[4:]


def main(place, above, eight, below, head_weight, *weights):
    smem = pl.BlockSpec(memory_space=pltpu.SMEM)
    vmem = pl.BlockSpec(memory_space=pltpu.VMEM)
    hbm = pl.BlockSpec(memory_space=pl.ANY)
    return pl.pallas_call(
        main_kernel,
        out_shape=(jax.ShapeDtypeStruct((4, OQ, WIDE), BF),) * 2,
        in_specs=[smem] + [vmem] * 4 + [hbm] * len(weights),
        out_specs=(vmem, vmem),
        scratch_shapes=[
            pltpu.VMEM((8, OQ, WIDE), BF),
            *[pltpu.VMEM(w.shape, BF) for w in weights],
            pltpu.SemaphoreType.DMA((len(weights),)),
            pltpu.VMEM((3 * LEV, (ROWS + 2 * HALO) * COLS), BF),
            pltpu.VMEM((9 * SLAB, (ROWS + 8) * COLS), BF),
            pltpu.VMEM((3 * JOINT, (ROWS + 8) * COLS), BF),
            pltpu.VMEM((JOINT, ROWS * COLS), F32),
            pltpu.VMEM((JOINT, ROWS * COLS), BF),
            pltpu.VMEM((3 * MIX, (ROWS + 6) * COLS), BF),
            pltpu.VMEM((MIX, (ROWS + 6) * COLS), F32),
            pltpu.VMEM((MIX, ROWS * COLS), BF),
            pltpu.VMEM((3 * MIX, (ROWS + 4) * COLS), BF),
            pltpu.VMEM((3 * MIX, (ROWS + 2) * COLS), BF),
        ],
        compiler_params=params(46),
        cost_estimate=pl.CostEstimate(
            flops=15_000_000_000, bytes_accessed=12_000_000, transcendentals=3_000_000
        ),
        name="sections",
    )(place, above, eight, below, head_weight, *weights)


def split_kernel(keep, came, own, next1, next2, next3):
    own[...] = keep[0].astype(F32) + came[0].astype(F32)
    for j, to in enumerate((next1, next2, next3), 1):
        to[...] = (keep[j].astype(F32) + came[j].astype(F32)).astype(BF)


def total_kernel(own, one, two, three, out):
    out[...] = (
        (own[...].astype(F32) + two[...].astype(F32))
        + (one[...].astype(F32) + three[...].astype(F32))
    ).astype(BF)


def stack_kernel(own, one, two, three, out):
    for j, v in enumerate((own, one, two, three)):
        out[j] = v[...]


def small(kernel, out_shape, *operands):
    return pl.pallas_call(
        kernel, out_shape=out_shape, compiler_params=params(16), name=kernel.__name__[:-7]
    )(*operands)


def moved(v, where):
    pairs = []
    for source in range(128):
        at = (source // 32, source // 8 % 4, source // 2 % 4, source % 2)
        to = where(*at)
        if to is not None:
            pairs.append((source, to[0] * 32 + to[1] * 8 + to[2] * 2 + to[3]))
    return lax.ppermute(v, ("dp", "segment", "space"), pairs)


DP, SEGMENT, CHIP = 0, 1, 2


def along(v, axes, by):
    def where(*at):
        to = list(at)
        to[axes[at[3]]] = (to[axes[at[3]]] + by) % 4
        return to

    return moved(v, where)


def to_partner(v):
    return moved(v, lambda z, x, y, c: (z, x, y, 1 - c))


STEPS = (0, -1, 1, -2)


def summed_everywhere(keep, send):
    piece = jax.ShapeDtypeStruct((OQ, WIDE), BF)
    wide = jax.ShapeDtypeStruct((OQ, WIDE), F32)
    turns = (1, 2, 3)
    own, *parts = small(split_kernel, (wide, piece, piece, piece), keep, to_partner(send))
    own = small(total_kernel, piece, own, *[along(p, (CHIP, DP), j) for p, j in zip(parts, turns)])
    own = small(total_kernel, piece, own, *[along(own, (DP, CHIP), j) for j in turns])
    four = jax.ShapeDtypeStruct((4, OQ, WIDE), BF)
    block = small(stack_kernel, four, own, *[along(own, (CHIP, SEGMENT), j) for j in turns])
    mine = (block,) + tuple(along(block, (SEGMENT, DP), -step) for step in STEPS[1:])
    return mine + tuple(to_partner(v) for v in mine)


def finish_kernel(place, *refs):
    blocks, (lw, pw, mw_hbm, tw_hbm) = refs[:8], refs[8:12]
    patch, lift, head, terrain, meso, merging, decoder = refs[12:19]
    mw, tw, stage, wide_m, wide_t, ht, gt, sems = refs[19:]
    reads = [
        pltpu.make_async_copy(mw_hbm, mw, sems.at[0]),
        pltpu.make_async_copy(tw_hbm, tw, sems.at[1]),
    ]
    for copy in reads:
        copy.start()
    segment, chip, core, depth = place[0], place[1] // 2, place[1] % 2, place[2]
    for i, block in enumerate(blocks):
        kind = core if i < 4 else 1 - core
        for j in range(4):
            along_segment = jnp.where(kind == 0, STEPS[i % 4], -j)
            group = jnp.where(
                kind == 0, lax.rem(chip - j + 4, 4), 4 + lax.rem(depth + STEPS[i % 4] + 4, 4)
            )
            row = lax.rem(segment + along_segment + 4, 4) * OQ
            stage[
                pl.ds(pl.multiple_of(row, OQ), OQ), pl.ds(pl.multiple_of(group * WIDE, WIDE), WIDE)
            ] = block[j].astype(F32)
    column = 9 * JOINT + 9 * MIX
    writes = [
        pltpu.make_async_copy(stage.at[:, : 9 * JOINT], merging, sems.at[2]),
        pltpu.make_async_copy(stage.at[:, 9 * JOINT : column], decoder, sems.at[3]),
    ]
    for copy in writes:
        copy.start()
    for seg in range(4):
        lo = seg * OQ
        at = seg * MQ
        ht[at : at + 64, :] = stage[lo : lo + OQ, column : column + 9 * LEV].astype(BF)
        spare = column + 9 * LEV
        ht[at + 64 : at + MQ, :640] = stage[lo : lo + 32, spare : spare + 640].astype(BF)
        ht[at + 64 : at + MQ, 640:] = stage[lo + 32 : lo + OQ, spare : spare + 512].astype(BF)
        gt[lo : lo + OQ, :] = stage[lo : lo + OQ, spare + 640 : spare + 896]
    for a in range(3):
        for tap in range(3 * a, 3 * a + 3):
            wide_m[:, tap * MESO : (tap + 1) * MESO] = dot_nt(
                ht[:, tap * LEV : (tap + 1) * LEV], lw[...]
            )
        part = slice(3 * a * MESO, 3 * (a + 1) * MESO)
        writes.append(pltpu.make_async_copy(wide_m.at[:, part], meso.at[:, part], sems.at[4 + a]))
        writes[-1].start()
    pw16 = sixteen(pw[...], 0).astype(BF)
    g = gt[...]
    for tap in range(9):
        wide_t[:, tap * TERR : (tap + 1) * TERR] = dot(
            g[:, tap * SLAB : (tap + 1) * SLAB].astype(BF), pw16
        )
    writes.append(pltpu.make_async_copy(wide_t, terrain, sems.at[7]))
    writes[-1].start()
    turned = g.T
    head[...] = turned[9 * SLAB + 8 : 9 * SLAB + 11, :]
    reads[1].wait()
    patch[...] = sum(
        dot(
            turned[tap * SLAB : (tap + 1) * SLAB, :].astype(BF),
            tw[:, tap * TERR : (tap + 1) * TERR],
        )
        for tap in range(9)
    )[:8]
    turned = ht[...].astype(F32).T.astype(BF)
    reads[0].wait()
    lift[...] = sum(
        dot(turned[tap * LEV : (tap + 1) * LEV, :], mw[:, tap * MESO : (tap + 1) * MESO])
        for tap in range(9)
    ).T
    for copy in writes:
        copy.wait()


def finish(place, blocks, lift_weight, patch_turned, meso_weight, terrain_weight):
    smem = pl.BlockSpec(memory_space=pltpu.SMEM)
    vmem = pl.BlockSpec(memory_space=pltpu.VMEM)
    hbm = pl.BlockSpec(memory_space=pl.ANY)
    patch, lift, head, terrain, meso, merging, decoder = pl.pallas_call(
        finish_kernel,
        out_shape=(
            jax.ShapeDtypeStruct((8, TERR), F32),
            jax.ShapeDtypeStruct((MESO, LEV), F32),
            jax.ShapeDtypeStruct((3, MIX), F32),
            jax.ShapeDtypeStruct((TERR, 9 * TERR), F32),
            jax.ShapeDtypeStruct((MESO, 9 * MESO), F32),
            jax.ShapeDtypeStruct((MIX, 9 * JOINT), F32),
            jax.ShapeDtypeStruct((MIX, 9 * MIX), F32),
        ),
        in_specs=[smem] + [vmem] * 10 + [hbm] * 2,
        out_specs=(vmem,) * 3 + (hbm,) * 4,
        scratch_shapes=[
            pltpu.VMEM((MESO, 9 * MESO), BF),
            pltpu.VMEM((TERR, 9 * TERR), BF),
            pltpu.VMEM((MIX, 8 * WIDE), F32),
            pltpu.VMEM((MESO, 9 * MESO), F32),
            pltpu.VMEM((TERR, 9 * TERR), F32),
            pltpu.VMEM((MESO, 9 * LEV), BF),
            pltpu.VMEM((MIX, 256), F32),
            pltpu.SemaphoreType.DMA((8,)),
        ],
        compiler_params=params(40),
        name="finish",
    )(place, *blocks, lift_weight, patch_turned, meso_weight, terrain_weight)
    return patch.T, terrain, lift, meso, merging, decoder, head


def packed(terrain_in, meso_in, wind_cot):
    samples, rows = meso_in.shape[0], meso_in.shape[3]
    source = lax.broadcasted_iota(jnp.int32, (2 * COLS, 2 * COLS), 0)
    target = lax.broadcasted_iota(jnp.int32, (2 * COLS, 2 * COLS), 1)
    pick = (source == 2 * (target % COLS) + target // COLS).astype(BF)
    split = dot(terrain_in.reshape(samples * 4 * rows, 2 * COLS), pick).astype(BF)
    patches = (
        split.reshape(samples, 2, rows, 2, 2, COLS)
        .transpose(0, 2, 1, 3, 4, 5)
        .reshape(samples, rows, 8, COLS)
    )
    levels = meso_in.reshape(samples, LEV, rows, COLS).transpose(0, 2, 1, 3)
    cot = wind_cot.transpose(0, 2, 1, 3)
    rest = jnp.zeros((samples, rows, PACK - LEV - 11, COLS), BF)
    return jnp.concatenate([levels, patches, cot, rest], axis=2)


def to_chip(v, by):
    return moved(v, lambda z, x, y, c: (z, x, y + by, c) if 0 <= y + by < 4 else None)


def local(
    terrain_in,
    meso_in,
    wind_cot,
    patch_weight,
    terrain_weight,
    lift_weight,
    meso_weight,
    merging_weight,
    decoder_weight,
    head_weight,
):
    own = packed(terrain_in, meso_in, wind_cot)
    place = jnp.stack([lax.axis_index(a) for a in ("segment", "space", "dp")]).astype(jnp.int32)
    eight, first, last = chip_rows(place, own, to_partner(own))
    above, below = to_chip(last, 1), to_chip(first, -1)
    patch_turned = patch_weight.T
    wm, wt, gt, dt = prep(
        meso_weight, lift_weight, terrain_weight, patch_turned, merging_weight, decoder_weight
    )
    keep, send = main(
        place, above, eight, below, head_weight, wm, wt, merging_weight, decoder_weight, dt, gt
    )
    blocks = summed_everywhere(keep, send)
    return finish(place, blocks, lift_weight, patch_turned, meso_weight, terrain_weight)


def solution(mesh):
    placed = (
        P("dp", None, "space", None),
        P("dp", None, None, "space", None),
        P("dp", None, "space", None),
        P(),
        P(),
        P(),
        P(),
        P(),
        P(),
        P(),
    )
    return jax.shard_map(
        local,
        mesh=mesh,
        in_specs=placed,
        out_specs=(P(), P(), P(), P(), P(), P(), P()),
        check_vma=False,
    )
```

time: 127 us -> 113 us (0.89)
  waiting for transfers between devices: 43.6 us -> 27.6 us
  Pallas kernels: 41.3 us -> 34.8 us
  local copies, waits for them, and re-layouts: 3.74 us -> 9.95 us
  starting transfers between devices: 36.5 us -> 39 us
    ppermute x21 -> x20, waiting for transfers between devices: 43.6 us -> 27.6 us  [moved(): return lax.ppermute(v, ('dp', 'segment', 'space'), pairs)]
    pallas_call x1, Pallas kernels: 32.8 us -> 24.1 us  [main(): pl.pallas_call(main_kernel, out_shape=(jax.ShapeDtypeStruct((4, OQ, WIDE)...]
    unnamed x26 -> x30, local copies, waits for them, and re-layouts: 3.61 us -> 9.84 us
    ppermute x21 -> x20, starting transfers between devices: 36.5 us -> 39 us  [moved(): return lax.ppermute(v, ('dp', 'segment', 'space'), pairs)]
    pallas_call x0 -> x2, Pallas kernels: none -> 1.98 us  [the longest x1 1.35 us: prep(): pl.pallas_call(prep_kernel, out_shape=(jax.ShapeDtypeStruct((MESO, 9 * LE...]
  transfers between devices with their start and end apart: 21 -> 20, of which waited for: 12 -> 14; matrix products, arithmetic and copies ran while one was open for 1% -> 0% of each run, Pallas kernels for 0% -> 1%
where the time goes in v3:
time: 113 us
  starting transfers between devices  39 us (35%)
  Pallas kernels  34.8 us (31%)
  waiting for transfers between devices  27.6 us (24%)
  local copies, waits for them, and re-layouts  9.95 us (9%)
    ppermute x20, starting transfers between devices, moved(): return lax.ppermute(v, ('dp', 'segment', 'space'), pairs)  39 us
    ppermute x20, waiting for transfers between devices, moved(): return lax.ppermute(v, ('dp', 'segment', 'space'), pairs)  27.6 us
    pallas_call x1, Pallas kernels, main(): pl.pallas_call(main_kernel, out_shape=(jax.ShapeDtypeStruct((4, OQ, WIDE)...  24.1 us
    unnamed x30, local copies, waits for them, and re-layouts  9.84 us
    pallas_call x1, Pallas kernels, finish(): pl.pallas_call(finish_kernel, out_shape=(jax.ShapeDtypeStruct((8, TERR),...  8.39 us
  transfers between devices with their start and end apart: 20, of which 14 were waited for; matrix products, arithmetic and copies ran while one was open for 0% of the time, Pallas kernels for 1%

profile of v3, /device:TPU:1, one launch (start us, length us, event | category | flops | bytes accessed | tf_op | source)
XLA Modules:
  0.0 112.7 jit_solution(11143988823541597313)
XLA Ops:
  6.3 3.3 %collective-permute-start.1 = (bf16[5,144,128]{2,1,0:T(8,128)(2,1)S(1)}, bf16[5,144,128]{2,1,0:T(8,128)(2,1)S(1)}, u32[]{:S(2)}, u32[]{:S(2)}) collective-permute-start(bf16[5,144,128]{2,1,0:T(8,128)(2,1)S(1)} %get-tuple-element.27), channel_id=1, source_target_pairs={{0,2},{1,3},{2,4},{3,5},{4,6},{5,7},{8,10},{9,11},{10,12},{11,13},... | collective-permute-start | bytes 552968 | tf_op jit(solution)/shard_map/ppermute | solution.py:362
  10.9 1.7 %copy-done.1 = bf16[384,3456]{1,0:T(8,128)(2,1)S(1)} copy-done((bf16[384,3456]{1,0:T(8,128)(2,1)S(1)}, bf16[384,3456]{1,0:T(8,128)(2,1)}, u32[]{:S(2)}) %copy-start.1) | copy-done | bytes 2654232
  12.6 1.8 %copy-done.4 = bf16[256,5760]{1,0:T(8,128)(2,1)S(1)} copy-done((bf16[256,5760]{1,0:T(8,128)(2,1)S(1)}, bf16[256,5760]{1,0:T(8,128)(2,1)}, u32[]{:S(2)}) %copy-start.4) | copy-done | bytes 2949144
  20.3 24.1 %sections.1 = (bf16[4,64,1280]{2,1,0:T(8,128)(2,1)S(1)}, bf16[4,64,1280]{2,1,0:T(8,128)(2,1)S(1)}) custom-call(s32[3]{0:T(128)S(1)} %pad_add_fusion.place, bf16[5,144,128]{2,1,0:T(8,128)(2,1)S(1)} %collective-permute-done.1.above, bf16[8,144,128]{2,1,0:T(8,128)(2,1)S(1)} %get-tuple-element.28.eight, bf16[5,144,128]{2,1,0:T(8,128)(2,1)S(1)} %collective-permute-done.2.below, ...), custom_call_target="tpu_custom_call" | custom-call | flops 15000000512 | bytes 12000000 | tf_op jit(solution)/shard_map/sections/pallas_call | solution.py:303
  45.2 1.7 %collective-permute-done.3.came = bf16[4,64,1280]{2,1,0:T(8,128)(2,1)S(1)} collective-permute-done((bf16[4,64,1280]{2,1,0:T(8,128)(2,1)S(1)}, bf16[4,64,1280]{2,1,0:T(8,128)(2,1)S(1)}, u32[]{:S(2)}, u32[]{:S(2)}) %collective-permute-start.3) | collective-permute-done | bytes 655392 | tf_op jit(solution)/shard_map/ppermute | solution.py:362
  47.0 1.7 %collective-permute-start.4 = (bf16[64,1280]{1,0:T(8,128)(2,1)S(1)}, bf16[64,1280]{1,0:T(8,128)(2,1)S(1)}, u32[]{:S(2)}, u32[]{:S(2)}) collective-permute-start(bf16[64,1280]{1,0:T(8,128)(2,1)S(1)} %get-tuple-element.37), channel_id=1, source_target_pairs={{0,2},{1,33},{2,4},{3,35},{4,6},{5,37},{6,0},{7,39},{8,10},{9,41},... | collective-permute-start | bytes 491528 | tf_op jit(solution)/shard_map/ppermute | solution.py:362
  48.7 3.3 %collective-permute-start.5 = (bf16[64,1280]{1,0:T(8,128)(2,1)S(1)}, bf16[64,1280]{1,0:T(8,128)(2,1)S(1)}, u32[]{:S(2)}, u32[]{:S(2)}) collective-permute-start(bf16[64,1280]{1,0:T(8,128)(2,1)S(1)} %get-tuple-element.38), channel_id=1, source_target_pairs={{0,4},{1,65},{2,6},{3,67},{4,0},{5,69},{6,2},{7,71},{8,12},{9,73},... | collective-permute-start | bytes 491528 | tf_op jit(solution)/shard_map/ppermute | solution.py:362
  53.9 2.9 %collective-permute-done.5.two = bf16[64,1280]{1,0:T(8,128)(2,1)S(1)} collective-permute-done((bf16[64,1280]{1,0:T(8,128)(2,1)S(1)}, bf16[64,1280]{1,0:T(8,128)(2,1)S(1)}, u32[]{:S(2)}, u32[]{:S(2)}) %collective-permute-start.5) | collective-permute-done | bytes 163872 | tf_op jit(solution)/shard_map/ppermute | solution.py:362
  56.9 3.6 %collective-permute-start.9 = (bf16[64,1280]{1,0:T(8,128)(2,1)S(1)}, bf16[64,1280]{1,0:T(8,128)(2,1)S(1)}, u32[]{:S(2)}, u32[]{:S(2)}) collective-permute-start(bf16[64,1280]{1,0:T(8,128)(2,1)S(1)} %total.2.own), channel_id=1, source_target_pairs={{0,96},{1,7},{2,98},{3,1},{4,100},{5,3},{6,102},{7,5},{8,104},{9,1... | collective-permute-start | bytes 491528 | tf_op jit(solution)/shard_map/ppermute | solution.py:362
  61.5 3.0 %collective-permute-done.9.three = bf16[64,1280]{1,0:T(8,128)(2,1)S(1)} collective-permute-done((bf16[64,1280]{1,0:T(8,128)(2,1)S(1)}, bf16[64,1280]{1,0:T(8,128)(2,1)S(1)}, u32[]{:S(2)}, u32[]{:S(2)}) %collective-permute-start.9) | collective-permute-done | bytes 163872 | tf_op jit(solution)/shard_map/ppermute | solution.py:362
  64.5 1.8 %collective-permute-done.8.two = bf16[64,1280]{1,0:T(8,128)(2,1)S(1)} collective-permute-done((bf16[64,1280]{1,0:T(8,128)(2,1)S(1)}, bf16[64,1280]{1,0:T(8,128)(2,1)S(1)}, u32[]{:S(2)}, u32[]{:S(2)}) %collective-permute-start.8) | collective-permute-done | bytes 163872 | tf_op jit(solution)/shard_map/ppermute | solution.py:362
  66.2 1.9 %collective-permute-done.7.one = bf16[64,1280]{1,0:T(8,128)(2,1)S(1)} collective-permute-done((bf16[64,1280]{1,0:T(8,128)(2,1)S(1)}, bf16[64,1280]{1,0:T(8,128)(2,1)S(1)}, u32[]{:S(2)}, u32[]{:S(2)}) %collective-permute-start.7) | collective-permute-done | bytes 163872 | tf_op jit(solution)/shard_map/ppermute | solution.py:362
  68.3 2.6 %collective-permute-start.12 = (bf16[64,1280]{1,0:T(8,128)(2,1)S(1)}, bf16[64,1280]{1,0:T(8,128)(2,1)S(1)}, u32[]{:S(2)}, u32[]{:S(2)}) collective-permute-start(bf16[64,1280]{1,0:T(8,128)(2,1)S(1)} %total.3.own), channel_id=1, source_target_pairs={{0,6},{1,25},{2,0},{3,27},{4,2},{5,29},{6,4},{7,31},{8,14},{9,1},{... | collective-permute-start | bytes 491528 | tf_op jit(solution)/shard_map/ppermute | solution.py:362
  71.9 2.9 %collective-permute-done.12.three = bf16[64,1280]{1,0:T(8,128)(2,1)S(1)} collective-permute-done((bf16[64,1280]{1,0:T(8,128)(2,1)S(1)}, bf16[64,1280]{1,0:T(8,128)(2,1)S(1)}, u32[]{:S(2)}, u32[]{:S(2)}) %collective-permute-start.12) | collective-permute-done | bytes 163872 | tf_op jit(solution)/shard_map/ppermute | solution.py:362
  74.8 1.8 %collective-permute-done.11.two = bf16[64,1280]{1,0:T(8,128)(2,1)S(1)} collective-permute-done((bf16[64,1280]{1,0:T(8,128)(2,1)S(1)}, bf16[64,1280]{1,0:T(8,128)(2,1)S(1)}, u32[]{:S(2)}, u32[]{:S(2)}) %collective-permute-start.11) | collective-permute-done | bytes 163872 | tf_op jit(solution)/shard_map/ppermute | solution.py:362
  76.6 1.9 %collective-permute-done.10.one = bf16[64,1280]{1,0:T(8,128)(2,1)S(1)} collective-permute-done((bf16[64,1280]{1,0:T(8,128)(2,1)S(1)}, bf16[64,1280]{1,0:T(8,128)(2,1)S(1)}, u32[]{:S(2)}, u32[]{:S(2)}) %collective-permute-start.10) | collective-permute-done | bytes 163872 | tf_op jit(solution)/shard_map/ppermute | solution.py:362
  78.6 2.0 %collective-permute-start.15 = (bf16[4,64,1280]{2,1,0:T(8,128)(2,1)S(1)}, bf16[4,64,1280]{2,1,0:T(8,128)(2,1)S(1)}, u32[]{:S(2)}, u32[]{:S(2)}) collective-permute-start(bf16[4,64,1280]{2,1,0:T(8,128)(2,1)S(1)} %stack.17.refs_0_), channel_id=1, source_target_pairs={{0,16},{1,65},{2,18},{3,67},{4,20},{5,69},{6,22},{7,71},{8,24},{9,... | collective-permute-start | bytes 1966088 | tf_op jit(solution)/shard_map/ppermute | solution.py:362
  82.1 5.2 %collective-permute-start.16 = (bf16[4,64,1280]{2,1,0:T(8,128)(2,1)S(1)}, bf16[4,64,1280]{2,1,0:T(8,128)(2,1)S(1)}, u32[]{:S(2)}, u32[]{:S(2)}) collective-permute-start(bf16[4,64,1280]{2,1,0:T(8,128)(2,1)S(1)} %stack.17.refs_0_), channel_id=1, source_target_pairs={{0,1},{1,0},{2,3},{3,2},{4,5},{5,4},{6,7},{7,6},{8,9},{9,8},{10,11... | collective-permute-start | bytes 1966088 | tf_op jit(solution)/shard_map/ppermute | solution.py:362
  87.3 2.7 %collective-permute-done.15.refs_3_ = bf16[4,64,1280]{2,1,0:T(8,128)(2,1)S(1)} collective-permute-done((bf16[4,64,1280]{2,1,0:T(8,128)(2,1)S(1)}, bf16[4,64,1280]{2,1,0:T(8,128)(2,1)S(1)}, u32[]{:S(2)}, u32[]{:S(2)}) %collective-permute-start.15) | collective-permute-done | bytes 655392 | tf_op jit(solution)/shard_map/ppermute | solution.py:362
  90.0 4.5 %collective-permute-start.19 = (bf16[4,64,1280]{2,1,0:T(8,128)(2,1)S(1)}, bf16[4,64,1280]{2,1,0:T(8,128)(2,1)S(1)}, u32[]{:S(2)}, u32[]{:S(2)}) collective-permute-start(bf16[4,64,1280]{2,1,0:T(8,128)(2,1)S(1)} %collective-permute-done.15.refs_3_), channel_id=1, source_target_pairs={{0,1},{1,0},{2,3},{3,2},{4,5},{5,4},{6,7},{7,6},{8,9},{9,8},{10,11... | collective-permute-start | bytes 1966088 | tf_op jit(solution)/shard_map/ppermute | solution.py:362
  94.4 2.1 %collective-permute-done.14.refs_2_ = bf16[4,64,1280]{2,1,0:T(8,128)(2,1)S(1)} collective-permute-done((bf16[4,64,1280]{2,1,0:T(8,128)(2,1)S(1)}, bf16[4,64,1280]{2,1,0:T(8,128)(2,1)S(1)}, u32[]{:S(2)}, u32[]{:S(2)}) %collective-permute-start.14) | collective-permute-done | bytes 655392 | tf_op jit(solution)/shard_map/ppermute | solution.py:362
  96.5 4.9 %collective-permute-start.18 = (bf16[4,64,1280]{2,1,0:T(8,128)(2,1)S(1)}, bf16[4,64,1280]{2,1,0:T(8,128)(2,1)S(1)}, u32[]{:S(2)}, u32[]{:S(2)}) collective-permute-start(bf16[4,64,1280]{2,1,0:T(8,128)(2,1)S(1)} %collective-permute-done.14.refs_2_), channel_id=1, source_target_pairs={{0,1},{1,0},{2,3},{3,2},{4,5},{5,4},{6,7},{7,6},{8,9},{9,8},{10,11... | collective-permute-start | bytes 1966088 | tf_op jit(solution)/shard_map/ppermute | solution.py:362
  101.5 1.7 %collective-permute-done.18.refs_6_ = bf16[4,64,1280]{2,1,0:T(8,128)(2,1)S(1)} collective-permute-done((bf16[4,64,1280]{2,1,0:T(8,128)(2,1)S(1)}, bf16[4,64,1280]{2,1,0:T(8,128)(2,1)S(1)}, u32[]{:S(2)}, u32[]{:S(2)}) %collective-permute-start.18) | collective-permute-done | bytes 655392 | tf_op jit(solution)/shard_map/ppermute | solution.py:362
  104.2 8.4 %finish.1 = (f32[8,256]{1,0:T(8,128)}, f32[384,128]{1,0:T(8,128)}, f32[3,256]{1,0:T(4,128)}, f32[256,2304]{1,0:T(8,128)}, f32[384,3456]{1,0:T(8,128)}, /*index=5*/f32[256,5760]{1,0:T(8,128)}, f32[256,2304]{1,0:T(8,128)}) custom-call(s32[3]{0:T(128)S(1)} %pad_add_fusion.place, bf16[4,64,1280]{2,1,0:T(8,128)(2,1)S(1)} %stack.17.refs_0_, ...), custom_call_target="tpu_custom_call" | custom-call | tf_op jit(solution)/shard_map/finish/pallas_call | solution.py:474
  (64 shorter events, 20.2 us)
Async XLA Ops:
  0.6 10.2 %copy-start.3 = (bf16[256,2304]{1,0:T(8,128)(2,1)S(1)}, bf16[256,2304]{1,0:T(8,128)(2,1)}, u32[]{:S(2)}) copy-start(bf16[256,2304]{1,0:T(8,128)(2,1)} %refs_11_.1) | copy-start | bytes 3538948
  2.9 2.7 %collective-permute-start = (bf16[2,4,144,128]{3,2,1,0:T(8,128)(2,1)S(1)}, bf16[2,4,144,128]{3,2,1,0:T(8,128)(2,1)S(1)}, u32[]{:S(2)}, u32[]{:S(2)}) collective-permute-start(bf16[2,4,144,128]{3,2,1,0:T(8,128)(2,1)S(1)} %maximum_maximum_fusion.own), channel_id=1, source_target_pairs={{0,1},{1,0},{2,3},{3,2},{4,5},{5,4},{6,7},{7,6},{8,9},{9,8},{10,11... | collective-permute-start | bytes 884744 | tf_op jit(solution)/shard_map/ppermute | solution.py:362
  6.3 14.0 %collective-permute-start.1 = (bf16[5,144,128]{2,1,0:T(8,128)(2,1)S(1)}, bf16[5,144,128]{2,1,0:T(8,128)(2,1)S(1)}, u32[]{:S(2)}, u32[]{:S(2)}) collective-permute-start(bf16[5,144,128]{2,1,0:T(8,128)(2,1)S(1)} %get-tuple-element.27), channel_id=1, source_target_pairs={{0,2},{1,3},{2,4},{3,5},{4,6},{5,7},{8,10},{9,11},{10,12},{11,13},... | collective-permute-start | bytes 552968 | tf_op jit(solution)/shard_map/ppermute | solution.py:362
  9.6 10.7 %collective-permute-start.2 = (bf16[5,144,128]{2,1,0:T(8,128)(2,1)S(1)}, bf16[5,144,128]{2,1,0:T(8,128)(2,1)S(1)}, u32[]{:S(2)}, u32[]{:S(2)}) collective-permute-start(bf16[5,144,128]{2,1,0:T(8,128)(2,1)S(1)} %get-tuple-element.29), channel_id=1, source_target_pairs={{2,0},{3,1},{4,2},{5,3},{6,4},{7,5},{10,8},{11,9},{12,10},{13,11},... | collective-permute-start | bytes 552968 | tf_op jit(solution)/shard_map/ppermute | solution.py:362
  44.4 59.8 %copy-start.2 = (bf16[384,3456]{1,0:T(8,128)(2,1)S(1)}, bf16[384,3456]{1,0:T(8,128)(2,1)}, u32[]{:S(2)}) copy-start(bf16[384,3456]{1,0:T(8,128)(2,1)} %refs_10_.1) | copy-start | bytes 7962628
  44.4 59.7 %copy-start.9 = (bf16[384,128]{1,0:T(8,128)(2,1)S(1)}, bf16[384,128]{1,0:T(8,128)(2,1)}, u32[]{:S(2)}) copy-start(bf16[384,128]{1,0:T(8,128)(2,1)} %refs_8_.1) | copy-start | bytes 294916
  44.4 59.7 %copy-start.11 = (bf16[256,8]{0,1:T(8,128)(2,1)S(1)}, bf16[256,8]{0,1:T(8,128)(2,1)}, u32[]{:S(2)}) copy-start(bf16[256,8]{0,1:T(8,128)(2,1)} %param.13) | copy-start | bytes 12292
  44.4 2.5 %collective-permute-start.3 = (bf16[4,64,1280]{2,1,0:T(8,128)(2,1)S(1)}, bf16[4,64,1280]{2,1,0:T(8,128)(2,1)S(1)}, u32[]{:S(2)}, u32[]{:S(2)}) collective-permute-start(bf16[4,64,1280]{2,1,0:T(8,128)(2,1)S(1)} %get-tuple-element.35), channel_id=1, source_target_pairs={{0,1},{1,0},{2,3},{3,2},{4,5},{5,4},{6,7},{7,6},{8,9},{9,8},{10,11... | collective-permute-start | bytes 1966088 | tf_op jit(solution)/shard_map/ppermute | solution.py:362
  47.0 6.8 %collective-permute-start.4 = (bf16[64,1280]{1,0:T(8,128)(2,1)S(1)}, bf16[64,1280]{1,0:T(8,128)(2,1)S(1)}, u32[]{:S(2)}, u32[]{:S(2)}) collective-permute-start(bf16[64,1280]{1,0:T(8,128)(2,1)S(1)} %get-tuple-element.37), channel_id=1, source_target_pairs={{0,2},{1,33},{2,4},{3,35},{4,6},{5,37},{6,0},{7,39},{8,10},{9,41},... | collective-permute-start | bytes 491528 | tf_op jit(solution)/shard_map/ppermute | solution.py:362
  48.7 8.0 %collective-permute-start.5 = (bf16[64,1280]{1,0:T(8,128)(2,1)S(1)}, bf16[64,1280]{1,0:T(8,128)(2,1)S(1)}, u32[]{:S(2)}, u32[]{:S(2)}) collective-permute-start(bf16[64,1280]{1,0:T(8,128)(2,1)S(1)} %get-tuple-element.38), channel_id=1, source_target_pairs={{0,4},{1,65},{2,6},{3,67},{4,0},{5,69},{6,2},{7,71},{8,12},{9,73},... | collective-permute-start | bytes 491528 | tf_op jit(solution)/shard_map/ppermute | solution.py:362
  52.0 4.8 %collective-permute-start.6 = (bf16[64,1280]{1,0:T(8,128)(2,1)S(1)}, bf16[64,1280]{1,0:T(8,128)(2,1)S(1)}, u32[]{:S(2)}, u32[]{:S(2)}) collective-permute-start(bf16[64,1280]{1,0:T(8,128)(2,1)S(1)} %get-tuple-element.39), channel_id=1, source_target_pairs={{0,6},{1,97},{2,0},{3,99},{4,2},{5,101},{6,4},{7,103},{8,14},{9,10... | collective-permute-start | bytes 491528 | tf_op jit(solution)/shard_map/ppermute | solution.py:362
  56.9 7.6 %collective-permute-start.9 = (bf16[64,1280]{1,0:T(8,128)(2,1)S(1)}, bf16[64,1280]{1,0:T(8,128)(2,1)S(1)}, u32[]{:S(2)}, u32[]{:S(2)}) collective-permute-start(bf16[64,1280]{1,0:T(8,128)(2,1)S(1)} %total.2.own), channel_id=1, source_target_pairs={{0,96},{1,7},{2,98},{3,1},{4,100},{5,3},{6,102},{7,5},{8,104},{9,1... | collective-permute-start | bytes 491528 | tf_op jit(solution)/shard_map/ppermute | solution.py:362
  60.5 5.8 %collective-permute-start.8 = (bf16[64,1280]{1,0:T(8,128)(2,1)S(1)}, bf16[64,1280]{1,0:T(8,128)(2,1)S(1)}, u32[]{:S(2)}, u32[]{:S(2)}) collective-permute-start(bf16[64,1280]{1,0:T(8,128)(2,1)S(1)} %total.2.own), channel_id=1, source_target_pairs={{0,64},{1,5},{2,66},{3,7},{4,68},{5,1},{6,70},{7,3},{8,72},{9,13},... | collective-permute-start | bytes 491528 | tf_op jit(solution)/shard_map/ppermute | solution.py:362
  60.8 7.4 %collective-permute-start.7 = (bf16[64,1280]{1,0:T(8,128)(2,1)S(1)}, bf16[64,1280]{1,0:T(8,128)(2,1)S(1)}, u32[]{:S(2)}, u32[]{:S(2)}) collective-permute-start(bf16[64,1280]{1,0:T(8,128)(2,1)S(1)} %total.2.own), channel_id=1, source_target_pairs={{0,32},{1,3},{2,34},{3,5},{4,36},{5,7},{6,38},{7,1},{8,40},{9,11},... | collective-permute-start | bytes 491528 | tf_op jit(solution)/shard_map/ppermute | solution.py:362
  68.3 6.6 %collective-permute-start.12 = (bf16[64,1280]{1,0:T(8,128)(2,1)S(1)}, bf16[64,1280]{1,0:T(8,128)(2,1)S(1)}, u32[]{:S(2)}, u32[]{:S(2)}) collective-permute-start(bf16[64,1280]{1,0:T(8,128)(2,1)S(1)} %total.3.own), channel_id=1, source_target_pairs={{0,6},{1,25},{2,0},{3,27},{4,2},{5,29},{6,4},{7,31},{8,14},{9,1},{... | collective-permute-start | bytes 491528 | tf_op jit(solution)/shard_map/ppermute | solution.py:362
  70.8 5.8 %collective-permute-start.11 = (bf16[64,1280]{1,0:T(8,128)(2,1)S(1)}, bf16[64,1280]{1,0:T(8,128)(2,1)S(1)}, u32[]{:S(2)}, u32[]{:S(2)}) collective-permute-start(bf16[64,1280]{1,0:T(8,128)(2,1)S(1)} %total.3.own), channel_id=1, source_target_pairs={{0,4},{1,17},{2,6},{3,19},{4,0},{5,21},{6,2},{7,23},{8,12},{9,25},... | collective-permute-start | bytes 491528 | tf_op jit(solution)/shard_map/ppermute | solution.py:362
  71.4 7.2 %collective-permute-start.10 = (bf16[64,1280]{1,0:T(8,128)(2,1)S(1)}, bf16[64,1280]{1,0:T(8,128)(2,1)S(1)}, u32[]{:S(2)}, u32[]{:S(2)}) collective-permute-start(bf16[64,1280]{1,0:T(8,128)(2,1)S(1)} %total.3.own), channel_id=1, source_target_pairs={{0,2},{1,9},{2,4},{3,11},{4,6},{5,13},{6,0},{7,15},{8,10},{9,17},{... | collective-permute-start | bytes 491528 | tf_op jit(solution)/shard_map/ppermute | solution.py:362
  78.6 11.4 %collective-permute-start.15 = (bf16[4,64,1280]{2,1,0:T(8,128)(2,1)S(1)}, bf16[4,64,1280]{2,1,0:T(8,128)(2,1)S(1)}, u32[]{:S(2)}, u32[]{:S(2)}) collective-permute-start(bf16[4,64,1280]{2,1,0:T(8,128)(2,1)S(1)} %stack.17.refs_0_), channel_id=1, source_target_pairs={{0,16},{1,65},{2,18},{3,67},{4,20},{5,69},{6,22},{7,71},{8,24},{9,... | collective-permute-start | bytes 1966088 | tf_op jit(solution)/shard_map/ppermute | solution.py:362
  80.6 15.9 %collective-permute-start.14 = (bf16[4,64,1280]{2,1,0:T(8,128)(2,1)S(1)}, bf16[4,64,1280]{2,1,0:T(8,128)(2,1)S(1)}, u32[]{:S(2)}, u32[]{:S(2)}) collective-permute-start(bf16[4,64,1280]{2,1,0:T(8,128)(2,1)S(1)} %stack.17.refs_0_), channel_id=1, source_target_pairs={{0,24},{1,97},{2,26},{3,99},{4,28},{5,101},{6,30},{7,103},{8,0},{9... | collective-permute-start | bytes 1966088 | tf_op jit(solution)/shard_map/ppermute | solution.py:362
  82.0 19.5 %collective-permute-start.13 = (bf16[4,64,1280]{2,1,0:T(8,128)(2,1)S(1)}, bf16[4,64,1280]{2,1,0:T(8,128)(2,1)S(1)}, u32[]{:S(2)}, u32[]{:S(2)}) collective-permute-start(bf16[4,64,1280]{2,1,0:T(8,128)(2,1)S(1)} %stack.17.refs_0_), channel_id=1, source_target_pairs={{0,8},{1,33},{2,10},{3,35},{4,12},{5,37},{6,14},{7,39},{8,16},{9,4... | collective-permute-start | bytes 1966088 | tf_op jit(solution)/shard_map/ppermute | solution.py:362
  82.1 19.4 %collective-permute-start.16 = (bf16[4,64,1280]{2,1,0:T(8,128)(2,1)S(1)}, bf16[4,64,1280]{2,1,0:T(8,128)(2,1)S(1)}, u32[]{:S(2)}, u32[]{:S(2)}) collective-permute-start(bf16[4,64,1280]{2,1,0:T(8,128)(2,1)S(1)} %stack.17.refs_0_), channel_id=1, source_target_pairs={{0,1},{1,0},{2,3},{3,2},{4,5},{5,4},{6,7},{7,6},{8,9},{9,8},{10,11... | collective-permute-start | bytes 1966088 | tf_op jit(solution)/shard_map/ppermute | solution.py:362
  90.0 11.5 %collective-permute-start.19 = (bf16[4,64,1280]{2,1,0:T(8,128)(2,1)S(1)}, bf16[4,64,1280]{2,1,0:T(8,128)(2,1)S(1)}, u32[]{:S(2)}, u32[]{:S(2)}) collective-permute-start(bf16[4,64,1280]{2,1,0:T(8,128)(2,1)S(1)} %collective-permute-done.15.refs_3_), channel_id=1, source_target_pairs={{0,1},{1,0},{2,3},{3,2},{4,5},{5,4},{6,7},{7,6},{8,9},{9,8},{10,11... | collective-permute-start | bytes 1966088 | tf_op jit(solution)/shard_map/ppermute | solution.py:362
  96.5 6.7 %collective-permute-start.18 = (bf16[4,64,1280]{2,1,0:T(8,128)(2,1)S(1)}, bf16[4,64,1280]{2,1,0:T(8,128)(2,1)S(1)}, u32[]{:S(2)}, u32[]{:S(2)}) collective-permute-start(bf16[4,64,1280]{2,1,0:T(8,128)(2,1)S(1)} %collective-permute-done.14.refs_2_), channel_id=1, source_target_pairs={{0,1},{1,0},{2,3},{3,2},{4,5},{5,4},{6,7},{7,6},{8,9},{9,8},{10,11... | collective-permute-start | bytes 1966088 | tf_op jit(solution)/shard_map/ppermute | solution.py:362
  101.5 2.7 %collective-permute-start.17 = (bf16[4,64,1280]{2,1,0:T(8,128)(2,1)S(1)}, bf16[4,64,1280]{2,1,0:T(8,128)(2,1)S(1)}, u32[]{:S(2)}, u32[]{:S(2)}) collective-permute-start(bf16[4,64,1280]{2,1,0:T(8,128)(2,1)S(1)} %collective-permute-done.13.refs_1_), channel_id=1, source_target_pairs={{0,1},{1,0},{2,3},{3,2},{4,5},{5,4},{6,7},{7,6},{8,9},{9,8},{10,11... | collective-permute-start | bytes 1966088 | tf_op jit(solution)/shard_map/ppermute | solution.py:362
  (10 other events, 17.8 us)

commit v4 on v3

--- a/solution.py
+++ b/solution.py
@@ -1,3 +1,4 @@
+import functools
 import math
 
 import jax
@@ -43,35 +44,24 @@
     return jnp.concatenate(parts, axis=0)
 
 
-def prep_kernel(mw, lw, tw, pw, gw, dw, wm, wt, gt, dt):
-    for tap in range(9):
-        wm[:, tap * LEV : (tap + 1) * LEV] = dot(
-            mw[:, tap * MESO : (tap + 1) * MESO], lw[...]
-        ).astype(BF)
-    pw16 = sixteen(pw[...], 0).astype(BF)
-    wt[...] = jnp.concatenate(
-        [dot_nt(tw[:, tap * TERR : (tap + 1) * TERR], pw16).astype(BF) for tap in range(9)], axis=1
-    )
-    for tap in range(9):
-        gt[:, tap * MIX : (tap + 1) * MIX] = gw[:, tap * JOINT : (tap + 1) * JOINT].T
-        dt[:, tap * MIX : (tap + 1) * MIX] = dw[:, tap * MIX : (tap + 1) * MIX].T
-
-
-def prep(meso_weight, lift_weight, terrain_weight, patch_turned, merging_weight, decoder_weight):
+def small_kernel(lw, pw, hw, lw_out, pw_out, head_turned):
+    lw_out[...] = lw[...]
+    pw_out[...] = sixteen(pw[...], 0).astype(BF)
+    head_turned[...] = sixteen(hw[...], 8).T.astype(BF)
+
+
+def small_weights(lift_weight, patch_turned, head_weight):
     return pl.pallas_call(
-        prep_kernel,
+        small_kernel,
         out_shape=(
-            jax.ShapeDtypeStruct((MESO, 9 * LEV), BF),
-            jax.ShapeDtypeStruct((TERR, 9 * SLAB), BF),
-            jax.ShapeDtypeStruct((JOINT, 9 * MIX), BF),
-            jax.ShapeDtypeStruct((MIX, 9 * MIX), BF),
+            jax.ShapeDtypeStruct((MESO, LEV), BF),
+            jax.ShapeDtypeStruct((SLAB, TERR), BF),
+            jax.ShapeDtypeStruct((MIX, SLAB), BF),
         ),
-        compiler_params=params(24),
-        cost_estimate=pl.CostEstimate(
-            flops=2 * 9 * 384 * 384 * 128, bytes_accessed=17_000_000, transcendentals=0
-        ),
-        name="prep",
-    )(meso_weight, lift_weight, terrain_weight, patch_turned, merging_weight, decoder_weight)
+        compiler_params=params(16),
+        cost_estimate=pl.CostEstimate(flops=0, bytes_accessed=4_000_000, transcendentals=0),
+        name="small_weights",
+    )(lift_weight, patch_turned, head_weight)
 
 
 def rows_kernel(place, own, partner, eight, first, last):
@@ -122,11 +112,12 @@
     return 0.5 * (1.0 + jnp.tanh(0.5 * v))
 
 
-def main_kernel(place, above, eight, below, hw, *refs):
-    n_w = 6
+def main_kernel(place, above, eight, below, lw, pw16, head_turned, *refs):
+    n_w = 4
     weights_hbm, keep, send, out = refs[:n_w], *refs[n_w : n_w + 3]
-    wm, wt, gw, dw, dt, gt = weights = refs[n_w + 3 : 2 * n_w + 3]
-    sems, x3, p9, j3, jslope, jdelta, m3, mslope, dout, d3, e3 = refs[2 * n_w + 3 :]
+    mw, tw, gw, dw = weights = refs[n_w + 3 : 2 * n_w + 3]
+    sems, wm, wt, dt, gt = refs[2 * n_w + 3 : 2 * n_w + 8]
+    x3, p9, j3, jslope, jdelta, m3, mslope, dout, d3, e3 = refs[2 * n_w + 8 :]
     copies = [
         pltpu.make_async_copy(u, v, sems.at[i]) for i, (u, v) in enumerate(zip(weights_hbm, weights))
     ]
@@ -162,9 +153,15 @@
                     tap = 3 * a + b
                     p9[tap * SLAB : (tap + 1) * SLAB, cut(r - a, 1)] = u[LEV:]
 
-    head_turned = sixteen(hw[...], 8).T.astype(BF)
     copies[0].wait()
+    for tap in range(9):
+        wm[:, tap * LEV : (tap + 1) * LEV] = dot(
+            mw[:, tap * MESO : (tap + 1) * MESO], lw[...]
+        ).astype(BF)
     copies[1].wait()
+    wt[...] = jnp.concatenate(
+        [dot_nt(tw[:, tap * TERR : (tap + 1) * TERR], pw16[...]).astype(BF) for tap in range(9)], axis=1
+    )
 
     for row in (0, 4, 8, 12):
         pre_t = dot(wt[...], p9[:, cut(row, 4)])
@@ -182,6 +179,11 @@
                 jslope[at : at + size, cut(row - 4, 4)] = sigma * (1.0 + pre * (1.0 - sigma))
 
     copies[2].wait()
+    copies[3].wait()
+    for tap in range(9):
+        gt[:, tap * MIX : (tap + 1) * MIX] = gw[:, tap * JOINT : (tap + 1) * JOINT].T
+        dt[:, tap * MIX : (tap + 1) * MIX] = dw[:, tap * MIX : (tap + 1) * MIX].T
+
     for row, rows in ((0, 4), (4, 5), (9, 5)):
         pre = sum(
             dot(gw[:, a * 3 * JOINT : (a + 1) * 3 * JOINT], j3[:, cut(row + a, rows)])
@@ -196,14 +198,13 @@
 
     scale = 1.0 / math.sqrt(8 * 32 * 128)
 
-    copies[3].wait()
     for row in (0, 4, 8):
         pre = sum(
             dot(dw[:, a * 3 * MIX : (a + 1) * 3 * MIX], m3[:, cut(row + a, 4)]) for a in range(3)
         )
         sigma = logistic(pre)
         cot = jnp.concatenate([slab(row + 3 + r)[LEV:] for r in range(4)], axis=1)
-        back = scale * dot(head_turned, cot)
+        back = scale * dot(head_turned[...], cot)
         v = sigma * (1.0 + pre * (1.0 - sigma)) * back
         left, right = neighbours(v)
         for b, u in enumerate((right, v, left)):
@@ -211,7 +212,6 @@
         lo, hi = max(row, 2), min(row + 4, 10)
         dout[:, cut(lo - 2, hi - lo)] = (pre * sigma)[:, cut(lo - row, hi - lo)].astype(BF)
 
-    copies[4].wait()
     for row in (0, 5):
         back = sum(
             dot(dt[:, a * 3 * MIX : (a + 1) * 3 * MIX], d3[:, cut(row + 2 - a, 5)])
@@ -222,7 +222,6 @@
         for b, u in enumerate((right, v, left)):
             e3[b * MIX : (b + 1) * MIX, cut(row, 5)] = u.astype(BF)
 
-    copies[5].wait()
     for row in (0, 4):
         back = sum(
             dot(gt[:, a * 3 * MIX : (a + 1) * 3 * MIX], e3[:, cut(row + 2 - a, 4)])
@@ -296,19 +295,23 @@
     send[...] = out[4:]
 
 
-def main(place, above, eight, below, head_weight, *weights):
+def main(place, above, eight, below, small_ones, *weights):
     smem = pl.BlockSpec(memory_space=pltpu.SMEM)
     vmem = pl.BlockSpec(memory_space=pltpu.VMEM)
-    hbm = pl.BlockSpec(memory_space=pl.ANY)
+    hbm = pl.BlockSpec(memory_space=pltpu.HBM)
     return pl.pallas_call(
         main_kernel,
         out_shape=(jax.ShapeDtypeStruct((4, OQ, WIDE), BF),) * 2,
-        in_specs=[smem] + [vmem] * 4 + [hbm] * len(weights),
+        in_specs=[smem] + [vmem] * 6 + [hbm] * len(weights),
         out_specs=(vmem, vmem),
         scratch_shapes=[
             pltpu.VMEM((8, OQ, WIDE), BF),
             *[pltpu.VMEM(w.shape, BF) for w in weights],
             pltpu.SemaphoreType.DMA((len(weights),)),
+            pltpu.VMEM((MESO, 9 * LEV), BF),
+            pltpu.VMEM((TERR, 9 * SLAB), BF),
+            pltpu.VMEM((MIX, 9 * MIX), BF),
+            pltpu.VMEM((JOINT, 9 * MIX), BF),
             pltpu.VMEM((3 * LEV, (ROWS + 2 * HALO) * COLS), BF),
             pltpu.VMEM((9 * SLAB, (ROWS + 8) * COLS), BF),
             pltpu.VMEM((3 * JOINT, (ROWS + 8) * COLS), BF),
@@ -320,12 +323,12 @@
             pltpu.VMEM((3 * MIX, (ROWS + 4) * COLS), BF),
             pltpu.VMEM((3 * MIX, (ROWS + 2) * COLS), BF),
         ],
-        compiler_params=params(46),
+        compiler_params=params(51),
         cost_estimate=pl.CostEstimate(
             flops=15_000_000_000, bytes_accessed=12_000_000, transcendentals=3_000_000
         ),
         name="sections",
-    )(place, above, eight, below, head_weight, *weights)
+    )(place, above, eight, below, *small_ones, *weights)
 
 
 def split_kernel(keep, came, own, next1, next2, next3):
@@ -335,10 +338,12 @@
 
 
 def total_kernel(own, one, two, three, out):
-    out[...] = (
-        (own[...].astype(F32) + two[...].astype(F32))
-        + (one[...].astype(F32) + three[...].astype(F32))
-    ).astype(BF)
+    parts = [v[...].astype(F32) for v in (own, one, two, three)]
+    out[...] = sum(parts[1:], parts[0]).astype(BF)
+
+
+def pair_kernel(own, other, out):
+    out[...] = (own[...].astype(F32) + other[...].astype(F32)).astype(BF)
 
 
 def stack_kernel(own, one, two, three, out):
@@ -374,6 +379,15 @@
     return moved(v, where)
 
 
+def across(v, axes, bits):
+    def where(*at):
+        to = list(at)
+        to[axes[at[3]]] ^= bits
+        return to
+
+    return moved(v, where)
+
+
 def to_partner(v):
     return moved(v, lambda z, x, y, c: (z, x, y, 1 - c))
 
@@ -387,50 +401,118 @@
     turns = (1, 2, 3)
     own, *parts = small(split_kernel, (wide, piece, piece, piece), keep, to_partner(send))
     own = small(total_kernel, piece, own, *[along(p, (CHIP, DP), j) for p, j in zip(parts, turns)])
-    own = small(total_kernel, piece, own, *[along(own, (DP, CHIP), j) for j in turns])
+    for bits in (1, 3):
+        own = small(pair_kernel, piece, own, across(own, (DP, CHIP), bits))
     four = jax.ShapeDtypeStruct((4, OQ, WIDE), BF)
     block = small(stack_kernel, four, own, *[along(own, (CHIP, SEGMENT), j) for j in turns])
     mine = (block,) + tuple(along(block, (SEGMENT, DP), -step) for step in STEPS[1:])
     return mine + tuple(to_partner(v) for v in mine)
 
 
+def origin(place, i, j, theirs):
+    segment, core, depth = place[0], place[1] % 2, place[2]
+    chip = place[1] // 2
+    kind = 1 - core if theirs else core
+    group = jnp.where(
+        kind == 0, lax.rem(chip - j + 4, 4), 4 + lax.rem(depth + STEPS[i] + 4, 4)
+    )
+    row = lax.rem(segment + jnp.where(kind == 0, STEPS[i], -j) + 4, 4)
+    return group, row
+
+
+def write_out(place, blocks, steps, merging, decoder, stage, sems):
+    def pieces(k, j):
+        group, row = origin(place, steps[k // 2], j, k % 2)
+        slot = stage.at[4 * k + j]
+        sem = sems.at[4 * k + j]
+        rows = pl.ds(pl.multiple_of(row * OQ, OQ), OQ)
+        left = 9 * JOINT - 4 * WIDE
+        yield group < 4, [
+            (slot, merging.at[rows, pl.ds(pl.multiple_of(group * WIDE, WIDE), WIDE)], sem)
+        ]
+        yield group == 4, [
+            (slot.at[:, :left], merging.at[rows, 4 * WIDE :], sem),
+            (slot.at[:, left:], decoder.at[rows, : WIDE - left], sems.at[4 * len(blocks)]),
+        ]
+        yield group == 5, [(slot, decoder.at[rows, WIDE - left : 2 * WIDE - left], sem)]
+        last = 9 * MIX - (2 * WIDE - left)
+        yield group == 6, [(slot.at[:, :last], decoder.at[rows, 2 * WIDE - left :], sem)]
+
+    def each(do):
+        for k in range(len(blocks)):
+            for j in range(4):
+                for when, copies in pieces(k, j):
+
+                    @pl.when(when)
+                    def _(copies=copies):
+                        for copy in copies:
+                            do(pltpu.make_async_copy(*copy))
+
+    for k, block in enumerate(blocks):
+        stage[4 * k : 4 * k + 4] = block[...].astype(F32)
+    each(lambda copy: copy.start())
+    return lambda: each(lambda copy: copy.wait())
+
+
+def early_kernel(step, n_old, place, *refs):
+    blocks, (merging, decoder, stage, sems) = refs[n_old : n_old + 2], refs[n_old + 2 :]
+    write_out(place, blocks, (step,), merging, decoder, stage, sems)()
+
+
+def write_early(place, step, mine, theirs, old):
+    smem = pl.BlockSpec(memory_space=pltpu.SMEM)
+    vmem = pl.BlockSpec(memory_space=pltpu.VMEM)
+    hbm = pl.BlockSpec(memory_space=pltpu.HBM)
+    return pl.pallas_call(
+        functools.partial(early_kernel, step, len(old)),
+        out_shape=(
+            jax.ShapeDtypeStruct((MIX, 9 * JOINT), F32),
+            jax.ShapeDtypeStruct((MIX, 9 * MIX), F32),
+        ),
+        in_specs=[smem] + [hbm] * len(old) + [vmem] * 2,
+        out_specs=(hbm, hbm),
+        scratch_shapes=[pltpu.VMEM((8, OQ, WIDE), F32), pltpu.SemaphoreType.DMA((9,))],
+        input_output_aliases={1 + i: i for i in range(len(old))},
+        compiler_params=params(12),
+        cost_estimate=pl.CostEstimate(flops=0, bytes_accessed=4_000_000, transcendentals=0),
+        name="early",
+    )(place, *old, mine, theirs)
+
+
 def finish_kernel(place, *refs):
-    blocks, (lw, pw, mw_hbm, tw_hbm) = refs[:8], refs[8:12]
-    patch, lift, head, terrain, meso, merging, decoder = refs[12:19]
-    mw, tw, stage, wide_m, wide_t, ht, gt, sems = refs[19:]
+    blocks, (lw, pw16, mw_hbm, tw_hbm) = refs[2:10], refs[10:14]
+    patch, lift, head, terrain, meso, merging, decoder = refs[14:21]
+    mw, tw, stage, rest, wide_m, wide_t, ht, gt, sems, late_sems = refs[21:]
     reads = [
         pltpu.make_async_copy(mw_hbm, mw, sems.at[0]),
         pltpu.make_async_copy(tw_hbm, tw, sems.at[1]),
     ]
     for copy in reads:
         copy.start()
-    segment, chip, core, depth = place[0], place[1] // 2, place[1] % 2, place[2]
-    for i, block in enumerate(blocks):
-        kind = core if i < 4 else 1 - core
-        for j in range(4):
-            along_segment = jnp.where(kind == 0, STEPS[i % 4], -j)
-            group = jnp.where(
-                kind == 0, lax.rem(chip - j + 4, 4), 4 + lax.rem(depth + STEPS[i % 4] + 4, 4)
-            )
-            row = lax.rem(segment + along_segment + 4, 4) * OQ
-            stage[
-                pl.ds(pl.multiple_of(row, OQ), OQ), pl.ds(pl.multiple_of(group * WIDE, WIDE), WIDE)
-            ] = block[j].astype(F32)
-    column = 9 * JOINT + 9 * MIX
-    writes = [
-        pltpu.make_async_copy(stage.at[:, : 9 * JOINT], merging, sems.at[2]),
-        pltpu.make_async_copy(stage.at[:, 9 * JOINT : column], decoder, sems.at[3]),
-    ]
-    for copy in writes:
-        copy.start()
+    late = [blocks[4 * theirs + i] for i in (1, 2) for theirs in (0, 1)]
+    written = write_out(place, late, (1, 2), merging, decoder, stage, late_sems)
+    for i in range(4):
+        for theirs in range(2):
+            for j in range(4):
+                group, row = origin(place, i, j, theirs)
+
+                @pl.when(group >= 6)
+                def _(i=i, theirs=theirs, j=j, group=group, row=row):
+                    rest[
+                        pl.ds(pl.multiple_of(row * OQ, OQ), OQ),
+                        pl.ds(pl.multiple_of((group - 6) * WIDE, WIDE), WIDE),
+                    ] = blocks[4 * theirs + i][j]
+
+    column = 9 * JOINT + 9 * MIX - 6 * WIDE
+    writes = []
     for seg in range(4):
         lo = seg * OQ
         at = seg * MQ
-        ht[at : at + 64, :] = stage[lo : lo + OQ, column : column + 9 * LEV].astype(BF)
+        ht[at : at + 64, :] = rest[lo : lo + OQ, column : column + 9 * LEV]
         spare = column + 9 * LEV
-        ht[at + 64 : at + MQ, :640] = stage[lo : lo + 32, spare : spare + 640].astype(BF)
-        ht[at + 64 : at + MQ, 640:] = stage[lo + 32 : lo + OQ, spare : spare + 512].astype(BF)
-        gt[lo : lo + OQ, :] = stage[lo : lo + OQ, spare + 640 : spare + 896]
+        ht[at + 64 : at + MQ, :640] = rest[lo : lo + 32, spare : spare + 640]
+        ht[at + 64 : at + MQ, 640:] = rest[lo + 32 : lo + OQ, spare : spare + 512]
+        gt[lo : lo + OQ, :] = rest[lo : lo + OQ, spare + 640 : spare + 896].astype(F32)
     for a in range(3):
         for tap in range(3 * a, 3 * a + 3):
             wide_m[:, tap * MESO : (tap + 1) * MESO] = dot_nt(
@@ -439,11 +521,10 @@
         part = slice(3 * a * MESO, 3 * (a + 1) * MESO)
         writes.append(pltpu.make_async_copy(wide_m.at[:, part], meso.at[:, part], sems.at[4 + a]))
         writes[-1].start()
-    pw16 = sixteen(pw[...], 0).astype(BF)
     g = gt[...]
     for tap in range(9):
         wide_t[:, tap * TERR : (tap + 1) * TERR] = dot(
-            g[:, tap * SLAB : (tap + 1) * SLAB].astype(BF), pw16
+            g[:, tap * SLAB : (tap + 1) * SLAB].astype(BF), pw16[...]
         )
     writes.append(pltpu.make_async_copy(wide_t, terrain, sems.at[7]))
     writes[-1].start()
@@ -465,12 +546,13 @@
     ).T
     for copy in writes:
         copy.wait()
-
-
-def finish(place, blocks, lift_weight, patch_turned, meso_weight, terrain_weight):
+    written()
+
+
+def finish(place, old, blocks, lift_copy, patch_turned, meso_weight, terrain_weight):
     smem = pl.BlockSpec(memory_space=pltpu.SMEM)
     vmem = pl.BlockSpec(memory_space=pltpu.VMEM)
-    hbm = pl.BlockSpec(memory_space=pl.ANY)
+    hbm = pl.BlockSpec(memory_space=pltpu.HBM)
     patch, lift, head, terrain, meso, merging, decoder = pl.pallas_call(
         finish_kernel,
         out_shape=(
@@ -482,21 +564,24 @@
             jax.ShapeDtypeStruct((MIX, 9 * JOINT), F32),
             jax.ShapeDtypeStruct((MIX, 9 * MIX), F32),
         ),
-        in_specs=[smem] + [vmem] * 10 + [hbm] * 2,
+        in_specs=[smem] + [hbm] * 2 + [vmem] * 10 + [hbm] * 2,
         out_specs=(vmem,) * 3 + (hbm,) * 4,
         scratch_shapes=[
             pltpu.VMEM((MESO, 9 * MESO), BF),
             pltpu.VMEM((TERR, 9 * TERR), BF),
-            pltpu.VMEM((MIX, 8 * WIDE), F32),
+            pltpu.VMEM((16, OQ, WIDE), F32),
+            pltpu.VMEM((MIX, 2 * WIDE), BF),
             pltpu.VMEM((MESO, 9 * MESO), F32),
             pltpu.VMEM((TERR, 9 * TERR), F32),
             pltpu.VMEM((MESO, 9 * LEV), BF),
             pltpu.VMEM((MIX, 256), F32),
             pltpu.SemaphoreType.DMA((8,)),
+            pltpu.SemaphoreType.DMA((17,)),
         ],
-        compiler_params=params(40),
+        input_output_aliases={1: 5, 2: 6},
+        compiler_params=params(36),
         name="finish",
-    )(place, *blocks, lift_weight, patch_turned, meso_weight, terrain_weight)
+    )(place, *old, *blocks, lift_copy, patch_turned, meso_weight, terrain_weight)
     return patch.T, terrain, lift, meso, merging, decoder, head
 
 
@@ -537,15 +622,22 @@
     place = jnp.stack([lax.axis_index(a) for a in ("segment", "space", "dp")]).astype(jnp.int32)
     eight, first, last = chip_rows(place, own, to_partner(own))
     above, below = to_chip(last, 1), to_chip(first, -1)
-    patch_turned = patch_weight.T
-    wm, wt, gt, dt = prep(
-        meso_weight, lift_weight, terrain_weight, patch_turned, merging_weight, decoder_weight
-    )
+    small_ones = small_weights(lift_weight, patch_weight.T, head_weight)
     keep, send = main(
-        place, above, eight, below, head_weight, wm, wt, merging_weight, decoder_weight, dt, gt
+        place,
+        above,
+        eight,
+        below,
+        small_ones,
+        meso_weight,
+        terrain_weight,
+        merging_weight,
+        decoder_weight,
     )
     blocks = summed_everywhere(keep, send)
-    return finish(place, blocks, lift_weight, patch_turned, meso_weight, terrain_weight)
+    old = write_early(place, 0, blocks[0], blocks[4], ())
+    old = write_early(place, 3, blocks[3], blocks[7], old)
+    return finish(place, old, blocks, *small_ones[:2], meso_weight, terrain_weight)
 
 
 def solution(mesh):

time: 113 us -> 110 us (0.973)
  local copies, waits for them, and re-layouts: 9.95 us -> 4.72 us
  starting transfers between devices: 39 us -> 40.8 us
  Pallas kernels: 34.8 us -> 36.4 us
    unnamed x30 -> x14, local copies, waits for them, and re-layouts: 9.84 us -> 4.61 us
    pallas_call x1 -> x3, Pallas kernels: 1.35 us -> 4.35 us  [the longest x2 4.24 us: write_early(): pl.pallas_call(functools.partial(early_kernel, step, len(old)), out_shape...]
    ppermute x20 -> x19, starting transfers between devices: 39 us -> 40.8 us  [moved(): return lax.ppermute(v, ('dp', 'segment', 'space'), pairs)]
    pallas_call x1, Pallas kernels: 8.39 us -> 6.82 us  [finish(): pl.pallas_call(finish_kernel, out_shape=(jax.ShapeDtypeStruct((8, TERR),...]
    ppermute x20 -> x19, waiting for transfers between devices: 27.6 us -> 26.8 us  [moved(): return lax.ppermute(v, ('dp', 'segment', 'space'), pairs)]
  transfers between devices with their start and end apart: 20 -> 19, of which waited for: 14 -> 12; matrix products, arithmetic and copies ran while one was open for 0% -> 0% of each run, Pallas kernels for 1% -> 4%
where the time goes in v4:
time: 110 us
  starting transfers between devices  40.8 us (37%)
  Pallas kernels  36.4 us (33%)
  waiting for transfers between devices  26.8 us (24%)
  local copies, waits for them, and re-layouts  4.72 us (4%)
    ppermute x19, starting transfers between devices, moved(): return lax.ppermute(v, ('dp', 'segment', 'space'), pairs)  40.8 us
    ppermute x19, waiting for transfers between devices, moved(): return lax.ppermute(v, ('dp', 'segment', 'space'), pairs)  26.8 us
    pallas_call x1, Pallas kernels, main(): pl.pallas_call(main_kernel, out_shape=(jax.ShapeDtypeStruct((4, OQ, WIDE)...  24.3 us
    pallas_call x1, Pallas kernels, finish(): pl.pallas_call(finish_kernel, out_shape=(jax.ShapeDtypeStruct((8, TERR),...  6.82 us
    unnamed x14, local copies, waits for them, and re-layouts  4.61 us
    pallas_call x2, Pallas kernels, write_early(): pl.pallas_call(functools.partial(early_kernel, step, len(old)), out_shape...  4.24 us
  transfers between devices with their start and end apart: 19, of which 12 were waited for; matrix products, arithmetic and copies ran while one was open for 0% of the time, Pallas kernels for 4%

profile of v4, /device:TPU:1, one launch (start us, length us, event | category | flops | bytes accessed | tf_op | source)
XLA Modules:
  0.0 110.1 jit_solution(12385930305399858510)
XLA Ops:
  2.8 1.5 %collective-permute-start = (bf16[2,4,144,128]{3,2,1,0:T(8,128)(2,1)S(1)}, bf16[2,4,144,128]{3,2,1,0:T(8,128)(2,1)S(1)}, u32[]{:S(2)}, u32[]{:S(2)}) collective-permute-start(bf16[2,4,144,128]{3,2,1,0:T(8,128)(2,1)S(1)} %maximum_maximum_fusion.own), channel_id=1, source_target_pairs={{0,1},{1,0},{2,3},{3,2},{4,5},{5,4},{6,7},{7,6},{8,9},{9,8},{10,11... | collective-permute-start | bytes 884744 | tf_op jit(solution)/shard_map/ppermute | solution.py:367
  6.2 3.3 %collective-permute-start.1 = (bf16[5,144,128]{2,1,0:T(8,128)(2,1)S(1)}, bf16[5,144,128]{2,1,0:T(8,128)(2,1)S(1)}, u32[]{:S(2)}, u32[]{:S(2)}) collective-permute-start(bf16[5,144,128]{2,1,0:T(8,128)(2,1)S(1)} %get-tuple-element.30), channel_id=1, source_target_pairs={{0,2},{1,3},{2,4},{3,5},{4,6},{5,7},{8,10},{9,11},{10,12},{11,13},... | collective-permute-start | bytes 552968 | tf_op jit(solution)/shard_map/ppermute | solution.py:367
  13.1 3.7 %collective-permute-done.2.below = bf16[5,144,128]{2,1,0:T(8,128)(2,1)S(1)} collective-permute-done((bf16[5,144,128]{2,1,0:T(8,128)(2,1)S(1)}, bf16[5,144,128]{2,1,0:T(8,128)(2,1)S(1)}, u32[]{:S(2)}, u32[]{:S(2)}) %collective-permute-start.2) | collective-permute-done | bytes 184352 | tf_op jit(solution)/shard_map/ppermute | solution.py:367
  16.9 24.3 %sections.1 = (bf16[4,64,1280]{2,1,0:T(8,128)(2,1)S(1)}, bf16[4,64,1280]{2,1,0:T(8,128)(2,1)S(1)}) custom-call(s32[3]{0:T(128)S(1)} %pad_add_fusion.place, bf16[5,144,128]{2,1,0:T(8,128)(2,1)S(1)} %collective-permute-done.1.above, bf16[8,144,128]{2,1,0:T(8,128)(2,1)S(1)} %get-tuple-element.31.eight, bf16[5,144,128]{2,1,0:T(8,128)(2,1)S(1)} %collective-permute-done.2.below, ...), custom_call_target="tpu_custom_call" | custom-call | flops 15000000512 | bytes 12000000 | tf_op jit(solution)/shard_map/sections/pallas_call | solution.py:302
  41.2 1.6 %collective-permute-start.3 = (bf16[4,64,1280]{2,1,0:T(8,128)(2,1)S(1)}, bf16[4,64,1280]{2,1,0:T(8,128)(2,1)S(1)}, u32[]{:S(2)}, u32[]{:S(2)}) collective-permute-start(bf16[4,64,1280]{2,1,0:T(8,128)(2,1)S(1)} %get-tuple-element.37), channel_id=1, source_target_pairs={{0,1},{1,0},{2,3},{3,2},{4,5},{5,4},{6,7},{7,6},{8,9},{9,8},{10,11... | collective-permute-start | bytes 1966088 | tf_op jit(solution)/shard_map/ppermute | solution.py:367
  42.8 1.7 %collective-permute-done.3.came = bf16[4,64,1280]{2,1,0:T(8,128)(2,1)S(1)} collective-permute-done((bf16[4,64,1280]{2,1,0:T(8,128)(2,1)S(1)}, bf16[4,64,1280]{2,1,0:T(8,128)(2,1)S(1)}, u32[]{:S(2)}, u32[]{:S(2)}) %collective-permute-start.3) | collective-permute-done | bytes 655392 | tf_op jit(solution)/shard_map/ppermute | solution.py:367
  44.6 1.7 %collective-permute-start.4 = (bf16[64,1280]{1,0:T(8,128)(2,1)S(1)}, bf16[64,1280]{1,0:T(8,128)(2,1)S(1)}, u32[]{:S(2)}, u32[]{:S(2)}) collective-permute-start(bf16[64,1280]{1,0:T(8,128)(2,1)S(1)} %get-tuple-element.39), channel_id=1, source_target_pairs={{0,2},{1,33},{2,4},{3,35},{4,6},{5,37},{6,0},{7,39},{8,10},{9,41},... | collective-permute-start | bytes 491528 | tf_op jit(solution)/shard_map/ppermute | solution.py:367
  46.3 3.3 %collective-permute-start.5 = (bf16[64,1280]{1,0:T(8,128)(2,1)S(1)}, bf16[64,1280]{1,0:T(8,128)(2,1)S(1)}, u32[]{:S(2)}, u32[]{:S(2)}) collective-permute-start(bf16[64,1280]{1,0:T(8,128)(2,1)S(1)} %get-tuple-element.40), channel_id=1, source_target_pairs={{0,4},{1,65},{2,6},{3,67},{4,0},{5,69},{6,2},{7,71},{8,12},{9,73},... | collective-permute-start | bytes 491528 | tf_op jit(solution)/shard_map/ppermute | solution.py:367
  51.4 2.6 %collective-permute-done.5.two = bf16[64,1280]{1,0:T(8,128)(2,1)S(1)} collective-permute-done((bf16[64,1280]{1,0:T(8,128)(2,1)S(1)}, bf16[64,1280]{1,0:T(8,128)(2,1)S(1)}, u32[]{:S(2)}, u32[]{:S(2)}) %collective-permute-start.5) | collective-permute-done | bytes 163872 | tf_op jit(solution)/shard_map/ppermute | solution.py:367
  55.6 3.2 %collective-permute-done.7.other = bf16[64,1280]{1,0:T(8,128)(2,1)S(1)} collective-permute-done((bf16[64,1280]{1,0:T(8,128)(2,1)S(1)}, bf16[64,1280]{1,0:T(8,128)(2,1)S(1)}, u32[]{:S(2)}, u32[]{:S(2)}) %collective-permute-start.7) | collective-permute-done | bytes 163872 | tf_op jit(solution)/shard_map/ppermute | solution.py:367
  60.0 4.2 %collective-permute-done.8.other = bf16[64,1280]{1,0:T(8,128)(2,1)S(1)} collective-permute-done((bf16[64,1280]{1,0:T(8,128)(2,1)S(1)}, bf16[64,1280]{1,0:T(8,128)(2,1)S(1)}, u32[]{:S(2)}, u32[]{:S(2)}) %collective-permute-start.8) | collective-permute-done | bytes 163872 | tf_op jit(solution)/shard_map/ppermute | solution.py:367
  64.3 2.6 %collective-permute-start.11 = (bf16[64,1280]{1,0:T(8,128)(2,1)S(1)}, bf16[64,1280]{1,0:T(8,128)(2,1)S(1)}, u32[]{:S(2)}, u32[]{:S(2)}) collective-permute-start(bf16[64,1280]{1,0:T(8,128)(2,1)S(1)} %pair.3.own), channel_id=1, source_target_pairs={{0,6},{1,25},{2,0},{3,27},{4,2},{5,29},{6,4},{7,31},{8,14},{9,1},{... | collective-permute-start | bytes 491528 | tf_op jit(solution)/shard_map/ppermute | solution.py:367
  68.0 2.9 %collective-permute-done.11.three = bf16[64,1280]{1,0:T(8,128)(2,1)S(1)} collective-permute-done((bf16[64,1280]{1,0:T(8,128)(2,1)S(1)}, bf16[64,1280]{1,0:T(8,128)(2,1)S(1)}, u32[]{:S(2)}, u32[]{:S(2)}) %collective-permute-start.11) | collective-permute-done | bytes 163872 | tf_op jit(solution)/shard_map/ppermute | solution.py:367
  70.8 1.8 %collective-permute-done.10.two = bf16[64,1280]{1,0:T(8,128)(2,1)S(1)} collective-permute-done((bf16[64,1280]{1,0:T(8,128)(2,1)S(1)}, bf16[64,1280]{1,0:T(8,128)(2,1)S(1)}, u32[]{:S(2)}, u32[]{:S(2)}) %collective-permute-start.10) | collective-permute-done | bytes 163872 | tf_op jit(solution)/shard_map/ppermute | solution.py:367
  72.6 1.7 %collective-permute-done.9.one = bf16[64,1280]{1,0:T(8,128)(2,1)S(1)} collective-permute-done((bf16[64,1280]{1,0:T(8,128)(2,1)S(1)}, bf16[64,1280]{1,0:T(8,128)(2,1)S(1)}, u32[]{:S(2)}, u32[]{:S(2)}) %collective-permute-start.9) | collective-permute-done | bytes 163872 | tf_op jit(solution)/shard_map/ppermute | solution.py:367
  74.3 2.3 %collective-permute-start.13 = (bf16[4,64,1280]{2,1,0:T(8,128)(2,1)S(1)}, bf16[4,64,1280]{2,1,0:T(8,128)(2,1)S(1)}, u32[]{:S(2)}, u32[]{:S(2)}) collective-permute-start(bf16[4,64,1280]{2,1,0:T(8,128)(2,1)S(1)} %stack.17.refs_0_.refs_2_), channel_id=1, source_target_pairs={{0,16},{1,65},{2,18},{3,67},{4,20},{5,69},{6,22},{7,71},{8,24},{9,... | collective-permute-start | bytes 1966088 | tf_op jit(solution)/shard_map/ppermute | solution.py:367
  76.6 1.7 %collective-permute-start.16 = (bf16[4,64,1280]{2,1,0:T(8,128)(2,1)S(1)}, bf16[4,64,1280]{2,1,0:T(8,128)(2,1)S(1)}, u32[]{:S(2)}, u32[]{:S(2)}) collective-permute-start(bf16[4,64,1280]{2,1,0:T(8,128)(2,1)S(1)} %stack.17.refs_0_.refs_2_), channel_id=1, source_target_pairs={{0,24},{1,97},{2,26},{3,99},{4,28},{5,101},{6,30},{7,103},{8,0},{9... | collective-permute-start | bytes 1966088 | tf_op jit(solution)/shard_map/ppermute | solution.py:367
  78.3 5.6 %collective-permute-start.12 = (bf16[4,64,1280]{2,1,0:T(8,128)(2,1)S(1)}, bf16[4,64,1280]{2,1,0:T(8,128)(2,1)S(1)}, u32[]{:S(2)}, u32[]{:S(2)}) collective-permute-start(bf16[4,64,1280]{2,1,0:T(8,128)(2,1)S(1)} %stack.17.refs_0_.refs_2_), channel_id=1, source_target_pairs={{0,1},{1,0},{2,3},{3,2},{4,5},{5,4},{6,7},{7,6},{8,9},{9,8},{10,11... | collective-permute-start | bytes 1966088 | tf_op jit(solution)/shard_map/ppermute | solution.py:367
  83.9 1.7 %collective-permute-done.13.refs_2_.refs_5_ = bf16[4,64,1280]{2,1,0:T(8,128)(2,1)S(1)} collective-permute-done((bf16[4,64,1280]{2,1,0:T(8,128)(2,1)S(1)}, bf16[4,64,1280]{2,1,0:T(8,128)(2,1)S(1)}, u32[]{:S(2)}, u32[]{:S(2)}) %collective-permute-start.13) | collective-permute-done | bytes 655392 | tf_op jit(solution)/shard_map/ppermute | solution.py:367
  85.7 5.4 %collective-permute-start.14 = (bf16[4,64,1280]{2,1,0:T(8,128)(2,1)S(1)}, bf16[4,64,1280]{2,1,0:T(8,128)(2,1)S(1)}, u32[]{:S(2)}, u32[]{:S(2)}) collective-permute-start(bf16[4,64,1280]{2,1,0:T(8,128)(2,1)S(1)} %collective-permute-done.13.refs_2_.refs_5_), channel_id=1, source_target_pairs={{0,1},{1,0},{2,3},{3,2},{4,5},{5,4},{6,7},{7,6},{8,9},{9,8},{10,11... | collective-permute-start | bytes 1966088 | tf_op jit(solution)/shard_map/ppermute | solution.py:367
  92.2 6.0 %collective-permute-start.18 = (bf16[4,64,1280]{2,1,0:T(8,128)(2,1)S(1)}, bf16[4,64,1280]{2,1,0:T(8,128)(2,1)S(1)}, u32[]{:S(2)}, u32[]{:S(2)}) collective-permute-start(bf16[4,64,1280]{2,1,0:T(8,128)(2,1)S(1)} %collective-permute-done.16.refs_4_), channel_id=1, source_target_pairs={{0,1},{1,0},{2,3},{3,2},{4,5},{5,4},{6,7},{7,6},{8,9},{9,8},{10,11... | collective-permute-start | bytes 1966088 | tf_op jit(solution)/shard_map/ppermute | solution.py:367
  98.1 2.3 %early.2 = (f32[256,5760]{1,0:T(8,128)}, f32[256,2304]{1,0:T(8,128)}) custom-call(s32[3]{0:T(128)S(1)} %pad_add_fusion.place, bf16[4,64,1280]{2,1,0:T(8,128)(2,1)S(1)} %stack.17.refs_0_.refs_2_, bf16[4,64,1280]{2,1,0:T(8,128)(2,1)S(1)} %collective-permute-done.12.refs_1_.refs_6_), custom_call_target="tpu_custom_call" | custom-call | bytes 4000000 | tf_op jit(solution)/shard_map/early/pallas_call | solution.py:466
  100.5 2.0 %early.3 = (f32[256,5760]{1,0:T(8,128)}, f32[256,2304]{1,0:T(8,128)}) custom-call(s32[3]{0:T(128)S(1)} %pad_add_fusion.place, f32[256,5760]{1,0:T(8,128)} %get-tuple-element.42.refs_0_, f32[256,2304]{1,0:T(8,128)} %get-tuple-element.43.refs_1_, ...), custom_call_target="tpu_custom_call", output_to_operand_aliasing={{0}: (1, {}), {1}: (2, {})} | custom-call | bytes 4000000 | tf_op jit(solution)/shard_map/early/pallas_call | solution.py:466
  103.1 6.8 %finish.1 = (f32[8,256]{1,0:T(8,128)}, f32[384,128]{1,0:T(8,128)}, f32[3,256]{1,0:T(4,128)}, f32[256,2304]{1,0:T(8,128)}, f32[384,3456]{1,0:T(8,128)}, /*index=5*/f32[256,5760]{1,0:T(8,128)}, f32[256,2304]{1,0:T(8,128)}) custom-call(s32[3]{0:T(128)S(1)} %pad_add_fusion.place, ...), custom_call_target="tpu_custom_call", output_to_operand_aliasing={{5}: (1, {}), {6}: (2, {})} | custom-call | tf_op jit(solution)/shard_map/finish/pallas_call | solution.py:556
  (49 shorter events, 15.3 us)
Async XLA Ops:
  0.6 0.8 copy-start
  2.8 2.7 %collective-permute-start = (bf16[2,4,144,128]{3,2,1,0:T(8,128)(2,1)S(1)}, bf16[2,4,144,128]{3,2,1,0:T(8,128)(2,1)S(1)}, u32[]{:S(2)}, u32[]{:S(2)}) collective-permute-start(bf16[2,4,144,128]{3,2,1,0:T(8,128)(2,1)S(1)} %maximum_maximum_fusion.own), channel_id=1, source_target_pairs={{0,1},{1,0},{2,3},{3,2},{4,5},{5,4},{6,7},{7,6},{8,9},{9,8},{10,11... | collective-permute-start | bytes 884744 | tf_op jit(solution)/shard_map/ppermute | solution.py:367
  6.2 7.0 %collective-permute-start.1 = (bf16[5,144,128]{2,1,0:T(8,128)(2,1)S(1)}, bf16[5,144,128]{2,1,0:T(8,128)(2,1)S(1)}, u32[]{:S(2)}, u32[]{:S(2)}) collective-permute-start(bf16[5,144,128]{2,1,0:T(8,128)(2,1)S(1)} %get-tuple-element.30), channel_id=1, source_target_pairs={{0,2},{1,3},{2,4},{3,5},{4,6},{5,7},{8,10},{9,11},{10,12},{11,13},... | collective-permute-start | bytes 552968 | tf_op jit(solution)/shard_map/ppermute | solution.py:367
  9.5 7.4 %collective-permute-start.2 = (bf16[5,144,128]{2,1,0:T(8,128)(2,1)S(1)}, bf16[5,144,128]{2,1,0:T(8,128)(2,1)S(1)}, u32[]{:S(2)}, u32[]{:S(2)}) collective-permute-start(bf16[5,144,128]{2,1,0:T(8,128)(2,1)S(1)} %get-tuple-element.32), channel_id=1, source_target_pairs={{2,0},{3,1},{4,2},{5,3},{6,4},{7,5},{10,8},{11,9},{12,10},{13,11},... | collective-permute-start | bytes 552968 | tf_op jit(solution)/shard_map/ppermute | solution.py:367
  10.8 0.9 copy-start.3
  11.7 0.7 copy-start.4
  41.2 3.3 %collective-permute-start.3 = (bf16[4,64,1280]{2,1,0:T(8,128)(2,1)S(1)}, bf16[4,64,1280]{2,1,0:T(8,128)(2,1)S(1)}, u32[]{:S(2)}, u32[]{:S(2)}) collective-permute-start(bf16[4,64,1280]{2,1,0:T(8,128)(2,1)S(1)} %get-tuple-element.37), channel_id=1, source_target_pairs={{0,1},{1,0},{2,3},{3,2},{4,5},{5,4},{6,7},{7,6},{8,9},{9,8},{10,11... | collective-permute-start | bytes 1966088 | tf_op jit(solution)/shard_map/ppermute | solution.py:367
  44.6 6.8 %collective-permute-start.4 = (bf16[64,1280]{1,0:T(8,128)(2,1)S(1)}, bf16[64,1280]{1,0:T(8,128)(2,1)S(1)}, u32[]{:S(2)}, u32[]{:S(2)}) collective-permute-start(bf16[64,1280]{1,0:T(8,128)(2,1)S(1)} %get-tuple-element.39), channel_id=1, source_target_pairs={{0,2},{1,33},{2,4},{3,35},{4,6},{5,37},{6,0},{7,39},{8,10},{9,41},... | collective-permute-start | bytes 491528 | tf_op jit(solution)/shard_map/ppermute | solution.py:367
  46.3 7.8 %collective-permute-start.5 = (bf16[64,1280]{1,0:T(8,128)(2,1)S(1)}, bf16[64,1280]{1,0:T(8,128)(2,1)S(1)}, u32[]{:S(2)}, u32[]{:S(2)}) collective-permute-start(bf16[64,1280]{1,0:T(8,128)(2,1)S(1)} %get-tuple-element.40), channel_id=1, source_target_pairs={{0,4},{1,65},{2,6},{3,67},{4,0},{5,69},{6,2},{7,71},{8,12},{9,73},... | collective-permute-start | bytes 491528 | tf_op jit(solution)/shard_map/ppermute | solution.py:367
  49.6 4.5 %collective-permute-start.6 = (bf16[64,1280]{1,0:T(8,128)(2,1)S(1)}, bf16[64,1280]{1,0:T(8,128)(2,1)S(1)}, u32[]{:S(2)}, u32[]{:S(2)}) collective-permute-start(bf16[64,1280]{1,0:T(8,128)(2,1)S(1)} %get-tuple-element.41), channel_id=1, source_target_pairs={{0,6},{1,97},{2,0},{3,99},{4,2},{5,101},{6,4},{7,103},{8,14},{9,10... | collective-permute-start | bytes 491528 | tf_op jit(solution)/shard_map/ppermute | solution.py:367
  54.2 4.5 %collective-permute-start.7 = (bf16[64,1280]{1,0:T(8,128)(2,1)S(1)}, bf16[64,1280]{1,0:T(8,128)(2,1)S(1)}, u32[]{:S(2)}, u32[]{:S(2)}) collective-permute-start(bf16[64,1280]{1,0:T(8,128)(2,1)S(1)} %total.1.own), channel_id=1, source_target_pairs={{0,32},{1,3},{2,34},{3,1},{4,36},{5,7},{6,38},{7,5},{8,40},{9,11},... | collective-permute-start | bytes 491528 | tf_op jit(solution)/shard_map/ppermute | solution.py:367
  58.8 5.5 %collective-permute-start.8 = (bf16[64,1280]{1,0:T(8,128)(2,1)S(1)}, bf16[64,1280]{1,0:T(8,128)(2,1)S(1)}, u32[]{:S(2)}, u32[]{:S(2)}) collective-permute-start(bf16[64,1280]{1,0:T(8,128)(2,1)S(1)} %pair.2.own), channel_id=1, source_target_pairs={{0,96},{1,7},{2,98},{3,5},{4,100},{5,3},{6,102},{7,1},{8,104},{9,1... | collective-permute-start | bytes 491528 | tf_op jit(solution)/shard_map/ppermute | solution.py:367
  64.3 6.6 %collective-permute-start.11 = (bf16[64,1280]{1,0:T(8,128)(2,1)S(1)}, bf16[64,1280]{1,0:T(8,128)(2,1)S(1)}, u32[]{:S(2)}, u32[]{:S(2)}) collective-permute-start(bf16[64,1280]{1,0:T(8,128)(2,1)S(1)} %pair.3.own), channel_id=1, source_target_pairs={{0,6},{1,25},{2,0},{3,27},{4,2},{5,29},{6,4},{7,31},{8,14},{9,1},{... | collective-permute-start | bytes 491528 | tf_op jit(solution)/shard_map/ppermute | solution.py:367
  66.8 5.8 %collective-permute-start.10 = (bf16[64,1280]{1,0:T(8,128)(2,1)S(1)}, bf16[64,1280]{1,0:T(8,128)(2,1)S(1)}, u32[]{:S(2)}, u32[]{:S(2)}) collective-permute-start(bf16[64,1280]{1,0:T(8,128)(2,1)S(1)} %pair.3.own), channel_id=1, source_target_pairs={{0,4},{1,17},{2,6},{3,19},{4,0},{5,21},{6,2},{7,23},{8,12},{9,25},... | collective-permute-start | bytes 491528 | tf_op jit(solution)/shard_map/ppermute | solution.py:367
  67.4 6.9 %collective-permute-start.9 = (bf16[64,1280]{1,0:T(8,128)(2,1)S(1)}, bf16[64,1280]{1,0:T(8,128)(2,1)S(1)}, u32[]{:S(2)}, u32[]{:S(2)}) collective-permute-start(bf16[64,1280]{1,0:T(8,128)(2,1)S(1)} %pair.3.own), channel_id=1, source_target_pairs={{0,2},{1,9},{2,4},{3,11},{4,6},{5,13},{6,0},{7,15},{8,10},{9,17},{... | collective-permute-start | bytes 491528 | tf_op jit(solution)/shard_map/ppermute | solution.py:367
  74.3 11.4 %collective-permute-start.13 = (bf16[4,64,1280]{2,1,0:T(8,128)(2,1)S(1)}, bf16[4,64,1280]{2,1,0:T(8,128)(2,1)S(1)}, u32[]{:S(2)}, u32[]{:S(2)}) collective-permute-start(bf16[4,64,1280]{2,1,0:T(8,128)(2,1)S(1)} %stack.17.refs_0_.refs_2_), channel_id=1, source_target_pairs={{0,16},{1,65},{2,18},{3,67},{4,20},{5,69},{6,22},{7,71},{8,24},{9,... | collective-permute-start | bytes 1966088 | tf_op jit(solution)/shard_map/ppermute | solution.py:367
  76.6 15.6 %collective-permute-start.16 = (bf16[4,64,1280]{2,1,0:T(8,128)(2,1)S(1)}, bf16[4,64,1280]{2,1,0:T(8,128)(2,1)S(1)}, u32[]{:S(2)}, u32[]{:S(2)}) collective-permute-start(bf16[4,64,1280]{2,1,0:T(8,128)(2,1)S(1)} %stack.17.refs_0_.refs_2_), channel_id=1, source_target_pairs={{0,24},{1,97},{2,26},{3,99},{4,28},{5,101},{6,30},{7,103},{8,0},{9... | collective-permute-start | bytes 1966088 | tf_op jit(solution)/shard_map/ppermute | solution.py:367
  78.3 19.8 %collective-permute-start.15 = (bf16[4,64,1280]{2,1,0:T(8,128)(2,1)S(1)}, bf16[4,64,1280]{2,1,0:T(8,128)(2,1)S(1)}, u32[]{:S(2)}, u32[]{:S(2)}) collective-permute-start(bf16[4,64,1280]{2,1,0:T(8,128)(2,1)S(1)} %stack.17.refs_0_.refs_2_), channel_id=1, source_target_pairs={{0,8},{1,33},{2,10},{3,35},{4,12},{5,37},{6,14},{7,39},{8,16},{9,4... | collective-permute-start | bytes 1966088 | tf_op jit(solution)/shard_map/ppermute | solution.py:367
  78.3 19.8 %collective-permute-start.12 = (bf16[4,64,1280]{2,1,0:T(8,128)(2,1)S(1)}, bf16[4,64,1280]{2,1,0:T(8,128)(2,1)S(1)}, u32[]{:S(2)}, u32[]{:S(2)}) collective-permute-start(bf16[4,64,1280]{2,1,0:T(8,128)(2,1)S(1)} %stack.17.refs_0_.refs_2_), channel_id=1, source_target_pairs={{0,1},{1,0},{2,3},{3,2},{4,5},{5,4},{6,7},{7,6},{8,9},{9,8},{10,11... | collective-permute-start | bytes 1966088 | tf_op jit(solution)/shard_map/ppermute | solution.py:367
  85.7 14.8 %collective-permute-start.14 = (bf16[4,64,1280]{2,1,0:T(8,128)(2,1)S(1)}, bf16[4,64,1280]{2,1,0:T(8,128)(2,1)S(1)}, u32[]{:S(2)}, u32[]{:S(2)}) collective-permute-start(bf16[4,64,1280]{2,1,0:T(8,128)(2,1)S(1)} %collective-permute-done.13.refs_2_.refs_5_), channel_id=1, source_target_pairs={{0,1},{1,0},{2,3},{3,2},{4,5},{5,4},{6,7},{7,6},{8,9},{9,8},{10,11... | collective-permute-start | bytes 1966088 | tf_op jit(solution)/shard_map/ppermute | solution.py:367
  92.2 10.3 %collective-permute-start.18 = (bf16[4,64,1280]{2,1,0:T(8,128)(2,1)S(1)}, bf16[4,64,1280]{2,1,0:T(8,128)(2,1)S(1)}, u32[]{:S(2)}, u32[]{:S(2)}) collective-permute-start(bf16[4,64,1280]{2,1,0:T(8,128)(2,1)S(1)} %collective-permute-done.16.refs_4_), channel_id=1, source_target_pairs={{0,1},{1,0},{2,3},{3,2},{4,5},{5,4},{6,7},{7,6},{8,9},{9,8},{10,11... | collective-permute-start | bytes 1966088 | tf_op jit(solution)/shard_map/ppermute | solution.py:367
  98.1 4.3 %collective-permute-start.17 = (bf16[4,64,1280]{2,1,0:T(8,128)(2,1)S(1)}, bf16[4,64,1280]{2,1,0:T(8,128)(2,1)S(1)}, u32[]{:S(2)}, u32[]{:S(2)}) collective-permute-start(bf16[4,64,1280]{2,1,0:T(8,128)(2,1)S(1)} %collective-permute-done.15.refs_3_), channel_id=1, source_target_pairs={{0,1},{1,0},{2,3},{3,2},{4,5},{5,4},{6,7},{7,6},{8,9},{9,8},{10,11... | collective-permute-start | bytes 1966088 | tf_op jit(solution)/shard_map/ppermute | solution.py:367
  100.4 2.0 %copy-start.1 = (bf16[384,3456]{1,0:T(8,128)(2,1)S(1)}, bf16[384,3456]{1,0:T(8,128)(2,1)}, u32[]{:S(2)}) copy-start(bf16[384,3456]{1,0:T(8,128)(2,1)} %refs_12_.1) | copy-start | bytes 7962628
  100.4 2.7 %copy-start.2 = (bf16[256,2304]{1,0:T(8,128)(2,1)S(1)}, bf16[256,2304]{1,0:T(8,128)(2,1)}, u32[]{:S(2)}) copy-start(bf16[256,2304]{1,0:T(8,128)(2,1)} %refs_13_.1) | copy-start | bytes 3538948
  (1 other events, 0.7 us)

commit v5 on v4

--- a/solution.py
+++ b/solution.py
@@ -346,9 +346,10 @@
     out[...] = (own[...].astype(F32) + other[...].astype(F32)).astype(BF)
 
 
-def stack_kernel(own, one, two, three, out):
+def stack_kernel(own, one, two, three, out, half0, half1):
     for j, v in enumerate((own, one, two, three)):
         out[j] = v[...]
+        (half0, half1)[j // 2][j % 2] = v[...]
 
 
 def small(kernel, out_shape, *operands):
@@ -392,10 +393,10 @@
     return moved(v, lambda z, x, y, c: (z, x, y, 1 - c))
 
 
-STEPS = (0, -1, 1, -2)
-
-
-def summed_everywhere(keep, send):
+PARTS = ((0, 0, 4), (-1, 0, 2), (-1, 2, 2), (1, 0, 2), (1, 2, 2), (-2, 0, 2), (-2, 2, 2))
+
+
+def summed_everywhere(place, keep, send):
     piece = jax.ShapeDtypeStruct((OQ, WIDE), BF)
     wide = jax.ShapeDtypeStruct((OQ, WIDE), F32)
     turns = (1, 2, 3)
@@ -404,104 +405,133 @@
     for bits in (1, 3):
         own = small(pair_kernel, piece, own, across(own, (DP, CHIP), bits))
     four = jax.ShapeDtypeStruct((4, OQ, WIDE), BF)
-    block = small(stack_kernel, four, own, *[along(own, (CHIP, SEGMENT), j) for j in turns])
-    mine = (block,) + tuple(along(block, (SEGMENT, DP), -step) for step in STEPS[1:])
-    return mine + tuple(to_partner(v) for v in mine)
-
-
-def origin(place, i, j, theirs):
-    segment, core, depth = place[0], place[1] % 2, place[2]
-    chip = place[1] // 2
+    two = jax.ShapeDtypeStruct((2, OQ, WIDE), BF)
+    block, half0, half1 = small(
+        stack_kernel, (four, two, two), own, *[along(own, (CHIP, SEGMENT), j) for j in turns]
+    )
+    rings = (SEGMENT, DP)
+    behind0, ahead1 = along(half0, rings, 1), along(half1, rings, -1)
+    behind1, ahead0 = along(half1, rings, 1), along(half0, rings, -1)
+    far0, far1 = along(behind0, rings, 1), along(ahead1, rings, -1)
+    mine = (block, behind0, behind1, ahead0, ahead1, far0, far1)
+    theirs = [to_partner(v) for v in mine[:5]]
+    written, token = write_early(place, ((0, 0), (0, 1)), (block, theirs[0]))
+    far0, token = lax.optimization_barrier((far0, token))
+    theirs.append(to_partner(far0))
+    written, token = write_early(place, ((1, 0), (2, 0), (3, 0), (4, 0)), mine[1:5], written, token)
+    far1, token = lax.optimization_barrier((far1, token))
+    theirs.append(to_partner(far1))
+    return mine[:5] + (far0, far1), theirs, (*written, token)
+
+
+def origin(place, part, j, theirs):
+    segment, chip, core, depth = place[0], place[1] // 2, place[1] % 2, place[2]
+    step, first, _ = PARTS[part]
     kind = 1 - core if theirs else core
     group = jnp.where(
-        kind == 0, lax.rem(chip - j + 4, 4), 4 + lax.rem(depth + STEPS[i] + 4, 4)
-    )
-    row = lax.rem(segment + jnp.where(kind == 0, STEPS[i], -j) + 4, 4)
+        kind == 0, lax.rem(chip - (first + j) + 4, 4), 4 + lax.rem(depth + step + 4, 4)
+    )
+    row = lax.rem(segment + jnp.where(kind == 0, step, -(first + j)) + 4, 4)
     return group, row
 
 
-def write_out(place, blocks, steps, merging, decoder, stage, sems):
-    def pieces(k, j):
-        group, row = origin(place, steps[k // 2], j, k % 2)
-        slot = stage.at[4 * k + j]
-        sem = sems.at[4 * k + j]
+def write_out(place, which, refs, merging, decoder, stage, sems):
+    chunks = []
+    for (part, theirs), ref in zip(which, refs):
+        for j in range(PARTS[part][2]):
+            stage[len(chunks)] = ref[j].astype(F32)
+            chunks.append((len(chunks), *origin(place, part, j, theirs)))
+
+    def pieces(i, group, row):
+        slot = stage.at[i]
         rows = pl.ds(pl.multiple_of(row * OQ, OQ), OQ)
         left = 9 * JOINT - 4 * WIDE
+        last = 9 * MIX - (2 * WIDE - left)
         yield group < 4, [
-            (slot, merging.at[rows, pl.ds(pl.multiple_of(group * WIDE, WIDE), WIDE)], sem)
+            (slot, merging.at[rows, pl.ds(pl.multiple_of(group * WIDE, WIDE), WIDE)])
         ]
         yield group == 4, [
-            (slot.at[:, :left], merging.at[rows, 4 * WIDE :], sem),
-            (slot.at[:, left:], decoder.at[rows, : WIDE - left], sems.at[4 * len(blocks)]),
+            (slot.at[:, :left], merging.at[rows, 4 * WIDE :]),
+            (slot.at[:, left:], decoder.at[rows, : WIDE - left]),
         ]
-        yield group == 5, [(slot, decoder.at[rows, WIDE - left : 2 * WIDE - left], sem)]
-        last = 9 * MIX - (2 * WIDE - left)
-        yield group == 6, [(slot.at[:, :last], decoder.at[rows, 2 * WIDE - left :], sem)]
+        yield group == 5, [(slot, decoder.at[rows, WIDE - left : 2 * WIDE - left])]
+        yield group == 6, [(slot.at[:, :last], decoder.at[rows, 2 * WIDE - left :])]
 
     def each(do):
-        for k in range(len(blocks)):
-            for j in range(4):
-                for when, copies in pieces(k, j):
-
-                    @pl.when(when)
-                    def _(copies=copies):
-                        for copy in copies:
-                            do(pltpu.make_async_copy(*copy))
-
-    for k, block in enumerate(blocks):
-        stage[4 * k : 4 * k + 4] = block[...].astype(F32)
+        for i, group, row in chunks:
+            for when, copies in pieces(i, group, row):
+
+                @pl.when(when)
+                def _(i=i, copies=copies):
+                    for n, (source, target) in enumerate(copies):
+                        do(pltpu.make_async_copy(source, target, sems.at[2 * i + n]))
+
     each(lambda copy: copy.start())
     return lambda: each(lambda copy: copy.wait())
 
 
-def early_kernel(step, n_old, place, *refs):
-    blocks, (merging, decoder, stage, sems) = refs[n_old : n_old + 2], refs[n_old + 2 :]
-    write_out(place, blocks, (step,), merging, decoder, stage, sems)()
-
-
-def write_early(place, step, mine, theirs, old):
+def early_kernel(which, n_old, place, *refs):
+    n = len(which)
+    n_old += min(n_old, 1)
+    parts, (merging, decoder, token, stage, sems) = refs[n_old : n_old + n], refs[n_old + n :]
+    write_out(place, which, parts, merging, decoder, stage, sems)()
+    token[...] = jnp.zeros(token.shape, F32)
+
+
+def write_early(place, which, parts, old=(), *after):
     smem = pl.BlockSpec(memory_space=pltpu.SMEM)
     vmem = pl.BlockSpec(memory_space=pltpu.VMEM)
     hbm = pl.BlockSpec(memory_space=pltpu.HBM)
-    return pl.pallas_call(
-        functools.partial(early_kernel, step, len(old)),
+    chunks = sum(PARTS[part][2] for part, _ in which)
+    *written, token = pl.pallas_call(
+        functools.partial(early_kernel, which, len(old)),
         out_shape=(
             jax.ShapeDtypeStruct((MIX, 9 * JOINT), F32),
             jax.ShapeDtypeStruct((MIX, 9 * MIX), F32),
+            jax.ShapeDtypeStruct((8, 128), F32),
         ),
-        in_specs=[smem] + [hbm] * len(old) + [vmem] * 2,
-        out_specs=(hbm, hbm),
-        scratch_shapes=[pltpu.VMEM((8, OQ, WIDE), F32), pltpu.SemaphoreType.DMA((9,))],
+        in_specs=[smem] + [hbm] * len(old) + [vmem] * (len(after) + len(parts)),
+        out_specs=(hbm, hbm, vmem),
+        scratch_shapes=[
+            pltpu.VMEM((chunks, OQ, WIDE), F32),
+            pltpu.SemaphoreType.DMA((2 * chunks,)),
+        ],
         input_output_aliases={1 + i: i for i in range(len(old))},
         compiler_params=params(12),
         cost_estimate=pl.CostEstimate(flops=0, bytes_accessed=4_000_000, transcendentals=0),
         name="early",
-    )(place, *old, mine, theirs)
+    )(place, *old, *after, *parts)
+    return written, token
+
+
+LATE = ((1, 1), (2, 1), (3, 1), (4, 1), (5, 0), (6, 0), (5, 1), (6, 1))
 
 
 def finish_kernel(place, *refs):
-    blocks, (lw, pw16, mw_hbm, tw_hbm) = refs[2:10], refs[10:14]
-    patch, lift, head, terrain, meso, merging, decoder = refs[14:21]
-    mw, tw, stage, rest, wide_m, wide_t, ht, gt, sems, late_sems = refs[21:]
+    n = len(PARTS)
+    sides, refs = (refs[3 : 3 + n], refs[3 + n : 3 + 2 * n]), refs[3 + 2 * n :]
+    lw, pw16, mw_hbm, tw_hbm = refs[:4]
+    patch, lift, head, terrain, meso, merging, decoder = refs[4:11]
+    mw, tw, stage, rest, wide_m, wide_t, ht, gt, sems, late_sems = refs[11:]
     reads = [
         pltpu.make_async_copy(mw_hbm, mw, sems.at[0]),
         pltpu.make_async_copy(tw_hbm, tw, sems.at[1]),
     ]
     for copy in reads:
         copy.start()
-    late = [blocks[4 * theirs + i] for i in (1, 2) for theirs in (0, 1)]
-    written = write_out(place, late, (1, 2), merging, decoder, stage, late_sems)
-    for i in range(4):
+    late = [sides[theirs][part] for part, theirs in LATE]
+    written = write_out(place, LATE, late, merging, decoder, stage, late_sems)
+    for part in range(n):
         for theirs in range(2):
-            for j in range(4):
-                group, row = origin(place, i, j, theirs)
+            for j in range(PARTS[part][2]):
+                group, row = origin(place, part, j, theirs)
 
                 @pl.when(group >= 6)
-                def _(i=i, theirs=theirs, j=j, group=group, row=row):
+                def _(part=part, theirs=theirs, j=j, group=group, row=row):
                     rest[
                         pl.ds(pl.multiple_of(row * OQ, OQ), OQ),
                         pl.ds(pl.multiple_of((group - 6) * WIDE, WIDE), WIDE),
-                    ] = blocks[4 * theirs + i][j]
+                    ] = sides[theirs][part][j]
 
     column = 9 * JOINT + 9 * MIX - 6 * WIDE
     writes = []
@@ -549,7 +579,7 @@
     written()
 
 
-def finish(place, old, blocks, lift_copy, patch_turned, meso_weight, terrain_weight):
+def finish(place, old, parts, lift_copy, patch_turned, meso_weight, terrain_weight):
     smem = pl.BlockSpec(memory_space=pltpu.SMEM)
     vmem = pl.BlockSpec(memory_space=pltpu.VMEM)
     hbm = pl.BlockSpec(memory_space=pltpu.HBM)
@@ -564,7 +594,7 @@
             jax.ShapeDtypeStruct((MIX, 9 * JOINT), F32),
             jax.ShapeDtypeStruct((MIX, 9 * MIX), F32),
         ),
-        in_specs=[smem] + [hbm] * 2 + [vmem] * 10 + [hbm] * 2,
+        in_specs=[smem] + [hbm] * 2 + [vmem] * (3 + len(parts)) + [hbm] * 2,
         out_specs=(vmem,) * 3 + (hbm,) * 4,
         scratch_shapes=[
             pltpu.VMEM((MESO, 9 * MESO), BF),
@@ -576,12 +606,12 @@
             pltpu.VMEM((MESO, 9 * LEV), BF),
             pltpu.VMEM((MIX, 256), F32),
             pltpu.SemaphoreType.DMA((8,)),
-            pltpu.SemaphoreType.DMA((17,)),
+            pltpu.SemaphoreType.DMA((32,)),
         ],
         input_output_aliases={1: 5, 2: 6},
         compiler_params=params(36),
         name="finish",
-    )(place, *old, *blocks, lift_copy, patch_turned, meso_weight, terrain_weight)
+    )(place, *old, *parts, lift_copy, patch_turned, meso_weight, terrain_weight)
     return patch.T, terrain, lift, meso, merging, decoder, head
 
 
@@ -634,10 +664,10 @@
         merging_weight,
         decoder_weight,
     )
-    blocks = summed_everywhere(keep, send)
-    old = write_early(place, 0, blocks[0], blocks[4], ())
-    old = write_early(place, 3, blocks[3], blocks[7], old)
-    return finish(place, old, blocks, *small_ones[:2], meso_weight, terrain_weight)
+    mine, theirs, written = summed_everywhere(place, keep, send)
+    return finish(
+        place, written, (*mine, *theirs), *small_ones[:2], meso_weight, terrain_weight
+    )
 
 
 def solution(mesh):

time: 110 us -> 107 us (0.973)
  starting transfers between devices: 40.8 us -> 35.5 us
  waiting for transfers between devices: 26.8 us -> 29.3 us
    ppermute x19 -> x25, starting transfers between devices: 40.8 us -> 35.5 us  [moved(): return lax.ppermute(v, ('dp', 'segment', 'space'), pairs)]
    ppermute x19 -> x25, waiting for transfers between devices: 26.8 us -> 29.3 us  [moved(): return lax.ppermute(v, ('dp', 'segment', 'space'), pairs)]
  transfers between devices with their start and end apart: 19 -> 25, of which waited for: 12 -> 15; matrix products, arithmetic and copies ran while one was open for 0% -> 0% of each run, Pallas kernels for 4% -> 4%
where the time goes in v5:
time: 107 us
  Pallas kernels  36.5 us (34%)
  starting transfers between devices  35.5 us (33%)
  waiting for transfers between devices  29.3 us (27%)
  local copies, waits for them, and re-layouts  4.07 us (4%)
    ppermute x25, starting transfers between devices, moved(): return lax.ppermute(v, ('dp', 'segment', 'space'), pairs)  35.5 us
    ppermute x25, waiting for transfers between devices, moved(): return lax.ppermute(v, ('dp', 'segment', 'space'), pairs)  29.3 us
    pallas_call x1, Pallas kernels, main(): pl.pallas_call(main_kernel, out_shape=(jax.ShapeDtypeStruct((4, OQ, WIDE)...  24.3 us
    pallas_call x1, Pallas kernels, finish(): pl.pallas_call(finish_kernel, out_shape=(jax.ShapeDtypeStruct((8, TERR),...  6.9 us
    pallas_call x2, Pallas kernels, write_early(): pl.pallas_call(functools.partial(early_kernel, which, len(old)), out_shap...  4.25 us
    unnamed x14, local copies, waits for them, and re-layouts  3.96 us
  transfers between devices with their start and end apart: 25, of which 15 were waited for; matrix products, arithmetic and copies ran while one was open for 0% of the time, Pallas kernels for 4%

profile of v5, /device:TPU:1, one launch (start us, length us, event | category | flops | bytes accessed | tf_op | source)
XLA Modules:
  0.0 106.8 jit_solution(7307169504329072790)
XLA Ops:
  2.8 1.5 %collective-permute-start = (bf16[2,4,144,128]{3,2,1,0:T(8,128)(2,1)S(1)}, bf16[2,4,144,128]{3,2,1,0:T(8,128)(2,1)S(1)}, u32[]{:S(2)}, u32[]{:S(2)}) collective-permute-start(bf16[2,4,144,128]{3,2,1,0:T(8,128)(2,1)S(1)} %maximum_maximum_fusion.own), channel_id=1, source_target_pairs={{0,1},{1,0},{2,3},{3,2},{4,5},{5,4},{6,7},{7,6},{8,9},{9,8},{10,11... | collective-permute-start | bytes 884744 | tf_op jit(solution)/shard_map/ppermute | solution.py:368
  6.2 3.3 %collective-permute-start.1 = (bf16[5,144,128]{2,1,0:T(8,128)(2,1)S(1)}, bf16[5,144,128]{2,1,0:T(8,128)(2,1)S(1)}, u32[]{:S(2)}, u32[]{:S(2)}) collective-permute-start(bf16[5,144,128]{2,1,0:T(8,128)(2,1)S(1)} %get-tuple-element.39), channel_id=1, source_target_pairs={{0,2},{1,3},{2,4},{3,5},{4,6},{5,7},{8,10},{9,11},{10,12},{11,13},... | collective-permute-start | bytes 552968 | tf_op jit(solution)/shard_map/ppermute | solution.py:368
  13.1 3.7 %collective-permute-done.2.below = bf16[5,144,128]{2,1,0:T(8,128)(2,1)S(1)} collective-permute-done((bf16[5,144,128]{2,1,0:T(8,128)(2,1)S(1)}, bf16[5,144,128]{2,1,0:T(8,128)(2,1)S(1)}, u32[]{:S(2)}, u32[]{:S(2)}) %collective-permute-start.2) | collective-permute-done | bytes 184352 | tf_op jit(solution)/shard_map/ppermute | solution.py:368
  16.9 24.3 %sections.1 = (bf16[4,64,1280]{2,1,0:T(8,128)(2,1)S(1)}, bf16[4,64,1280]{2,1,0:T(8,128)(2,1)S(1)}) custom-call(s32[3]{0:T(128)S(1)} %pad_add_fusion.place, bf16[5,144,128]{2,1,0:T(8,128)(2,1)S(1)} %collective-permute-done.1.above, bf16[8,144,128]{2,1,0:T(8,128)(2,1)S(1)} %get-tuple-element.40.eight, bf16[5,144,128]{2,1,0:T(8,128)(2,1)S(1)} %collective-permute-done.2.below, ...), custom_call_target="tpu_custom_call" | custom-call | flops 15000000512 | bytes 12000000 | tf_op jit(solution)/shard_map/sections/pallas_call | solution.py:302
  41.2 1.6 %collective-permute-start.3 = (bf16[4,64,1280]{2,1,0:T(8,128)(2,1)S(1)}, bf16[4,64,1280]{2,1,0:T(8,128)(2,1)S(1)}, u32[]{:S(2)}, u32[]{:S(2)}) collective-permute-start(bf16[4,64,1280]{2,1,0:T(8,128)(2,1)S(1)} %get-tuple-element.46), channel_id=1, source_target_pairs={{0,1},{1,0},{2,3},{3,2},{4,5},{5,4},{6,7},{7,6},{8,9},{9,8},{10,11... | collective-permute-start | bytes 1966088 | tf_op jit(solution)/shard_map/ppermute | solution.py:368
  42.8 1.7 %collective-permute-done.3.came = bf16[4,64,1280]{2,1,0:T(8,128)(2,1)S(1)} collective-permute-done((bf16[4,64,1280]{2,1,0:T(8,128)(2,1)S(1)}, bf16[4,64,1280]{2,1,0:T(8,128)(2,1)S(1)}, u32[]{:S(2)}, u32[]{:S(2)}) %collective-permute-start.3) | collective-permute-done | bytes 655392 | tf_op jit(solution)/shard_map/ppermute | solution.py:368
  44.6 1.7 %collective-permute-start.4 = (bf16[64,1280]{1,0:T(8,128)(2,1)S(1)}, bf16[64,1280]{1,0:T(8,128)(2,1)S(1)}, u32[]{:S(2)}, u32[]{:S(2)}) collective-permute-start(bf16[64,1280]{1,0:T(8,128)(2,1)S(1)} %get-tuple-element.48), channel_id=1, source_target_pairs={{0,2},{1,33},{2,4},{3,35},{4,6},{5,37},{6,0},{7,39},{8,10},{9,41},... | collective-permute-start | bytes 491528 | tf_op jit(solution)/shard_map/ppermute | solution.py:368
  46.3 3.3 %collective-permute-start.5 = (bf16[64,1280]{1,0:T(8,128)(2,1)S(1)}, bf16[64,1280]{1,0:T(8,128)(2,1)S(1)}, u32[]{:S(2)}, u32[]{:S(2)}) collective-permute-start(bf16[64,1280]{1,0:T(8,128)(2,1)S(1)} %get-tuple-element.49), channel_id=1, source_target_pairs={{0,4},{1,65},{2,6},{3,67},{4,0},{5,69},{6,2},{7,71},{8,12},{9,73},... | collective-permute-start | bytes 491528 | tf_op jit(solution)/shard_map/ppermute | solution.py:368
  51.5 2.6 %collective-permute-done.5.two = bf16[64,1280]{1,0:T(8,128)(2,1)S(1)} collective-permute-done((bf16[64,1280]{1,0:T(8,128)(2,1)S(1)}, bf16[64,1280]{1,0:T(8,128)(2,1)S(1)}, u32[]{:S(2)}, u32[]{:S(2)}) %collective-permute-start.5) | collective-permute-done | bytes 163872 | tf_op jit(solution)/shard_map/ppermute | solution.py:368
  55.5 3.2 %collective-permute-done.7.other = bf16[64,1280]{1,0:T(8,128)(2,1)S(1)} collective-permute-done((bf16[64,1280]{1,0:T(8,128)(2,1)S(1)}, bf16[64,1280]{1,0:T(8,128)(2,1)S(1)}, u32[]{:S(2)}, u32[]{:S(2)}) %collective-permute-start.7) | collective-permute-done | bytes 163872 | tf_op jit(solution)/shard_map/ppermute | solution.py:368
  60.0 4.2 %collective-permute-done.8.other = bf16[64,1280]{1,0:T(8,128)(2,1)S(1)} collective-permute-done((bf16[64,1280]{1,0:T(8,128)(2,1)S(1)}, bf16[64,1280]{1,0:T(8,128)(2,1)S(1)}, u32[]{:S(2)}, u32[]{:S(2)}) %collective-permute-start.8) | collective-permute-done | bytes 163872 | tf_op jit(solution)/shard_map/ppermute | solution.py:368
  64.3 2.5 %collective-permute-start.11 = (bf16[64,1280]{1,0:T(8,128)(2,1)S(1)}, bf16[64,1280]{1,0:T(8,128)(2,1)S(1)}, u32[]{:S(2)}, u32[]{:S(2)}) collective-permute-start(bf16[64,1280]{1,0:T(8,128)(2,1)S(1)} %pair.3.own), channel_id=1, source_target_pairs={{0,6},{1,25},{2,0},{3,27},{4,2},{5,29},{6,4},{7,31},{8,14},{9,1},{... | collective-permute-start | bytes 491528 | tf_op jit(solution)/shard_map/ppermute | solution.py:368
  67.9 2.9 %collective-permute-done.11.three = bf16[64,1280]{1,0:T(8,128)(2,1)S(1)} collective-permute-done((bf16[64,1280]{1,0:T(8,128)(2,1)S(1)}, bf16[64,1280]{1,0:T(8,128)(2,1)S(1)}, u32[]{:S(2)}, u32[]{:S(2)}) %collective-permute-start.11) | collective-permute-done | bytes 163872 | tf_op jit(solution)/shard_map/ppermute | solution.py:368
  70.8 1.8 %collective-permute-done.10.two = bf16[64,1280]{1,0:T(8,128)(2,1)S(1)} collective-permute-done((bf16[64,1280]{1,0:T(8,128)(2,1)S(1)}, bf16[64,1280]{1,0:T(8,128)(2,1)S(1)}, u32[]{:S(2)}, u32[]{:S(2)}) %collective-permute-start.10) | collective-permute-done | bytes 163872 | tf_op jit(solution)/shard_map/ppermute | solution.py:368
  72.6 1.7 %collective-permute-done.9.one = bf16[64,1280]{1,0:T(8,128)(2,1)S(1)} collective-permute-done((bf16[64,1280]{1,0:T(8,128)(2,1)S(1)}, bf16[64,1280]{1,0:T(8,128)(2,1)S(1)}, u32[]{:S(2)}, u32[]{:S(2)}) %collective-permute-start.9) | collective-permute-done | bytes 163872 | tf_op jit(solution)/shard_map/ppermute | solution.py:368
  74.3 4.6 %collective-permute-start.12 = (bf16[4,64,1280]{2,1,0:T(8,128)(2,1)S(1)}, bf16[4,64,1280]{2,1,0:T(8,128)(2,1)S(1)}, u32[]{:S(2)}, u32[]{:S(2)}) collective-permute-start(bf16[4,64,1280]{2,1,0:T(8,128)(2,1)S(1)} %get-tuple-element.51.refs_0_.refs_3_), channel_id=1, source_target_pairs={{0,1},{1,0},{2,3},{3,2},{4,5},{5,4},{6,7},{7,6},{8,9},{9,8},{10,11... | collective-permute-start | bytes 1966088 | tf_op jit(solution)/shard_map/ppermute | solution.py:368
  78.9 3.0 %collective-permute-start.17 = (bf16[2,64,1280]{2,1,0:T(8,128)(2,1)S(1)}, bf16[2,64,1280]{2,1,0:T(8,128)(2,1)S(1)}, u32[]{:S(2)}, u32[]{:S(2)}) collective-permute-start(bf16[2,64,1280]{2,1,0:T(8,128)(2,1)S(1)} %get-tuple-element.57), channel_id=1, source_target_pairs={{0,24},{1,97},{2,26},{3,99},{4,28},{5,101},{6,30},{7,103},{8,0},{9... | collective-permute-start | bytes 983048 | tf_op jit(solution)/shard_map/ppermute | solution.py:368
  81.9 1.5 %collective-permute-start.16 = (bf16[2,64,1280]{2,1,0:T(8,128)(2,1)S(1)}, bf16[2,64,1280]{2,1,0:T(8,128)(2,1)S(1)}, u32[]{:S(2)}, u32[]{:S(2)}) collective-permute-start(bf16[2,64,1280]{2,1,0:T(8,128)(2,1)S(1)} %get-tuple-element.54), channel_id=1, source_target_pairs={{0,24},{1,97},{2,26},{3,99},{4,28},{5,101},{6,30},{7,103},{8,0},{9... | collective-permute-start | bytes 983048 | tf_op jit(solution)/shard_map/ppermute | solution.py:368
  83.3 3.3 %collective-permute-done.13.refs_3_.refs_4_ = bf16[2,64,1280]{2,1,0:T(8,128)(2,1)S(1)} collective-permute-done((bf16[2,64,1280]{2,1,0:T(8,128)(2,1)S(1)}, bf16[2,64,1280]{2,1,0:T(8,128)(2,1)S(1)}, u32[]{:S(2)}, u32[]{:S(2)}) %collective-permute-start.13) | collective-permute-done | bytes 327712 | tf_op jit(solution)/shard_map/ppermute | solution.py:368
  86.6 2.7 %collective-permute-start.18 = (bf16[2,64,1280]{2,1,0:T(8,128)(2,1)S(1)}, bf16[2,64,1280]{2,1,0:T(8,128)(2,1)S(1)}, u32[]{:S(2)}, u32[]{:S(2)}) collective-permute-start(bf16[2,64,1280]{2,1,0:T(8,128)(2,1)S(1)} %collective-permute-done.17.refs_6_.refs_7_), channel_id=1, source_target_pairs={{0,24},{1,97},{2,26},{3,99},{4,28},{5,101},{6,30},{7,103},{8,0},{9... | collective-permute-start | bytes 983048 | tf_op jit(solution)/shard_map/ppermute | solution.py:368
  89.4 1.7 %collective-permute-start.21 = (bf16[2,64,1280]{2,1,0:T(8,128)(2,1)S(1)}, bf16[2,64,1280]{2,1,0:T(8,128)(2,1)S(1)}, u32[]{:S(2)}, u32[]{:S(2)}) collective-permute-start(bf16[2,64,1280]{2,1,0:T(8,128)(2,1)S(1)} %collective-permute-done.16.refs_5_.refs_6_), channel_id=1, source_target_pairs={{0,1},{1,0},{2,3},{3,2},{4,5},{5,4},{6,7},{7,6},{8,9},{9,8},{10,11... | collective-permute-start | bytes 983048 | tf_op jit(solution)/shard_map/ppermute | solution.py:368
  91.1 2.3 %early.2 = (f32[256,5760]{1,0:T(8,128)}, f32[256,2304]{1,0:T(8,128)}, f32[8,128]{1,0:T(8,128)S(1)}) custom-call(s32[3]{0:T(128)S(1)} %pad_add_fusion.place, bf16[4,64,1280]{2,1,0:T(8,128)(2,1)S(1)} %get-tuple-element.51.refs_0_.refs_3_, bf16[4,64,1280]{2,1,0:T(8,128)(2,1)S(1)} %collective-permute-done.12.refs_1_.refs_10_), custom_call_target="tpu_custom_call" | custom-call | bytes 4000000 | tf_op jit(solution)/shard_map/early/pallas_call | solution.py:486
  95.6 1.9 %early.3 = (f32[256,5760]{1,0:T(8,128)}, f32[256,2304]{1,0:T(8,128)}, f32[8,128]{1,0:T(8,128)S(1)}) custom-call(s32[3]{0:T(128)S(1)} %pad_add_fusion.place, f32[256,5760]{1,0:T(8,128)} %get-tuple-element.52.refs_0_, f32[256,2304]{1,0:T(8,128)} %get-tuple-element.53.refs_1_, ...), custom_call_target="tpu_custom_call", output_to_operand_aliasing={{0}: (1, {}), {1}: (2, {})} | custom-call | bytes 4000000 | tf_op jit(solution)/shard_map/early/pallas_call | solution.py:486
  99.8 6.9 %finish.1 = (f32[8,256]{1,0:T(8,128)}, f32[384,128]{1,0:T(8,128)}, f32[3,256]{1,0:T(4,128)}, f32[256,2304]{1,0:T(8,128)}, f32[384,3456]{1,0:T(8,128)}, /*index=5*/f32[256,5760]{1,0:T(8,128)}, f32[256,2304]{1,0:T(8,128)}) custom-call(s32[3]{0:T(128)S(1)} %pad_add_fusion.place, ...), custom_call_target="tpu_custom_call", output_to_operand_aliasing={{5}: (1, {}), {6}: (2, {})} | custom-call | tf_op jit(solution)/shard_map/finish/pallas_call | solution.py:586
  (61 shorter events, 18.1 us)
Async XLA Ops:
  2.8 2.7 %collective-permute-start = (bf16[2,4,144,128]{3,2,1,0:T(8,128)(2,1)S(1)}, bf16[2,4,144,128]{3,2,1,0:T(8,128)(2,1)S(1)}, u32[]{:S(2)}, u32[]{:S(2)}) collective-permute-start(bf16[2,4,144,128]{3,2,1,0:T(8,128)(2,1)S(1)} %maximum_maximum_fusion.own), channel_id=1, source_target_pairs={{0,1},{1,0},{2,3},{3,2},{4,5},{5,4},{6,7},{7,6},{8,9},{9,8},{10,11... | collective-permute-start | bytes 884744 | tf_op jit(solution)/shard_map/ppermute | solution.py:368
  6.2 7.0 %collective-permute-start.1 = (bf16[5,144,128]{2,1,0:T(8,128)(2,1)S(1)}, bf16[5,144,128]{2,1,0:T(8,128)(2,1)S(1)}, u32[]{:S(2)}, u32[]{:S(2)}) collective-permute-start(bf16[5,144,128]{2,1,0:T(8,128)(2,1)S(1)} %get-tuple-element.39), channel_id=1, source_target_pairs={{0,2},{1,3},{2,4},{3,5},{4,6},{5,7},{8,10},{9,11},{10,12},{11,13},... | collective-permute-start | bytes 552968 | tf_op jit(solution)/shard_map/ppermute | solution.py:368
  9.5 7.4 %collective-permute-start.2 = (bf16[5,144,128]{2,1,0:T(8,128)(2,1)S(1)}, bf16[5,144,128]{2,1,0:T(8,128)(2,1)S(1)}, u32[]{:S(2)}, u32[]{:S(2)}) collective-permute-start(bf16[5,144,128]{2,1,0:T(8,128)(2,1)S(1)} %get-tuple-element.41), channel_id=1, source_target_pairs={{2,0},{3,1},{4,2},{5,3},{6,4},{7,5},{10,8},{11,9},{12,10},{13,11},... | collective-permute-start | bytes 552968 | tf_op jit(solution)/shard_map/ppermute | solution.py:368
  41.2 3.3 %collective-permute-start.3 = (bf16[4,64,1280]{2,1,0:T(8,128)(2,1)S(1)}, bf16[4,64,1280]{2,1,0:T(8,128)(2,1)S(1)}, u32[]{:S(2)}, u32[]{:S(2)}) collective-permute-start(bf16[4,64,1280]{2,1,0:T(8,128)(2,1)S(1)} %get-tuple-element.46), channel_id=1, source_target_pairs={{0,1},{1,0},{2,3},{3,2},{4,5},{5,4},{6,7},{7,6},{8,9},{9,8},{10,11... | collective-permute-start | bytes 1966088 | tf_op jit(solution)/shard_map/ppermute | solution.py:368
  44.6 6.8 %collective-permute-start.4 = (bf16[64,1280]{1,0:T(8,128)(2,1)S(1)}, bf16[64,1280]{1,0:T(8,128)(2,1)S(1)}, u32[]{:S(2)}, u32[]{:S(2)}) collective-permute-start(bf16[64,1280]{1,0:T(8,128)(2,1)S(1)} %get-tuple-element.48), channel_id=1, source_target_pairs={{0,2},{1,33},{2,4},{3,35},{4,6},{5,37},{6,0},{7,39},{8,10},{9,41},... | collective-permute-start | bytes 491528 | tf_op jit(solution)/shard_map/ppermute | solution.py:368
  46.3 7.7 %collective-permute-start.5 = (bf16[64,1280]{1,0:T(8,128)(2,1)S(1)}, bf16[64,1280]{1,0:T(8,128)(2,1)S(1)}, u32[]{:S(2)}, u32[]{:S(2)}) collective-permute-start(bf16[64,1280]{1,0:T(8,128)(2,1)S(1)} %get-tuple-element.49), channel_id=1, source_target_pairs={{0,4},{1,65},{2,6},{3,67},{4,0},{5,69},{6,2},{7,71},{8,12},{9,73},... | collective-permute-start | bytes 491528 | tf_op jit(solution)/shard_map/ppermute | solution.py:368
  49.6 4.5 %collective-permute-start.6 = (bf16[64,1280]{1,0:T(8,128)(2,1)S(1)}, bf16[64,1280]{1,0:T(8,128)(2,1)S(1)}, u32[]{:S(2)}, u32[]{:S(2)}) collective-permute-start(bf16[64,1280]{1,0:T(8,128)(2,1)S(1)} %get-tuple-element.50), channel_id=1, source_target_pairs={{0,6},{1,97},{2,0},{3,99},{4,2},{5,101},{6,4},{7,103},{8,14},{9,10... | collective-permute-start | bytes 491528 | tf_op jit(solution)/shard_map/ppermute | solution.py:368
  54.2 4.5 %collective-permute-start.7 = (bf16[64,1280]{1,0:T(8,128)(2,1)S(1)}, bf16[64,1280]{1,0:T(8,128)(2,1)S(1)}, u32[]{:S(2)}, u32[]{:S(2)}) collective-permute-start(bf16[64,1280]{1,0:T(8,128)(2,1)S(1)} %total.1.own), channel_id=1, source_target_pairs={{0,32},{1,3},{2,34},{3,1},{4,36},{5,7},{6,38},{7,5},{8,40},{9,11},... | collective-permute-start | bytes 491528 | tf_op jit(solution)/shard_map/ppermute | solution.py:368
  58.8 5.5 %collective-permute-start.8 = (bf16[64,1280]{1,0:T(8,128)(2,1)S(1)}, bf16[64,1280]{1,0:T(8,128)(2,1)S(1)}, u32[]{:S(2)}, u32[]{:S(2)}) collective-permute-start(bf16[64,1280]{1,0:T(8,128)(2,1)S(1)} %pair.2.own), channel_id=1, source_target_pairs={{0,96},{1,7},{2,98},{3,5},{4,100},{5,3},{6,102},{7,1},{8,104},{9,1... | collective-permute-start | bytes 491528 | tf_op jit(solution)/shard_map/ppermute | solution.py:368
  64.3 6.6 %collective-permute-start.11 = (bf16[64,1280]{1,0:T(8,128)(2,1)S(1)}, bf16[64,1280]{1,0:T(8,128)(2,1)S(1)}, u32[]{:S(2)}, u32[]{:S(2)}) collective-permute-start(bf16[64,1280]{1,0:T(8,128)(2,1)S(1)} %pair.3.own), channel_id=1, source_target_pairs={{0,6},{1,25},{2,0},{3,27},{4,2},{5,29},{6,4},{7,31},{8,14},{9,1},{... | collective-permute-start | bytes 491528 | tf_op jit(solution)/shard_map/ppermute | solution.py:368
  66.8 5.8 %collective-permute-start.10 = (bf16[64,1280]{1,0:T(8,128)(2,1)S(1)}, bf16[64,1280]{1,0:T(8,128)(2,1)S(1)}, u32[]{:S(2)}, u32[]{:S(2)}) collective-permute-start(bf16[64,1280]{1,0:T(8,128)(2,1)S(1)} %pair.3.own), channel_id=1, source_target_pairs={{0,4},{1,17},{2,6},{3,19},{4,0},{5,21},{6,2},{7,23},{8,12},{9,25},... | collective-permute-start | bytes 491528 | tf_op jit(solution)/shard_map/ppermute | solution.py:368
  67.3 6.9 %collective-permute-start.9 = (bf16[64,1280]{1,0:T(8,128)(2,1)S(1)}, bf16[64,1280]{1,0:T(8,128)(2,1)S(1)}, u32[]{:S(2)}, u32[]{:S(2)}) collective-permute-start(bf16[64,1280]{1,0:T(8,128)(2,1)S(1)} %pair.3.own), channel_id=1, source_target_pairs={{0,2},{1,9},{2,4},{3,11},{4,6},{5,13},{6,0},{7,15},{8,10},{9,17},{... | collective-permute-start | bytes 491528 | tf_op jit(solution)/shard_map/ppermute | solution.py:368
  74.3 16.7 %collective-permute-start.12 = (bf16[4,64,1280]{2,1,0:T(8,128)(2,1)S(1)}, bf16[4,64,1280]{2,1,0:T(8,128)(2,1)S(1)}, u32[]{:S(2)}, u32[]{:S(2)}) collective-permute-start(bf16[4,64,1280]{2,1,0:T(8,128)(2,1)S(1)} %get-tuple-element.51.refs_0_.refs_3_), channel_id=1, source_target_pairs={{0,1},{1,0},{2,3},{3,2},{4,5},{5,4},{6,7},{7,6},{8,9},{9,8},{10,11... | collective-permute-start | bytes 1966088 | tf_op jit(solution)/shard_map/ppermute | solution.py:368
  78.9 7.7 %collective-permute-start.13 = (bf16[2,64,1280]{2,1,0:T(8,128)(2,1)S(1)}, bf16[2,64,1280]{2,1,0:T(8,128)(2,1)S(1)}, u32[]{:S(2)}, u32[]{:S(2)}) collective-permute-start(bf16[2,64,1280]{2,1,0:T(8,128)(2,1)S(1)} %get-tuple-element.54), channel_id=1, source_target_pairs={{0,8},{1,33},{2,10},{3,35},{4,12},{5,37},{6,14},{7,39},{8,16},{9,4... | collective-permute-start | bytes 983048 | tf_op jit(solution)/shard_map/ppermute | solution.py:368
  78.9 7.7 %collective-permute-start.17 = (bf16[2,64,1280]{2,1,0:T(8,128)(2,1)S(1)}, bf16[2,64,1280]{2,1,0:T(8,128)(2,1)S(1)}, u32[]{:S(2)}, u32[]{:S(2)}) collective-permute-start(bf16[2,64,1280]{2,1,0:T(8,128)(2,1)S(1)} %get-tuple-element.57), channel_id=1, source_target_pairs={{0,24},{1,97},{2,26},{3,99},{4,28},{5,101},{6,30},{7,103},{8,0},{9... | collective-permute-start | bytes 983048 | tf_op jit(solution)/shard_map/ppermute | solution.py:368
  81.9 7.5 %collective-permute-start.16 = (bf16[2,64,1280]{2,1,0:T(8,128)(2,1)S(1)}, bf16[2,64,1280]{2,1,0:T(8,128)(2,1)S(1)}, u32[]{:S(2)}, u32[]{:S(2)}) collective-permute-start(bf16[2,64,1280]{2,1,0:T(8,128)(2,1)S(1)} %get-tuple-element.54), channel_id=1, source_target_pairs={{0,24},{1,97},{2,26},{3,99},{4,28},{5,101},{6,30},{7,103},{8,0},{9... | collective-permute-start | bytes 983048 | tf_op jit(solution)/shard_map/ppermute | solution.py:368
  83.3 10.1 %collective-permute-start.15 = (bf16[2,64,1280]{2,1,0:T(8,128)(2,1)S(1)}, bf16[2,64,1280]{2,1,0:T(8,128)(2,1)S(1)}, u32[]{:S(2)}, u32[]{:S(2)}) collective-permute-start(bf16[2,64,1280]{2,1,0:T(8,128)(2,1)S(1)} %get-tuple-element.57), channel_id=1, source_target_pairs={{0,8},{1,33},{2,10},{3,35},{4,12},{5,37},{6,14},{7,39},{8,16},{9,4... | collective-permute-start | bytes 983048 | tf_op jit(solution)/shard_map/ppermute | solution.py:368
  86.6 7.7 %collective-permute-start.14 = (bf16[2,64,1280]{2,1,0:T(8,128)(2,1)S(1)}, bf16[2,64,1280]{2,1,0:T(8,128)(2,1)S(1)}, u32[]{:S(2)}, u32[]{:S(2)}) collective-permute-start(bf16[2,64,1280]{2,1,0:T(8,128)(2,1)S(1)} %collective-permute-done.13.refs_3_.refs_4_), channel_id=1, source_target_pairs={{0,8},{1,33},{2,10},{3,35},{4,12},{5,37},{6,14},{7,39},{8,16},{9,4... | collective-permute-start | bytes 983048 | tf_op jit(solution)/shard_map/ppermute | solution.py:368
  86.6 10.9 %collective-permute-start.18 = (bf16[2,64,1280]{2,1,0:T(8,128)(2,1)S(1)}, bf16[2,64,1280]{2,1,0:T(8,128)(2,1)S(1)}, u32[]{:S(2)}, u32[]{:S(2)}) collective-permute-start(bf16[2,64,1280]{2,1,0:T(8,128)(2,1)S(1)} %collective-permute-done.17.refs_6_.refs_7_), channel_id=1, source_target_pairs={{0,24},{1,97},{2,26},{3,99},{4,28},{5,101},{6,30},{7,103},{8,0},{9... | collective-permute-start | bytes 983048 | tf_op jit(solution)/shard_map/ppermute | solution.py:368
  89.4 8.6 %collective-permute-start.21 = (bf16[2,64,1280]{2,1,0:T(8,128)(2,1)S(1)}, bf16[2,64,1280]{2,1,0:T(8,128)(2,1)S(1)}, u32[]{:S(2)}, u32[]{:S(2)}) collective-permute-start(bf16[2,64,1280]{2,1,0:T(8,128)(2,1)S(1)} %collective-permute-done.16.refs_5_.refs_6_), channel_id=1, source_target_pairs={{0,1},{1,0},{2,3},{3,2},{4,5},{5,4},{6,7},{7,6},{8,9},{9,8},{10,11... | collective-permute-start | bytes 983048 | tf_op jit(solution)/shard_map/ppermute | solution.py:368
  91.1 7.1 %collective-permute-start.19 = (bf16[2,64,1280]{2,1,0:T(8,128)(2,1)S(1)}, bf16[2,64,1280]{2,1,0:T(8,128)(2,1)S(1)}, u32[]{:S(2)}, u32[]{:S(2)}) collective-permute-start(bf16[2,64,1280]{2,1,0:T(8,128)(2,1)S(1)} %collective-permute-done.13.refs_3_.refs_4_), channel_id=1, source_target_pairs={{0,1},{1,0},{2,3},{3,2},{4,5},{5,4},{6,7},{7,6},{8,9},{9,8},{10,11... | collective-permute-start | bytes 983048 | tf_op jit(solution)/shard_map/ppermute | solution.py:368
  93.4 4.7 %collective-permute-start.22 = (bf16[2,64,1280]{2,1,0:T(8,128)(2,1)S(1)}, bf16[2,64,1280]{2,1,0:T(8,128)(2,1)S(1)}, u32[]{:S(2)}, u32[]{:S(2)}) collective-permute-start(bf16[2,64,1280]{2,1,0:T(8,128)(2,1)S(1)} %collective-permute-done.17.refs_6_.refs_7_), channel_id=1, source_target_pairs={{0,1},{1,0},{2,3},{3,2},{4,5},{5,4},{6,7},{7,6},{8,9},{9,8},{10,11... | collective-permute-start | bytes 983048 | tf_op jit(solution)/shard_map/ppermute | solution.py:368
  94.3 3.9 %collective-permute-start.20 = (bf16[2,64,1280]{2,1,0:T(8,128)(2,1)S(1)}, bf16[2,64,1280]{2,1,0:T(8,128)(2,1)S(1)}, u32[]{:S(2)}, u32[]{:S(2)}) collective-permute-start(bf16[2,64,1280]{2,1,0:T(8,128)(2,1)S(1)} %collective-permute-done.15.refs_4_.refs_5_), channel_id=1, source_target_pairs={{0,1},{1,0},{2,3},{3,2},{4,5},{5,4},{6,7},{7,6},{8,9},{9,8},{10,11... | collective-permute-start | bytes 983048 | tf_op jit(solution)/shard_map/ppermute | solution.py:368
  97.5 1.8 %collective-permute-start.24 = (bf16[2,64,1280]{2,1,0:T(8,128)(2,1)S(1)}, bf16[2,64,1280]{2,1,0:T(8,128)(2,1)S(1)}, u32[]{:S(2)}, u32[]{:S(2)}) collective-permute-start(bf16[2,64,1280]{2,1,0:T(8,128)(2,1)S(1)} %collective-permute-done.18.refs_9_), channel_id=1, source_target_pairs={{0,1},{1,0},{2,3},{3,2},{4,5},{5,4},{6,7},{7,6},{8,9},{9,8},{10,11... | collective-permute-start | bytes 983048 | tf_op jit(solution)/shard_map/ppermute | solution.py:368
  (7 other events, 13.1 us)

commit v6 on v5

--- a/solution.py
+++ b/solution.py
@@ -121,7 +121,7 @@
     copies = [
         pltpu.make_async_copy(u, v, sems.at[i]) for i, (u, v) in enumerate(zip(weights_hbm, weights))
     ]
-    for copy in copies:
+    for copy in copies[:2]:
         copy.start()
     segment, depth = place[0], place[2]
     chip, core = place[1] // 2, place[1] % 2
@@ -159,6 +159,8 @@
             mw[:, tap * MESO : (tap + 1) * MESO], lw[...]
         ).astype(BF)
     copies[1].wait()
+    for copy in copies[2:]:
+        copy.start()
     wt[...] = jnp.concatenate(
         [dot_nt(tw[:, tap * TERR : (tap + 1) * TERR], pw16[...]).astype(BF) for tap in range(9)], axis=1
     )
@@ -412,16 +414,21 @@
     rings = (SEGMENT, DP)
     behind0, ahead1 = along(half0, rings, 1), along(half1, rings, -1)
     behind1, ahead0 = along(half1, rings, 1), along(half0, rings, -1)
+    mine = [block, behind0, behind1, ahead0, ahead1]
+    theirs = [to_partner(v) for v in mine]
+    written, token = write_early(place, ((0, 0), (0, 1)), (block, theirs[0]))
+    behind0, token = lax.optimization_barrier((behind0, token))
     far0, far1 = along(behind0, rings, 1), along(ahead1, rings, -1)
-    mine = (block, behind0, behind1, ahead0, ahead1, far0, far1)
-    theirs = [to_partner(v) for v in mine[:5]]
-    written, token = write_early(place, ((0, 0), (0, 1)), (block, theirs[0]))
+    written, token = write_early(
+        place, ((1, 0), (2, 0), (3, 0), (4, 0)), mine[1:], written, token
+    )
     far0, token = lax.optimization_barrier((far0, token))
-    theirs.append(to_partner(far0))
-    written, token = write_early(place, ((1, 0), (2, 0), (3, 0), (4, 0)), mine[1:5], written, token)
-    far1, token = lax.optimization_barrier((far1, token))
-    theirs.append(to_partner(far1))
-    return mine[:5] + (far0, far1), theirs, (*written, token)
+    written, token = write_early(
+        place, ((1, 1), (2, 1), (3, 1), (4, 1)), theirs[1:], written, token
+    )
+    mine += [far0, far1]
+    theirs += [to_partner(far0), to_partner(far1)]
+    return mine, theirs, (*written, token)
 
 
 def origin(place, part, j, theirs):
@@ -504,7 +511,7 @@
     return written, token
 
 
-LATE = ((1, 1), (2, 1), (3, 1), (4, 1), (5, 0), (6, 0), (5, 1), (6, 1))
+LATE = ((5, 0), (6, 0), (5, 1), (6, 1))
 
 
 def finish_kernel(place, *refs):
@@ -599,14 +606,14 @@
         scratch_shapes=[
             pltpu.VMEM((MESO, 9 * MESO), BF),
             pltpu.VMEM((TERR, 9 * TERR), BF),
-            pltpu.VMEM((16, OQ, WIDE), F32),
+            pltpu.VMEM((8, OQ, WIDE), F32),
             pltpu.VMEM((MIX, 2 * WIDE), BF),
             pltpu.VMEM((MESO, 9 * MESO), F32),
             pltpu.VMEM((TERR, 9 * TERR), F32),
             pltpu.VMEM((MESO, 9 * LEV), BF),
             pltpu.VMEM((MIX, 256), F32),
             pltpu.SemaphoreType.DMA((8,)),
-            pltpu.SemaphoreType.DMA((32,)),
+            pltpu.SemaphoreType.DMA((16,)),
         ],
         input_output_aliases={1: 5, 2: 6},
         compiler_params=params(36),

time: 107 us -> 111 us (1.037)
  Pallas kernels: 36.5 us -> 38.5 us
  starting transfers between devices: 35.5 us -> 37.2 us
    pallas_call x2 -> x3, Pallas kernels: 4.25 us -> 6.58 us  [write_early(): pl.pallas_call(functools.partial(early_kernel, which, len(old)), out_shap...]
    ppermute x25, starting transfers between devices: 35.5 us -> 37.2 us  [moved(): return lax.ppermute(v, ('dp', 'segment', 'space'), pairs)]
  transfers between devices with their start and end apart: 25 -> 25, of which waited for: 15 -> 13; matrix products, arithmetic and copies ran while one was open for 0% -> 0% of each run, Pallas kernels for 4% -> 6%
where the time goes in v6:
time: 111 us
  Pallas kernels  38.5 us (35%)
  starting transfers between devices  37.2 us (34%)
  waiting for transfers between devices  28.7 us (26%)
  local copies, waits for them, and re-layouts  4.69 us (4%)
    ppermute x25, starting transfers between devices, moved(): return lax.ppermute(v, ('dp', 'segment', 'space'), pairs)  37.2 us
    ppermute x25, waiting for transfers between devices, moved(): return lax.ppermute(v, ('dp', 'segment', 'space'), pairs)  28.7 us
    pallas_call x1, Pallas kernels, main(): pl.pallas_call(main_kernel, out_shape=(jax.ShapeDtypeStruct((4, OQ, WIDE)...  24.3 us
    pallas_call x3, Pallas kernels, write_early(): pl.pallas_call(functools.partial(early_kernel, which, len(old)), out_shap...  6.58 us
    pallas_call x1, Pallas kernels, finish(): pl.pallas_call(finish_kernel, out_shape=(jax.ShapeDtypeStruct((8, TERR),...  6.55 us
    unnamed x14, local copies, waits for them, and re-layouts  4.58 us
  transfers between devices with their start and end apart: 25, of which 13 were waited for; matrix products, arithmetic and copies ran while one was open for 0% of the time, Pallas kernels for 6%

profile of v6, /device:TPU:1, one launch (start us, length us, event | category | flops | bytes accessed | tf_op | source)
XLA Modules:
  0.0 110.5 jit_solution(1120675070321126724)
XLA Ops:
  6.2 3.3 %collective-permute-start.1 = (bf16[5,144,128]{2,1,0:T(8,128)(2,1)S(1)}, bf16[5,144,128]{2,1,0:T(8,128)(2,1)S(1)}, u32[]{:S(2)}, u32[]{:S(2)}) collective-permute-start(bf16[5,144,128]{2,1,0:T(8,128)(2,1)S(1)} %get-tuple-element.42), channel_id=1, source_target_pairs={{0,2},{1,3},{2,4},{3,5},{4,6},{5,7},{8,10},{9,11},{10,12},{11,13},... | collective-permute-start | bytes 552968 | tf_op jit(solution)/shard_map/ppermute | solution.py:370
  13.1 3.7 %collective-permute-done.2.below = bf16[5,144,128]{2,1,0:T(8,128)(2,1)S(1)} collective-permute-done((bf16[5,144,128]{2,1,0:T(8,128)(2,1)S(1)}, bf16[5,144,128]{2,1,0:T(8,128)(2,1)S(1)}, u32[]{:S(2)}, u32[]{:S(2)}) %collective-permute-start.2) | collective-permute-done | bytes 184352 | tf_op jit(solution)/shard_map/ppermute | solution.py:370
  16.9 24.3 %sections.1 = (bf16[4,64,1280]{2,1,0:T(8,128)(2,1)S(1)}, bf16[4,64,1280]{2,1,0:T(8,128)(2,1)S(1)}) custom-call(s32[3]{0:T(128)S(1)} %pad_add_fusion.place, bf16[5,144,128]{2,1,0:T(8,128)(2,1)S(1)} %collective-permute-done.1.above, bf16[8,144,128]{2,1,0:T(8,128)(2,1)S(1)} %get-tuple-element.43.eight, bf16[5,144,128]{2,1,0:T(8,128)(2,1)S(1)} %collective-permute-done.2.below, ...), custom_call_target="tpu_custom_call" | custom-call | flops 15000000512 | bytes 12000000 | tf_op jit(solution)/shard_map/sections/pallas_call | solution.py:304
  41.2 1.6 %collective-permute-start.3 = (bf16[4,64,1280]{2,1,0:T(8,128)(2,1)S(1)}, bf16[4,64,1280]{2,1,0:T(8,128)(2,1)S(1)}, u32[]{:S(2)}, u32[]{:S(2)}) collective-permute-start(bf16[4,64,1280]{2,1,0:T(8,128)(2,1)S(1)} %get-tuple-element.49), channel_id=1, source_target_pairs={{0,1},{1,0},{2,3},{3,2},{4,5},{5,4},{6,7},{7,6},{8,9},{9,8},{10,11... | collective-permute-start | bytes 1966088 | tf_op jit(solution)/shard_map/ppermute | solution.py:370
  42.8 1.7 %collective-permute-done.3.came = bf16[4,64,1280]{2,1,0:T(8,128)(2,1)S(1)} collective-permute-done((bf16[4,64,1280]{2,1,0:T(8,128)(2,1)S(1)}, bf16[4,64,1280]{2,1,0:T(8,128)(2,1)S(1)}, u32[]{:S(2)}, u32[]{:S(2)}) %collective-permute-start.3) | collective-permute-done | bytes 655392 | tf_op jit(solution)/shard_map/ppermute | solution.py:370
  44.6 1.7 %collective-permute-start.4 = (bf16[64,1280]{1,0:T(8,128)(2,1)S(1)}, bf16[64,1280]{1,0:T(8,128)(2,1)S(1)}, u32[]{:S(2)}, u32[]{:S(2)}) collective-permute-start(bf16[64,1280]{1,0:T(8,128)(2,1)S(1)} %get-tuple-element.51), channel_id=1, source_target_pairs={{0,2},{1,33},{2,4},{3,35},{4,6},{5,37},{6,0},{7,39},{8,10},{9,41},... | collective-permute-start | bytes 491528 | tf_op jit(solution)/shard_map/ppermute | solution.py:370
  46.3 3.3 %collective-permute-start.5 = (bf16[64,1280]{1,0:T(8,128)(2,1)S(1)}, bf16[64,1280]{1,0:T(8,128)(2,1)S(1)}, u32[]{:S(2)}, u32[]{:S(2)}) collective-permute-start(bf16[64,1280]{1,0:T(8,128)(2,1)S(1)} %get-tuple-element.52), channel_id=1, source_target_pairs={{0,4},{1,65},{2,6},{3,67},{4,0},{5,69},{6,2},{7,71},{8,12},{9,73},... | collective-permute-start | bytes 491528 | tf_op jit(solution)/shard_map/ppermute | solution.py:370
  51.5 2.6 %collective-permute-done.5.two = bf16[64,1280]{1,0:T(8,128)(2,1)S(1)} collective-permute-done((bf16[64,1280]{1,0:T(8,128)(2,1)S(1)}, bf16[64,1280]{1,0:T(8,128)(2,1)S(1)}, u32[]{:S(2)}, u32[]{:S(2)}) %collective-permute-start.5) | collective-permute-done | bytes 163872 | tf_op jit(solution)/shard_map/ppermute | solution.py:370
  55.5 3.2 %collective-permute-done.7.other = bf16[64,1280]{1,0:T(8,128)(2,1)S(1)} collective-permute-done((bf16[64,1280]{1,0:T(8,128)(2,1)S(1)}, bf16[64,1280]{1,0:T(8,128)(2,1)S(1)}, u32[]{:S(2)}, u32[]{:S(2)}) %collective-permute-start.7) | collective-permute-done | bytes 163872 | tf_op jit(solution)/shard_map/ppermute | solution.py:370
  60.0 4.2 %collective-permute-done.8.other = bf16[64,1280]{1,0:T(8,128)(2,1)S(1)} collective-permute-done((bf16[64,1280]{1,0:T(8,128)(2,1)S(1)}, bf16[64,1280]{1,0:T(8,128)(2,1)S(1)}, u32[]{:S(2)}, u32[]{:S(2)}) %collective-permute-start.8) | collective-permute-done | bytes 163872 | tf_op jit(solution)/shard_map/ppermute | solution.py:370
  64.3 2.5 %collective-permute-start.11 = (bf16[64,1280]{1,0:T(8,128)(2,1)S(1)}, bf16[64,1280]{1,0:T(8,128)(2,1)S(1)}, u32[]{:S(2)}, u32[]{:S(2)}) collective-permute-start(bf16[64,1280]{1,0:T(8,128)(2,1)S(1)} %pair.3.own), channel_id=1, source_target_pairs={{0,6},{1,25},{2,0},{3,27},{4,2},{5,29},{6,4},{7,31},{8,14},{9,1},{... | collective-permute-start | bytes 491528 | tf_op jit(solution)/shard_map/ppermute | solution.py:370
  67.9 2.9 %collective-permute-done.11.three = bf16[64,1280]{1,0:T(8,128)(2,1)S(1)} collective-permute-done((bf16[64,1280]{1,0:T(8,128)(2,1)S(1)}, bf16[64,1280]{1,0:T(8,128)(2,1)S(1)}, u32[]{:S(2)}, u32[]{:S(2)}) %collective-permute-start.11) | collective-permute-done | bytes 163872 | tf_op jit(solution)/shard_map/ppermute | solution.py:370
  70.8 1.8 %collective-permute-done.10.two = bf16[64,1280]{1,0:T(8,128)(2,1)S(1)} collective-permute-done((bf16[64,1280]{1,0:T(8,128)(2,1)S(1)}, bf16[64,1280]{1,0:T(8,128)(2,1)S(1)}, u32[]{:S(2)}, u32[]{:S(2)}) %collective-permute-start.10) | collective-permute-done | bytes 163872 | tf_op jit(solution)/shard_map/ppermute | solution.py:370
  72.6 1.7 %collective-permute-done.9.one = bf16[64,1280]{1,0:T(8,128)(2,1)S(1)} collective-permute-done((bf16[64,1280]{1,0:T(8,128)(2,1)S(1)}, bf16[64,1280]{1,0:T(8,128)(2,1)S(1)}, u32[]{:S(2)}, u32[]{:S(2)}) %collective-permute-start.9) | collective-permute-done | bytes 163872 | tf_op jit(solution)/shard_map/ppermute | solution.py:370
  74.3 4.6 %collective-permute-start.12 = (bf16[4,64,1280]{2,1,0:T(8,128)(2,1)S(1)}, bf16[4,64,1280]{2,1,0:T(8,128)(2,1)S(1)}, u32[]{:S(2)}, u32[]{:S(2)}) collective-permute-start(bf16[4,64,1280]{2,1,0:T(8,128)(2,1)S(1)} %get-tuple-element.54.refs_0_.refs_3_), channel_id=1, source_target_pairs={{0,1},{1,0},{2,3},{3,2},{4,5},{5,4},{6,7},{7,6},{8,9},{9,8},{10,11... | collective-permute-start | bytes 1966088 | tf_op jit(solution)/shard_map/ppermute | solution.py:370
  78.9 3.0 %collective-permute-start.16 = (bf16[2,64,1280]{2,1,0:T(8,128)(2,1)S(1)}, bf16[2,64,1280]{2,1,0:T(8,128)(2,1)S(1)}, u32[]{:S(2)}, u32[]{:S(2)}) collective-permute-start(bf16[2,64,1280]{2,1,0:T(8,128)(2,1)S(1)} %get-tuple-element.60), channel_id=1, source_target_pairs={{0,24},{1,97},{2,26},{3,99},{4,28},{5,101},{6,30},{7,103},{8,0},{9... | collective-permute-start | bytes 983048 | tf_op jit(solution)/shard_map/ppermute | solution.py:370
  81.9 2.7 %collective-permute-start.15 = (bf16[2,64,1280]{2,1,0:T(8,128)(2,1)S(1)}, bf16[2,64,1280]{2,1,0:T(8,128)(2,1)S(1)}, u32[]{:S(2)}, u32[]{:S(2)}) collective-permute-start(bf16[2,64,1280]{2,1,0:T(8,128)(2,1)S(1)} %get-tuple-element.57), channel_id=1, source_target_pairs={{0,24},{1,97},{2,26},{3,99},{4,28},{5,101},{6,30},{7,103},{8,0},{9... | collective-permute-start | bytes 983048 | tf_op jit(solution)/shard_map/ppermute | solution.py:370
  85.9 3.4 %collective-permute-start.22 = (bf16[2,64,1280]{2,1,0:T(8,128)(2,1)S(1)}, bf16[2,64,1280]{2,1,0:T(8,128)(2,1)S(1)}, u32[]{:S(2)}, u32[]{:S(2)}) collective-permute-start(bf16[2,64,1280]{2,1,0:T(8,128)(2,1)S(1)} %collective-permute-done.16.refs_6_.refs_7_), channel_id=1, source_target_pairs={{0,24},{1,97},{2,26},{3,99},{4,28},{5,101},{6,30},{7,103},{8,0},{9... | collective-permute-start | bytes 983048 | tf_op jit(solution)/shard_map/ppermute | solution.py:370
  89.3 2.3 %early.3 = (f32[256,5760]{1,0:T(8,128)}, f32[256,2304]{1,0:T(8,128)}, f32[8,128]{1,0:T(8,128)S(1)}) custom-call(s32[3]{0:T(128)S(1)} %pad_add_fusion.place, bf16[4,64,1280]{2,1,0:T(8,128)(2,1)S(1)} %get-tuple-element.54.refs_0_.refs_3_, bf16[4,64,1280]{2,1,0:T(8,128)(2,1)S(1)} %collective-permute-done.12.refs_1_.refs_10_), custom_call_target="tpu_custom_call" | custom-call | bytes 4000000 | tf_op jit(solution)/shard_map/early/pallas_call | solution.py:493
  93.6 1.9 %early.4 = (f32[256,5760]{1,0:T(8,128)}, f32[256,2304]{1,0:T(8,128)}, f32[8,128]{1,0:T(8,128)S(1)}) custom-call(s32[3]{0:T(128)S(1)} %pad_add_fusion.place, f32[256,5760]{1,0:T(8,128)} %get-tuple-element.55.refs_0_, f32[256,2304]{1,0:T(8,128)} %get-tuple-element.56.refs_1_, ...), custom_call_target="tpu_custom_call", output_to_operand_aliasing={{0}: (1, {}), {1}: (2, {})} | custom-call | bytes 4000000 | tf_op jit(solution)/shard_map/early/pallas_call | solution.py:493
  96.0 3.2 %collective-permute-done.17.refs_8_ = bf16[2,64,1280]{2,1,0:T(8,128)(2,1)S(1)} collective-permute-done((bf16[2,64,1280]{2,1,0:T(8,128)(2,1)S(1)}, bf16[2,64,1280]{2,1,0:T(8,128)(2,1)S(1)}, u32[]{:S(2)}, u32[]{:S(2)}) %collective-permute-start.17) | collective-permute-done | bytes 327712 | tf_op jit(solution)/shard_map/ppermute | solution.py:370
  99.2 1.6 %collective-permute-start.24 = (bf16[2,64,1280]{2,1,0:T(8,128)(2,1)S(1)}, bf16[2,64,1280]{2,1,0:T(8,128)(2,1)S(1)}, u32[]{:S(2)}, u32[]{:S(2)}) collective-permute-start(bf16[2,64,1280]{2,1,0:T(8,128)(2,1)S(1)} %collective-permute-done.22.refs_9_), channel_id=1, source_target_pairs={{0,1},{1,0},{2,3},{3,2},{4,5},{5,4},{6,7},{7,6},{8,9},{9,8},{10,11... | collective-permute-start | bytes 983048 | tf_op jit(solution)/shard_map/ppermute | solution.py:370
  100.8 2.3 %early.5 = (f32[256,5760]{1,0:T(8,128)}, f32[256,2304]{1,0:T(8,128)}, f32[8,128]{1,0:T(8,128)S(1)}) custom-call(s32[3]{0:T(128)S(1)} %pad_add_fusion.place, f32[256,5760]{1,0:T(8,128)} %get-tuple-element.61.refs_0_, f32[256,2304]{1,0:T(8,128)} %get-tuple-element.62.refs_1_, ...), custom_call_target="tpu_custom_call", output_to_operand_aliasing={{0}: (1, {}), {1}: (2, {})} | custom-call | bytes 4000000 | tf_op jit(solution)/shard_map/early/pallas_call | solution.py:493
  103.8 6.5 %finish.1 = (f32[8,256]{1,0:T(8,128)}, f32[384,128]{1,0:T(8,128)}, f32[3,256]{1,0:T(4,128)}, f32[256,2304]{1,0:T(8,128)}, f32[384,3456]{1,0:T(8,128)}, /*index=5*/f32[256,5760]{1,0:T(8,128)}, f32[256,2304]{1,0:T(8,128)}) custom-call(s32[3]{0:T(128)S(1)} %pad_add_fusion.place, ...), custom_call_target="tpu_custom_call", output_to_operand_aliasing={{5}: (1, {}), {6}: (2, {})} | custom-call | tf_op jit(solution)/shard_map/finish/pallas_call | solution.py:593
  (62 shorter events, 19.4 us)
Async XLA Ops:
  2.8 2.7 %collective-permute-start = (bf16[2,4,144,128]{3,2,1,0:T(8,128)(2,1)S(1)}, bf16[2,4,144,128]{3,2,1,0:T(8,128)(2,1)S(1)}, u32[]{:S(2)}, u32[]{:S(2)}) collective-permute-start(bf16[2,4,144,128]{3,2,1,0:T(8,128)(2,1)S(1)} %maximum_maximum_fusion.own), channel_id=1, source_target_pairs={{0,1},{1,0},{2,3},{3,2},{4,5},{5,4},{6,7},{7,6},{8,9},{9,8},{10,11... | collective-permute-start | bytes 884744 | tf_op jit(solution)/shard_map/ppermute | solution.py:370
  6.2 7.0 %collective-permute-start.1 = (bf16[5,144,128]{2,1,0:T(8,128)(2,1)S(1)}, bf16[5,144,128]{2,1,0:T(8,128)(2,1)S(1)}, u32[]{:S(2)}, u32[]{:S(2)}) collective-permute-start(bf16[5,144,128]{2,1,0:T(8,128)(2,1)S(1)} %get-tuple-element.42), channel_id=1, source_target_pairs={{0,2},{1,3},{2,4},{3,5},{4,6},{5,7},{8,10},{9,11},{10,12},{11,13},... | collective-permute-start | bytes 552968 | tf_op jit(solution)/shard_map/ppermute | solution.py:370
  9.5 7.4 %collective-permute-start.2 = (bf16[5,144,128]{2,1,0:T(8,128)(2,1)S(1)}, bf16[5,144,128]{2,1,0:T(8,128)(2,1)S(1)}, u32[]{:S(2)}, u32[]{:S(2)}) collective-permute-start(bf16[5,144,128]{2,1,0:T(8,128)(2,1)S(1)} %get-tuple-element.44), channel_id=1, source_target_pairs={{2,0},{3,1},{4,2},{5,3},{6,4},{7,5},{10,8},{11,9},{12,10},{13,11},... | collective-permute-start | bytes 552968 | tf_op jit(solution)/shard_map/ppermute | solution.py:370
  41.2 3.3 %collective-permute-start.3 = (bf16[4,64,1280]{2,1,0:T(8,128)(2,1)S(1)}, bf16[4,64,1280]{2,1,0:T(8,128)(2,1)S(1)}, u32[]{:S(2)}, u32[]{:S(2)}) collective-permute-start(bf16[4,64,1280]{2,1,0:T(8,128)(2,1)S(1)} %get-tuple-element.49), channel_id=1, source_target_pairs={{0,1},{1,0},{2,3},{3,2},{4,5},{5,4},{6,7},{7,6},{8,9},{9,8},{10,11... | collective-permute-start | bytes 1966088 | tf_op jit(solution)/shard_map/ppermute | solution.py:370
  44.6 6.8 %collective-permute-start.4 = (bf16[64,1280]{1,0:T(8,128)(2,1)S(1)}, bf16[64,1280]{1,0:T(8,128)(2,1)S(1)}, u32[]{:S(2)}, u32[]{:S(2)}) collective-permute-start(bf16[64,1280]{1,0:T(8,128)(2,1)S(1)} %get-tuple-element.51), channel_id=1, source_target_pairs={{0,2},{1,33},{2,4},{3,35},{4,6},{5,37},{6,0},{7,39},{8,10},{9,41},... | collective-permute-start | bytes 491528 | tf_op jit(solution)/shard_map/ppermute | solution.py:370
  46.3 7.7 %collective-permute-start.5 = (bf16[64,1280]{1,0:T(8,128)(2,1)S(1)}, bf16[64,1280]{1,0:T(8,128)(2,1)S(1)}, u32[]{:S(2)}, u32[]{:S(2)}) collective-permute-start(bf16[64,1280]{1,0:T(8,128)(2,1)S(1)} %get-tuple-element.52), channel_id=1, source_target_pairs={{0,4},{1,65},{2,6},{3,67},{4,0},{5,69},{6,2},{7,71},{8,12},{9,73},... | collective-permute-start | bytes 491528 | tf_op jit(solution)/shard_map/ppermute | solution.py:370
  49.6 4.5 %collective-permute-start.6 = (bf16[64,1280]{1,0:T(8,128)(2,1)S(1)}, bf16[64,1280]{1,0:T(8,128)(2,1)S(1)}, u32[]{:S(2)}, u32[]{:S(2)}) collective-permute-start(bf16[64,1280]{1,0:T(8,128)(2,1)S(1)} %get-tuple-element.53), channel_id=1, source_target_pairs={{0,6},{1,97},{2,0},{3,99},{4,2},{5,101},{6,4},{7,103},{8,14},{9,10... | collective-permute-start | bytes 491528 | tf_op jit(solution)/shard_map/ppermute | solution.py:370
  54.2 4.5 %collective-permute-start.7 = (bf16[64,1280]{1,0:T(8,128)(2,1)S(1)}, bf16[64,1280]{1,0:T(8,128)(2,1)S(1)}, u32[]{:S(2)}, u32[]{:S(2)}) collective-permute-start(bf16[64,1280]{1,0:T(8,128)(2,1)S(1)} %total.1.own), channel_id=1, source_target_pairs={{0,32},{1,3},{2,34},{3,1},{4,36},{5,7},{6,38},{7,5},{8,40},{9,11},... | collective-permute-start | bytes 491528 | tf_op jit(solution)/shard_map/ppermute | solution.py:370
  58.8 5.5 %collective-permute-start.8 = (bf16[64,1280]{1,0:T(8,128)(2,1)S(1)}, bf16[64,1280]{1,0:T(8,128)(2,1)S(1)}, u32[]{:S(2)}, u32[]{:S(2)}) collective-permute-start(bf16[64,1280]{1,0:T(8,128)(2,1)S(1)} %pair.2.own), channel_id=1, source_target_pairs={{0,96},{1,7},{2,98},{3,5},{4,100},{5,3},{6,102},{7,1},{8,104},{9,1... | collective-permute-start | bytes 491528 | tf_op jit(solution)/shard_map/ppermute | solution.py:370
  64.3 6.6 %collective-permute-start.11 = (bf16[64,1280]{1,0:T(8,128)(2,1)S(1)}, bf16[64,1280]{1,0:T(8,128)(2,1)S(1)}, u32[]{:S(2)}, u32[]{:S(2)}) collective-permute-start(bf16[64,1280]{1,0:T(8,128)(2,1)S(1)} %pair.3.own), channel_id=1, source_target_pairs={{0,6},{1,25},{2,0},{3,27},{4,2},{5,29},{6,4},{7,31},{8,14},{9,1},{... | collective-permute-start | bytes 491528 | tf_op jit(solution)/shard_map/ppermute | solution.py:370
  66.8 5.8 %collective-permute-start.10 = (bf16[64,1280]{1,0:T(8,128)(2,1)S(1)}, bf16[64,1280]{1,0:T(8,128)(2,1)S(1)}, u32[]{:S(2)}, u32[]{:S(2)}) collective-permute-start(bf16[64,1280]{1,0:T(8,128)(2,1)S(1)} %pair.3.own), channel_id=1, source_target_pairs={{0,4},{1,17},{2,6},{3,19},{4,0},{5,21},{6,2},{7,23},{8,12},{9,25},... | collective-permute-start | bytes 491528 | tf_op jit(solution)/shard_map/ppermute | solution.py:370
  67.3 6.9 %collective-permute-start.9 = (bf16[64,1280]{1,0:T(8,128)(2,1)S(1)}, bf16[64,1280]{1,0:T(8,128)(2,1)S(1)}, u32[]{:S(2)}, u32[]{:S(2)}) collective-permute-start(bf16[64,1280]{1,0:T(8,128)(2,1)S(1)} %pair.3.own), channel_id=1, source_target_pairs={{0,2},{1,9},{2,4},{3,11},{4,6},{5,13},{6,0},{7,15},{8,10},{9,17},{... | collective-permute-start | bytes 491528 | tf_op jit(solution)/shard_map/ppermute | solution.py:370
  74.3 15.0 %collective-permute-start.12 = (bf16[4,64,1280]{2,1,0:T(8,128)(2,1)S(1)}, bf16[4,64,1280]{2,1,0:T(8,128)(2,1)S(1)}, u32[]{:S(2)}, u32[]{:S(2)}) collective-permute-start(bf16[4,64,1280]{2,1,0:T(8,128)(2,1)S(1)} %get-tuple-element.54.refs_0_.refs_3_), channel_id=1, source_target_pairs={{0,1},{1,0},{2,3},{3,2},{4,5},{5,4},{6,7},{7,6},{8,9},{9,8},{10,11... | collective-permute-start | bytes 1966088 | tf_op jit(solution)/shard_map/ppermute | solution.py:370
  78.9 7.0 %collective-permute-start.16 = (bf16[2,64,1280]{2,1,0:T(8,128)(2,1)S(1)}, bf16[2,64,1280]{2,1,0:T(8,128)(2,1)S(1)}, u32[]{:S(2)}, u32[]{:S(2)}) collective-permute-start(bf16[2,64,1280]{2,1,0:T(8,128)(2,1)S(1)} %get-tuple-element.60), channel_id=1, source_target_pairs={{0,24},{1,97},{2,26},{3,99},{4,28},{5,101},{6,30},{7,103},{8,0},{9... | collective-permute-start | bytes 983048 | tf_op jit(solution)/shard_map/ppermute | solution.py:370
  81.9 9.8 %collective-permute-start.13 = (bf16[2,64,1280]{2,1,0:T(8,128)(2,1)S(1)}, bf16[2,64,1280]{2,1,0:T(8,128)(2,1)S(1)}, u32[]{:S(2)}, u32[]{:S(2)}) collective-permute-start(bf16[2,64,1280]{2,1,0:T(8,128)(2,1)S(1)} %get-tuple-element.57), channel_id=1, source_target_pairs={{0,8},{1,33},{2,10},{3,35},{4,12},{5,37},{6,14},{7,39},{8,16},{9,4... | collective-permute-start | bytes 983048 | tf_op jit(solution)/shard_map/ppermute | solution.py:370
  81.9 9.9 %collective-permute-start.15 = (bf16[2,64,1280]{2,1,0:T(8,128)(2,1)S(1)}, bf16[2,64,1280]{2,1,0:T(8,128)(2,1)S(1)}, u32[]{:S(2)}, u32[]{:S(2)}) collective-permute-start(bf16[2,64,1280]{2,1,0:T(8,128)(2,1)S(1)} %get-tuple-element.57), channel_id=1, source_target_pairs={{0,24},{1,97},{2,26},{3,99},{4,28},{5,101},{6,30},{7,103},{8,0},{9... | collective-permute-start | bytes 983048 | tf_op jit(solution)/shard_map/ppermute | solution.py:370
  84.5 8.3 %collective-permute-start.14 = (bf16[2,64,1280]{2,1,0:T(8,128)(2,1)S(1)}, bf16[2,64,1280]{2,1,0:T(8,128)(2,1)S(1)}, u32[]{:S(2)}, u32[]{:S(2)}) collective-permute-start(bf16[2,64,1280]{2,1,0:T(8,128)(2,1)S(1)} %get-tuple-element.60), channel_id=1, source_target_pairs={{0,8},{1,33},{2,10},{3,35},{4,12},{5,37},{6,14},{7,39},{8,16},{9,4... | collective-permute-start | bytes 983048 | tf_op jit(solution)/shard_map/ppermute | solution.py:370
  85.9 9.6 %collective-permute-start.22 = (bf16[2,64,1280]{2,1,0:T(8,128)(2,1)S(1)}, bf16[2,64,1280]{2,1,0:T(8,128)(2,1)S(1)}, u32[]{:S(2)}, u32[]{:S(2)}) collective-permute-start(bf16[2,64,1280]{2,1,0:T(8,128)(2,1)S(1)} %collective-permute-done.16.refs_6_.refs_7_), channel_id=1, source_target_pairs={{0,24},{1,97},{2,26},{3,99},{4,28},{5,101},{6,30},{7,103},{8,0},{9... | collective-permute-start | bytes 983048 | tf_op jit(solution)/shard_map/ppermute | solution.py:370
  91.7 7.5 %collective-permute-start.17 = (bf16[2,64,1280]{2,1,0:T(8,128)(2,1)S(1)}, bf16[2,64,1280]{2,1,0:T(8,128)(2,1)S(1)}, u32[]{:S(2)}, u32[]{:S(2)}) collective-permute-start(bf16[2,64,1280]{2,1,0:T(8,128)(2,1)S(1)} %collective-permute-done.13.refs_3_.refs_4_), channel_id=1, source_target_pairs={{0,8},{1,33},{2,10},{3,35},{4,12},{5,37},{6,14},{7,39},{8,16},{9,4... | collective-permute-start | bytes 983048 | tf_op jit(solution)/shard_map/ppermute | solution.py:370
  91.7 9.0 %collective-permute-start.20 = (bf16[2,64,1280]{2,1,0:T(8,128)(2,1)S(1)}, bf16[2,64,1280]{2,1,0:T(8,128)(2,1)S(1)}, u32[]{:S(2)}, u32[]{:S(2)}) collective-permute-start(bf16[2,64,1280]{2,1,0:T(8,128)(2,1)S(1)} %collective-permute-done.15.refs_5_.refs_6_), channel_id=1, source_target_pairs={{0,1},{1,0},{2,3},{3,2},{4,5},{5,4},{6,7},{7,6},{8,9},{9,8},{10,11... | collective-permute-start | bytes 983048 | tf_op jit(solution)/shard_map/ppermute | solution.py:370
  92.6 8.2 %collective-permute-start.18 = (bf16[2,64,1280]{2,1,0:T(8,128)(2,1)S(1)}, bf16[2,64,1280]{2,1,0:T(8,128)(2,1)S(1)}, u32[]{:S(2)}, u32[]{:S(2)}) collective-permute-start(bf16[2,64,1280]{2,1,0:T(8,128)(2,1)S(1)} %collective-permute-done.13.refs_3_.refs_4_), channel_id=1, source_target_pairs={{0,1},{1,0},{2,3},{3,2},{4,5},{5,4},{6,7},{7,6},{8,9},{9,8},{10,11... | collective-permute-start | bytes 983048 | tf_op jit(solution)/shard_map/ppermute | solution.py:370
  92.8 8.0 %collective-permute-start.21 = (bf16[2,64,1280]{2,1,0:T(8,128)(2,1)S(1)}, bf16[2,64,1280]{2,1,0:T(8,128)(2,1)S(1)}, u32[]{:S(2)}, u32[]{:S(2)}) collective-permute-start(bf16[2,64,1280]{2,1,0:T(8,128)(2,1)S(1)} %collective-permute-done.16.refs_6_.refs_7_), channel_id=1, source_target_pairs={{0,1},{1,0},{2,3},{3,2},{4,5},{5,4},{6,7},{7,6},{8,9},{9,8},{10,11... | collective-permute-start | bytes 983048 | tf_op jit(solution)/shard_map/ppermute | solution.py:370
  95.5 5.3 %collective-permute-start.19 = (bf16[2,64,1280]{2,1,0:T(8,128)(2,1)S(1)}, bf16[2,64,1280]{2,1,0:T(8,128)(2,1)S(1)}, u32[]{:S(2)}, u32[]{:S(2)}) collective-permute-start(bf16[2,64,1280]{2,1,0:T(8,128)(2,1)S(1)} %collective-permute-done.14.refs_4_.refs_5_), channel_id=1, source_target_pairs={{0,1},{1,0},{2,3},{3,2},{4,5},{5,4},{6,7},{7,6},{8,9},{9,8},{10,11... | collective-permute-start | bytes 983048 | tf_op jit(solution)/shard_map/ppermute | solution.py:370
  99.2 4.0 %collective-permute-start.24 = (bf16[2,64,1280]{2,1,0:T(8,128)(2,1)S(1)}, bf16[2,64,1280]{2,1,0:T(8,128)(2,1)S(1)}, u32[]{:S(2)}, u32[]{:S(2)}) collective-permute-start(bf16[2,64,1280]{2,1,0:T(8,128)(2,1)S(1)} %collective-permute-done.22.refs_9_), channel_id=1, source_target_pairs={{0,1},{1,0},{2,3},{3,2},{4,5},{5,4},{6,7},{7,6},{8,9},{9,8},{10,11... | collective-permute-start | bytes 983048 | tf_op jit(solution)/shard_map/ppermute | solution.py:370
  (7 other events, 10.8 us)

commit v7 on v5

--- a/solution.py
+++ b/solution.py
@@ -142,8 +142,11 @@
 
     n_in, n_join = ROWS + 2 * HALO, ROWS + 8
 
+    there = {0: (chip > 0).astype(F32), 1: (chip < 3).astype(F32)}
     for r in range(n_in):
         v = slab(r).astype(F32)
+        if not HALO <= r < HALO + ROWS:
+            v = v * there[r // (HALO + ROWS)]
         left, right = neighbours(v)
         for b, u in enumerate((left, v, right)):
             u = u.astype(BF)
@@ -205,7 +208,7 @@
         sigma = logistic(pre)
         cot = jnp.concatenate([slab(row + 3 + r)[LEV:] for r in range(4)], axis=1)
         back = scale * dot(head_turned[...], cot)
-        v = sigma * (1.0 + pre * (1.0 - sigma)) * back
+        v = jnp.where(inside(row - 2, 4), sigma * (1.0 + pre * (1.0 - sigma)) * back, 0.0)
         left, right = neighbours(v)
         for b, u in enumerate((right, v, left)):
             d3[b * MIX : (b + 1) * MIX, cut(row, 4)] = u.astype(BF)
@@ -363,8 +366,7 @@
     for source in range(128):
         at = (source // 32, source // 8 % 4, source // 2 % 4, source % 2)
         to = where(*at)
-        if to is not None:
-            pairs.append((source, to[0] * 32 + to[1] * 8 + to[2] * 2 + to[3]))
+        pairs.append((source, to[0] * 32 + to[1] * 8 + to[2] * 2 + to[3]))
     return lax.ppermute(v, ("dp", "segment", "space"), pairs)
 
 
@@ -418,9 +420,10 @@
     written, token = write_early(place, ((0, 0), (0, 1)), (block, theirs[0]))
     far0, token = lax.optimization_barrier((far0, token))
     theirs.append(to_partner(far0))
-    written, token = write_early(place, ((1, 0), (2, 0), (3, 0), (4, 0)), mine[1:5], written, token)
-    far1, token = lax.optimization_barrier((far1, token))
     theirs.append(to_partner(far1))
+    written, token = write_early(
+        place, ((1, 0), (2, 0), (3, 0), (4, 0)), mine[1:5], written, token
+    )
     return mine[:5] + (far0, far1), theirs, (*written, token)
 
 
@@ -510,15 +513,9 @@
 def finish_kernel(place, *refs):
     n = len(PARTS)
     sides, refs = (refs[3 : 3 + n], refs[3 + n : 3 + 2 * n]), refs[3 + 2 * n :]
-    lw, pw16, mw_hbm, tw_hbm = refs[:4]
+    lw, pw16, mw, tw = refs[:4]
     patch, lift, head, terrain, meso, merging, decoder = refs[4:11]
-    mw, tw, stage, rest, wide_m, wide_t, ht, gt, sems, late_sems = refs[11:]
-    reads = [
-        pltpu.make_async_copy(mw_hbm, mw, sems.at[0]),
-        pltpu.make_async_copy(tw_hbm, tw, sems.at[1]),
-    ]
-    for copy in reads:
-        copy.start()
+    stage, rest, wide_m, wide_t, ht, gt, sems, late_sems = refs[11:]
     late = [sides[theirs][part] for part, theirs in LATE]
     written = write_out(place, LATE, late, merging, decoder, stage, late_sems)
     for part in range(n):
@@ -543,24 +540,19 @@
         ht[at + 64 : at + MQ, :640] = rest[lo : lo + 32, spare : spare + 640]
         ht[at + 64 : at + MQ, 640:] = rest[lo + 32 : lo + OQ, spare : spare + 512]
         gt[lo : lo + OQ, :] = rest[lo : lo + OQ, spare + 640 : spare + 896].astype(F32)
-    for a in range(3):
-        for tap in range(3 * a, 3 * a + 3):
-            wide_m[:, tap * MESO : (tap + 1) * MESO] = dot_nt(
-                ht[:, tap * LEV : (tap + 1) * LEV], lw[...]
-            )
-        part = slice(3 * a * MESO, 3 * (a + 1) * MESO)
-        writes.append(pltpu.make_async_copy(wide_m.at[:, part], meso.at[:, part], sems.at[4 + a]))
-        writes[-1].start()
     g = gt[...]
     for tap in range(9):
-        wide_t[:, tap * TERR : (tap + 1) * TERR] = dot(
-            g[:, tap * SLAB : (tap + 1) * SLAB].astype(BF), pw16[...]
-        )
-    writes.append(pltpu.make_async_copy(wide_t, terrain, sems.at[7]))
-    writes[-1].start()
+        part = slice(tap * MESO, (tap + 1) * MESO)
+        wide_m[:, part] = dot_nt(ht[:, tap * LEV : (tap + 1) * LEV], lw[...])
+        writes.append(pltpu.make_async_copy(wide_m.at[:, part], meso.at[:, part], sems.at[tap]))
+        writes[-1].start()
+    for tap in range(9):
+        part = slice(tap * TERR, (tap + 1) * TERR)
+        wide_t[:, part] = dot(g[:, tap * SLAB : (tap + 1) * SLAB].astype(BF), pw16[...])
+        writes.append(pltpu.make_async_copy(wide_t.at[:, part], terrain.at[:, part], sems.at[9 + tap]))
+        writes[-1].start()
     turned = g.T
     head[...] = turned[9 * SLAB + 8 : 9 * SLAB + 11, :]
-    reads[1].wait()
     patch[...] = sum(
         dot(
             turned[tap * SLAB : (tap + 1) * SLAB, :].astype(BF),
@@ -569,7 +561,6 @@
         for tap in range(9)
     )[:8]
     turned = ht[...].astype(F32).T.astype(BF)
-    reads[0].wait()
     lift[...] = sum(
         dot(turned[tap * LEV : (tap + 1) * LEV, :], mw[:, tap * MESO : (tap + 1) * MESO])
         for tap in range(9)
@@ -594,18 +585,16 @@
             jax.ShapeDtypeStruct((MIX, 9 * JOINT), F32),
             jax.ShapeDtypeStruct((MIX, 9 * MIX), F32),
         ),
-        in_specs=[smem] + [hbm] * 2 + [vmem] * (3 + len(parts)) + [hbm] * 2,
+        in_specs=[smem] + [hbm] * 2 + [vmem] * (5 + len(parts)),
         out_specs=(vmem,) * 3 + (hbm,) * 4,
         scratch_shapes=[
-            pltpu.VMEM((MESO, 9 * MESO), BF),
-            pltpu.VMEM((TERR, 9 * TERR), BF),
             pltpu.VMEM((16, OQ, WIDE), F32),
             pltpu.VMEM((MIX, 2 * WIDE), BF),
             pltpu.VMEM((MESO, 9 * MESO), F32),
             pltpu.VMEM((TERR, 9 * TERR), F32),
             pltpu.VMEM((MESO, 9 * LEV), BF),
             pltpu.VMEM((MIX, 256), F32),
-            pltpu.SemaphoreType.DMA((8,)),
+            pltpu.SemaphoreType.DMA((18,)),
             pltpu.SemaphoreType.DMA((32,)),
         ],
         input_output_aliases={1: 5, 2: 6},
@@ -633,7 +622,7 @@
 
 
 def to_chip(v, by):
-    return moved(v, lambda z, x, y, c: (z, x, y + by, c) if 0 <= y + by < 4 else None)
+    return along(v, (CHIP, CHIP), by)
 
 
 def local(

time: 107 us -> 102 us (0.953)
  waiting for transfers between devices: 29.3 us -> 24.8 us
    ppermute x25, waiting for transfers between devices: 29.3 us -> 24.8 us  [moved(): return lax.ppermute(v, ('dp', 'segment', 'space'), pairs)]
  transfers between devices with their start and end apart: 25 -> 25, of which waited for: 15 -> 13; matrix products, arithmetic and copies ran while one was open for 0% -> 0% of each run, Pallas kernels for 4% -> 4%
where the time goes in v7:
time: 102 us; the launch traced here: 101 us
  Pallas kernels  36 us (35%)
  starting transfers between devices  34.7 us (34%)
  waiting for transfers between devices  24.8 us (24%)
  local copies, waits for them, and re-layouts  4.62 us (5%)
    ppermute x25, starting transfers between devices, moved(): return lax.ppermute(v, ('dp', 'segment', 'space'), pairs)  34.7 us
    ppermute x25, waiting for transfers between devices, moved(): return lax.ppermute(v, ('dp', 'segment', 'space'), pairs)  24.8 us
    pallas_call x1, Pallas kernels, main(): pl.pallas_call(main_kernel, out_shape=(jax.ShapeDtypeStruct((4, OQ, WIDE)...  24.2 us
    pallas_call x1, Pallas kernels, finish(): pl.pallas_call(finish_kernel, out_shape=(jax.ShapeDtypeStruct((8, TERR),...  6.42 us
    unnamed x14, local copies, waits for them, and re-layouts  4.51 us
    pallas_call x2, Pallas kernels, write_early(): pl.pallas_call(functools.partial(early_kernel, which, len(old)), out_shap...  4.25 us
  transfers between devices with their start and end apart: 25, of which 13 were waited for; matrix products, arithmetic and copies ran while one was open for 0% of the time, Pallas kernels for 4%

profile of v7, /device:TPU:1, one launch (start us, length us, event | category | flops | bytes accessed | tf_op | source)
XLA Modules:
  0.0 101.5 jit_solution(725520254085682259)
XLA Ops:
  2.8 1.5 %collective-permute-start = (bf16[2,4,144,128]{3,2,1,0:T(8,128)(2,1)S(1)}, bf16[2,4,144,128]{3,2,1,0:T(8,128)(2,1)S(1)}, u32[]{:S(2)}, u32[]{:S(2)}) collective-permute-start(bf16[2,4,144,128]{3,2,1,0:T(8,128)(2,1)S(1)} %maximum_maximum_fusion.own), channel_id=1, source_target_pairs={{0,1},{1,0},{2,3},{3,2},{4,5},{5,4},{6,7},{7,6},{8,9},{9,8},{10,11... | collective-permute-start | bytes 884744 | tf_op jit(solution)/shard_map/ppermute | solution.py:370
  7.6 1.5 %collective-permute-start.2 = (bf16[5,144,128]{2,1,0:T(8,128)(2,1)S(1)}, bf16[5,144,128]{2,1,0:T(8,128)(2,1)S(1)}, u32[]{:S(2)}, u32[]{:S(2)}) collective-permute-start(bf16[5,144,128]{2,1,0:T(8,128)(2,1)S(1)} %get-tuple-element.39), channel_id=1, source_target_pairs={{0,6},{1,7},{2,0},{3,1},{4,2},{5,3},{6,4},{7,5},{8,14},{9,15},{10,... | collective-permute-start | bytes 552968 | tf_op jit(solution)/shard_map/ppermute | solution.py:370
  11.5 2.1 %collective-permute-done.1.above = bf16[5,144,128]{2,1,0:T(8,128)(2,1)S(1)} collective-permute-done((bf16[5,144,128]{2,1,0:T(8,128)(2,1)S(1)}, bf16[5,144,128]{2,1,0:T(8,128)(2,1)S(1)}, u32[]{:S(2)}, u32[]{:S(2)}) %collective-permute-start.1) | collective-permute-done | bytes 184352 | tf_op jit(solution)/shard_map/ppermute | solution.py:370
  13.6 24.2 %sections.1 = (bf16[4,64,1280]{2,1,0:T(8,128)(2,1)S(1)}, bf16[4,64,1280]{2,1,0:T(8,128)(2,1)S(1)}) custom-call(s32[3]{0:T(128)S(1)} %pad_add_fusion.place, bf16[5,144,128]{2,1,0:T(8,128)(2,1)S(1)} %collective-permute-done.1.above, bf16[8,144,128]{2,1,0:T(8,128)(2,1)S(1)} %get-tuple-element.38.eight, bf16[5,144,128]{2,1,0:T(8,128)(2,1)S(1)} %collective-permute-done.2.below, ...), custom_call_target="tpu_custom_call" | custom-call | flops 15000000512 | bytes 12000000 | tf_op jit(solution)/shard_map/sections/pallas_call | solution.py:305
  39.0 1.7 %collective-permute-done.3.came = bf16[4,64,1280]{2,1,0:T(8,128)(2,1)S(1)} collective-permute-done((bf16[4,64,1280]{2,1,0:T(8,128)(2,1)S(1)}, bf16[4,64,1280]{2,1,0:T(8,128)(2,1)S(1)}, u32[]{:S(2)}, u32[]{:S(2)}) %collective-permute-start.3) | collective-permute-done | bytes 655392 | tf_op jit(solution)/shard_map/ppermute | solution.py:370
  40.8 1.7 %collective-permute-start.4 = (bf16[64,1280]{1,0:T(8,128)(2,1)S(1)}, bf16[64,1280]{1,0:T(8,128)(2,1)S(1)}, u32[]{:S(2)}, u32[]{:S(2)}) collective-permute-start(bf16[64,1280]{1,0:T(8,128)(2,1)S(1)} %get-tuple-element.46), channel_id=1, source_target_pairs={{0,2},{1,33},{2,4},{3,35},{4,6},{5,37},{6,0},{7,39},{8,10},{9,41},... | collective-permute-start | bytes 491528 | tf_op jit(solution)/shard_map/ppermute | solution.py:370
  42.6 3.3 %collective-permute-start.5 = (bf16[64,1280]{1,0:T(8,128)(2,1)S(1)}, bf16[64,1280]{1,0:T(8,128)(2,1)S(1)}, u32[]{:S(2)}, u32[]{:S(2)}) collective-permute-start(bf16[64,1280]{1,0:T(8,128)(2,1)S(1)} %get-tuple-element.47), channel_id=1, source_target_pairs={{0,4},{1,65},{2,6},{3,67},{4,0},{5,69},{6,2},{7,71},{8,12},{9,73},... | collective-permute-start | bytes 491528 | tf_op jit(solution)/shard_map/ppermute | solution.py:370
  47.4 3.0 %collective-permute-done.5.two = bf16[64,1280]{1,0:T(8,128)(2,1)S(1)} collective-permute-done((bf16[64,1280]{1,0:T(8,128)(2,1)S(1)}, bf16[64,1280]{1,0:T(8,128)(2,1)S(1)}, u32[]{:S(2)}, u32[]{:S(2)}) %collective-permute-start.5) | collective-permute-done | bytes 163872 | tf_op jit(solution)/shard_map/ppermute | solution.py:370
  51.8 3.3 %collective-permute-done.7.other = bf16[64,1280]{1,0:T(8,128)(2,1)S(1)} collective-permute-done((bf16[64,1280]{1,0:T(8,128)(2,1)S(1)}, bf16[64,1280]{1,0:T(8,128)(2,1)S(1)}, u32[]{:S(2)}, u32[]{:S(2)}) %collective-permute-start.7) | collective-permute-done | bytes 163872 | tf_op jit(solution)/shard_map/ppermute | solution.py:370
  55.1 2.7 %collective-permute-start.8 = (bf16[64,1280]{1,0:T(8,128)(2,1)S(1)}, bf16[64,1280]{1,0:T(8,128)(2,1)S(1)}, u32[]{:S(2)}, u32[]{:S(2)}) collective-permute-start(bf16[64,1280]{1,0:T(8,128)(2,1)S(1)} %pair.2.own), channel_id=1, source_target_pairs={{0,96},{1,7},{2,98},{3,5},{4,100},{5,3},{6,102},{7,1},{8,104},{9,1... | collective-permute-start | bytes 491528 | tf_op jit(solution)/shard_map/ppermute | solution.py:370
  57.8 2.8 %collective-permute-done.8.other = bf16[64,1280]{1,0:T(8,128)(2,1)S(1)} collective-permute-done((bf16[64,1280]{1,0:T(8,128)(2,1)S(1)}, bf16[64,1280]{1,0:T(8,128)(2,1)S(1)}, u32[]{:S(2)}, u32[]{:S(2)}) %collective-permute-start.8) | collective-permute-done | bytes 163872 | tf_op jit(solution)/shard_map/ppermute | solution.py:370
  60.6 2.5 %collective-permute-start.11 = (bf16[64,1280]{1,0:T(8,128)(2,1)S(1)}, bf16[64,1280]{1,0:T(8,128)(2,1)S(1)}, u32[]{:S(2)}, u32[]{:S(2)}) collective-permute-start(bf16[64,1280]{1,0:T(8,128)(2,1)S(1)} %pair.3.own), channel_id=1, source_target_pairs={{0,6},{1,25},{2,0},{3,27},{4,2},{5,29},{6,4},{7,31},{8,14},{9,1},{... | collective-permute-start | bytes 491528 | tf_op jit(solution)/shard_map/ppermute | solution.py:370
  64.3 2.9 %collective-permute-done.11.three = bf16[64,1280]{1,0:T(8,128)(2,1)S(1)} collective-permute-done((bf16[64,1280]{1,0:T(8,128)(2,1)S(1)}, bf16[64,1280]{1,0:T(8,128)(2,1)S(1)}, u32[]{:S(2)}, u32[]{:S(2)}) %collective-permute-start.11) | collective-permute-done | bytes 163872 | tf_op jit(solution)/shard_map/ppermute | solution.py:370
  67.2 1.8 %collective-permute-done.10.two = bf16[64,1280]{1,0:T(8,128)(2,1)S(1)} collective-permute-done((bf16[64,1280]{1,0:T(8,128)(2,1)S(1)}, bf16[64,1280]{1,0:T(8,128)(2,1)S(1)}, u32[]{:S(2)}, u32[]{:S(2)}) %collective-permute-start.10) | collective-permute-done | bytes 163872 | tf_op jit(solution)/shard_map/ppermute | solution.py:370
  68.9 1.7 %collective-permute-done.9.one = bf16[64,1280]{1,0:T(8,128)(2,1)S(1)} collective-permute-done((bf16[64,1280]{1,0:T(8,128)(2,1)S(1)}, bf16[64,1280]{1,0:T(8,128)(2,1)S(1)}, u32[]{:S(2)}, u32[]{:S(2)}) %collective-permute-start.9) | collective-permute-done | bytes 163872 | tf_op jit(solution)/shard_map/ppermute | solution.py:370
  70.6 4.5 %collective-permute-start.12 = (bf16[4,64,1280]{2,1,0:T(8,128)(2,1)S(1)}, bf16[4,64,1280]{2,1,0:T(8,128)(2,1)S(1)}, u32[]{:S(2)}, u32[]{:S(2)}) collective-permute-start(bf16[4,64,1280]{2,1,0:T(8,128)(2,1)S(1)} %get-tuple-element.49.refs_0_.refs_3_), channel_id=1, source_target_pairs={{0,1},{1,0},{2,3},{3,2},{4,5},{5,4},{6,7},{7,6},{8,9},{9,8},{10,11... | collective-permute-start | bytes 1966088 | tf_op jit(solution)/shard_map/ppermute | solution.py:370
  75.1 3.0 %collective-permute-start.17 = (bf16[2,64,1280]{2,1,0:T(8,128)(2,1)S(1)}, bf16[2,64,1280]{2,1,0:T(8,128)(2,1)S(1)}, u32[]{:S(2)}, u32[]{:S(2)}) collective-permute-start(bf16[2,64,1280]{2,1,0:T(8,128)(2,1)S(1)} %get-tuple-element.55), channel_id=1, source_target_pairs={{0,24},{1,97},{2,26},{3,99},{4,28},{5,101},{6,30},{7,103},{8,0},{9... | collective-permute-start | bytes 983048 | tf_op jit(solution)/shard_map/ppermute | solution.py:370
  78.1 1.5 %collective-permute-start.16 = (bf16[2,64,1280]{2,1,0:T(8,128)(2,1)S(1)}, bf16[2,64,1280]{2,1,0:T(8,128)(2,1)S(1)}, u32[]{:S(2)}, u32[]{:S(2)}) collective-permute-start(bf16[2,64,1280]{2,1,0:T(8,128)(2,1)S(1)} %get-tuple-element.52), channel_id=1, source_target_pairs={{0,24},{1,97},{2,26},{3,99},{4,28},{5,101},{6,30},{7,103},{8,0},{9... | collective-permute-start | bytes 983048 | tf_op jit(solution)/shard_map/ppermute | solution.py:370
  79.6 3.3 %collective-permute-done.13.refs_3_.refs_4_ = bf16[2,64,1280]{2,1,0:T(8,128)(2,1)S(1)} collective-permute-done((bf16[2,64,1280]{2,1,0:T(8,128)(2,1)S(1)}, bf16[2,64,1280]{2,1,0:T(8,128)(2,1)S(1)}, u32[]{:S(2)}, u32[]{:S(2)}) %collective-permute-start.13) | collective-permute-done | bytes 327712 | tf_op jit(solution)/shard_map/ppermute | solution.py:370
  82.8 2.7 %collective-permute-start.18 = (bf16[2,64,1280]{2,1,0:T(8,128)(2,1)S(1)}, bf16[2,64,1280]{2,1,0:T(8,128)(2,1)S(1)}, u32[]{:S(2)}, u32[]{:S(2)}) collective-permute-start(bf16[2,64,1280]{2,1,0:T(8,128)(2,1)S(1)} %collective-permute-done.17.refs_6_.refs_7_), channel_id=1, source_target_pairs={{0,24},{1,97},{2,26},{3,99},{4,28},{5,101},{6,30},{7,103},{8,0},{9... | collective-permute-start | bytes 983048 | tf_op jit(solution)/shard_map/ppermute | solution.py:370
  85.6 1.7 %collective-permute-start.21 = (bf16[2,64,1280]{2,1,0:T(8,128)(2,1)S(1)}, bf16[2,64,1280]{2,1,0:T(8,128)(2,1)S(1)}, u32[]{:S(2)}, u32[]{:S(2)}) collective-permute-start(bf16[2,64,1280]{2,1,0:T(8,128)(2,1)S(1)} %collective-permute-done.16.refs_5_.refs_6_), channel_id=1, source_target_pairs={{0,1},{1,0},{2,3},{3,2},{4,5},{5,4},{6,7},{7,6},{8,9},{9,8},{10,11... | collective-permute-start | bytes 983048 | tf_op jit(solution)/shard_map/ppermute | solution.py:370
  87.3 2.3 %early.2 = (f32[256,5760]{1,0:T(8,128)}, f32[256,2304]{1,0:T(8,128)}, f32[8,128]{1,0:T(8,128)S(1)}) custom-call(s32[3]{0:T(128)S(1)} %pad_add_fusion.place, bf16[4,64,1280]{2,1,0:T(8,128)(2,1)S(1)} %get-tuple-element.49.refs_0_.refs_3_, bf16[4,64,1280]{2,1,0:T(8,128)(2,1)S(1)} %collective-permute-done.12.refs_1_.refs_10_), custom_call_target="tpu_custom_call" | custom-call | bytes 4000000 | tf_op jit(solution)/shard_map/early/pallas_call | solution.py:489
  92.3 1.9 %early.3 = (f32[256,5760]{1,0:T(8,128)}, f32[256,2304]{1,0:T(8,128)}, f32[8,128]{1,0:T(8,128)S(1)}) custom-call(s32[3]{0:T(128)S(1)} %pad_add_fusion.place, f32[256,5760]{1,0:T(8,128)} %get-tuple-element.50.refs_0_, f32[256,2304]{1,0:T(8,128)} %get-tuple-element.51.refs_1_, ...), custom_call_target="tpu_custom_call", output_to_operand_aliasing={{0}: (1, {}), {1}: (2, {})} | custom-call | bytes 4000000 | tf_op jit(solution)/shard_map/early/pallas_call | solution.py:489
  94.9 6.4 %finish.1 = (f32[8,256]{1,0:T(8,128)}, f32[384,128]{1,0:T(8,128)}, f32[3,256]{1,0:T(4,128)}, f32[256,2304]{1,0:T(8,128)}, f32[384,3456]{1,0:T(8,128)}, /*index=5*/f32[256,5760]{1,0:T(8,128)}, f32[256,2304]{1,0:T(8,128)}) custom-call(s32[3]{0:T(128)S(1)} %pad_add_fusion.place, ...), custom_call_target="tpu_custom_call", output_to_operand_aliasing={{5}: (1, {}), {6}: (2, {})} | custom-call | tf_op jit(solution)/shard_map/finish/pallas_call | solution.py:577
  (61 shorter events, 16.6 us)
Async XLA Ops:
  2.8 2.7 %collective-permute-start = (bf16[2,4,144,128]{3,2,1,0:T(8,128)(2,1)S(1)}, bf16[2,4,144,128]{3,2,1,0:T(8,128)(2,1)S(1)}, u32[]{:S(2)}, u32[]{:S(2)}) collective-permute-start(bf16[2,4,144,128]{3,2,1,0:T(8,128)(2,1)S(1)} %maximum_maximum_fusion.own), channel_id=1, source_target_pairs={{0,1},{1,0},{2,3},{3,2},{4,5},{5,4},{6,7},{7,6},{8,9},{9,8},{10,11... | collective-permute-start | bytes 884744 | tf_op jit(solution)/shard_map/ppermute | solution.py:370
  6.2 7.4 %collective-permute-start.1 = (bf16[5,144,128]{2,1,0:T(8,128)(2,1)S(1)}, bf16[5,144,128]{2,1,0:T(8,128)(2,1)S(1)}, u32[]{:S(2)}, u32[]{:S(2)}) collective-permute-start(bf16[5,144,128]{2,1,0:T(8,128)(2,1)S(1)} %get-tuple-element.37), channel_id=1, source_target_pairs={{0,2},{1,3},{2,4},{3,5},{4,6},{5,7},{6,0},{7,1},{8,10},{9,11},{10,... | collective-permute-start | bytes 552968 | tf_op jit(solution)/shard_map/ppermute | solution.py:370
  7.6 6.0 %collective-permute-start.2 = (bf16[5,144,128]{2,1,0:T(8,128)(2,1)S(1)}, bf16[5,144,128]{2,1,0:T(8,128)(2,1)S(1)}, u32[]{:S(2)}, u32[]{:S(2)}) collective-permute-start(bf16[5,144,128]{2,1,0:T(8,128)(2,1)S(1)} %get-tuple-element.39), channel_id=1, source_target_pairs={{0,6},{1,7},{2,0},{3,1},{4,2},{5,3},{6,4},{7,5},{8,14},{9,15},{10,... | collective-permute-start | bytes 552968 | tf_op jit(solution)/shard_map/ppermute | solution.py:370
  37.8 2.9 %collective-permute-start.3 = (bf16[4,64,1280]{2,1,0:T(8,128)(2,1)S(1)}, bf16[4,64,1280]{2,1,0:T(8,128)(2,1)S(1)}, u32[]{:S(2)}, u32[]{:S(2)}) collective-permute-start(bf16[4,64,1280]{2,1,0:T(8,128)(2,1)S(1)} %get-tuple-element.44), channel_id=1, source_target_pairs={{0,1},{1,0},{2,3},{3,2},{4,5},{5,4},{6,7},{7,6},{8,9},{9,8},{10,11... | collective-permute-start | bytes 1966088 | tf_op jit(solution)/shard_map/ppermute | solution.py:370
  40.8 6.6 %collective-permute-start.4 = (bf16[64,1280]{1,0:T(8,128)(2,1)S(1)}, bf16[64,1280]{1,0:T(8,128)(2,1)S(1)}, u32[]{:S(2)}, u32[]{:S(2)}) collective-permute-start(bf16[64,1280]{1,0:T(8,128)(2,1)S(1)} %get-tuple-element.46), channel_id=1, source_target_pairs={{0,2},{1,33},{2,4},{3,35},{4,6},{5,37},{6,0},{7,39},{8,10},{9,41},... | collective-permute-start | bytes 491528 | tf_op jit(solution)/shard_map/ppermute | solution.py:370
  42.6 7.9 %collective-permute-start.5 = (bf16[64,1280]{1,0:T(8,128)(2,1)S(1)}, bf16[64,1280]{1,0:T(8,128)(2,1)S(1)}, u32[]{:S(2)}, u32[]{:S(2)}) collective-permute-start(bf16[64,1280]{1,0:T(8,128)(2,1)S(1)} %get-tuple-element.47), channel_id=1, source_target_pairs={{0,4},{1,65},{2,6},{3,67},{4,0},{5,69},{6,2},{7,71},{8,12},{9,73},... | collective-permute-start | bytes 491528 | tf_op jit(solution)/shard_map/ppermute | solution.py:370
  45.8 4.6 %collective-permute-start.6 = (bf16[64,1280]{1,0:T(8,128)(2,1)S(1)}, bf16[64,1280]{1,0:T(8,128)(2,1)S(1)}, u32[]{:S(2)}, u32[]{:S(2)}) collective-permute-start(bf16[64,1280]{1,0:T(8,128)(2,1)S(1)} %get-tuple-element.48), channel_id=1, source_target_pairs={{0,6},{1,97},{2,0},{3,99},{4,2},{5,101},{6,4},{7,103},{8,14},{9,10... | collective-permute-start | bytes 491528 | tf_op jit(solution)/shard_map/ppermute | solution.py:370
  50.5 4.5 %collective-permute-start.7 = (bf16[64,1280]{1,0:T(8,128)(2,1)S(1)}, bf16[64,1280]{1,0:T(8,128)(2,1)S(1)}, u32[]{:S(2)}, u32[]{:S(2)}) collective-permute-start(bf16[64,1280]{1,0:T(8,128)(2,1)S(1)} %total.1.own), channel_id=1, source_target_pairs={{0,32},{1,3},{2,34},{3,1},{4,36},{5,7},{6,38},{7,5},{8,40},{9,11},... | collective-permute-start | bytes 491528 | tf_op jit(solution)/shard_map/ppermute | solution.py:370
  55.1 5.5 %collective-permute-start.8 = (bf16[64,1280]{1,0:T(8,128)(2,1)S(1)}, bf16[64,1280]{1,0:T(8,128)(2,1)S(1)}, u32[]{:S(2)}, u32[]{:S(2)}) collective-permute-start(bf16[64,1280]{1,0:T(8,128)(2,1)S(1)} %pair.2.own), channel_id=1, source_target_pairs={{0,96},{1,7},{2,98},{3,5},{4,100},{5,3},{6,102},{7,1},{8,104},{9,1... | collective-permute-start | bytes 491528 | tf_op jit(solution)/shard_map/ppermute | solution.py:370
  60.6 6.6 %collective-permute-start.11 = (bf16[64,1280]{1,0:T(8,128)(2,1)S(1)}, bf16[64,1280]{1,0:T(8,128)(2,1)S(1)}, u32[]{:S(2)}, u32[]{:S(2)}) collective-permute-start(bf16[64,1280]{1,0:T(8,128)(2,1)S(1)} %pair.3.own), channel_id=1, source_target_pairs={{0,6},{1,25},{2,0},{3,27},{4,2},{5,29},{6,4},{7,31},{8,14},{9,1},{... | collective-permute-start | bytes 491528 | tf_op jit(solution)/shard_map/ppermute | solution.py:370
  63.1 5.8 %collective-permute-start.10 = (bf16[64,1280]{1,0:T(8,128)(2,1)S(1)}, bf16[64,1280]{1,0:T(8,128)(2,1)S(1)}, u32[]{:S(2)}, u32[]{:S(2)}) collective-permute-start(bf16[64,1280]{1,0:T(8,128)(2,1)S(1)} %pair.3.own), channel_id=1, source_target_pairs={{0,4},{1,17},{2,6},{3,19},{4,0},{5,21},{6,2},{7,23},{8,12},{9,25},... | collective-permute-start | bytes 491528 | tf_op jit(solution)/shard_map/ppermute | solution.py:370
  63.7 6.9 %collective-permute-start.9 = (bf16[64,1280]{1,0:T(8,128)(2,1)S(1)}, bf16[64,1280]{1,0:T(8,128)(2,1)S(1)}, u32[]{:S(2)}, u32[]{:S(2)}) collective-permute-start(bf16[64,1280]{1,0:T(8,128)(2,1)S(1)} %pair.3.own), channel_id=1, source_target_pairs={{0,2},{1,9},{2,4},{3,11},{4,6},{5,13},{6,0},{7,15},{8,10},{9,17},{... | collective-permute-start | bytes 491528 | tf_op jit(solution)/shard_map/ppermute | solution.py:370
  70.6 16.7 %collective-permute-start.12 = (bf16[4,64,1280]{2,1,0:T(8,128)(2,1)S(1)}, bf16[4,64,1280]{2,1,0:T(8,128)(2,1)S(1)}, u32[]{:S(2)}, u32[]{:S(2)}) collective-permute-start(bf16[4,64,1280]{2,1,0:T(8,128)(2,1)S(1)} %get-tuple-element.49.refs_0_.refs_3_), channel_id=1, source_target_pairs={{0,1},{1,0},{2,3},{3,2},{4,5},{5,4},{6,7},{7,6},{8,9},{9,8},{10,11... | collective-permute-start | bytes 1966088 | tf_op jit(solution)/shard_map/ppermute | solution.py:370
  75.1 7.7 %collective-permute-start.13 = (bf16[2,64,1280]{2,1,0:T(8,128)(2,1)S(1)}, bf16[2,64,1280]{2,1,0:T(8,128)(2,1)S(1)}, u32[]{:S(2)}, u32[]{:S(2)}) collective-permute-start(bf16[2,64,1280]{2,1,0:T(8,128)(2,1)S(1)} %get-tuple-element.52), channel_id=1, source_target_pairs={{0,8},{1,33},{2,10},{3,35},{4,12},{5,37},{6,14},{7,39},{8,16},{9,4... | collective-permute-start | bytes 983048 | tf_op jit(solution)/shard_map/ppermute | solution.py:370
  75.1 7.7 %collective-permute-start.17 = (bf16[2,64,1280]{2,1,0:T(8,128)(2,1)S(1)}, bf16[2,64,1280]{2,1,0:T(8,128)(2,1)S(1)}, u32[]{:S(2)}, u32[]{:S(2)}) collective-permute-start(bf16[2,64,1280]{2,1,0:T(8,128)(2,1)S(1)} %get-tuple-element.55), channel_id=1, source_target_pairs={{0,24},{1,97},{2,26},{3,99},{4,28},{5,101},{6,30},{7,103},{8,0},{9... | collective-permute-start | bytes 983048 | tf_op jit(solution)/shard_map/ppermute | solution.py:370
  78.1 7.5 %collective-permute-start.16 = (bf16[2,64,1280]{2,1,0:T(8,128)(2,1)S(1)}, bf16[2,64,1280]{2,1,0:T(8,128)(2,1)S(1)}, u32[]{:S(2)}, u32[]{:S(2)}) collective-permute-start(bf16[2,64,1280]{2,1,0:T(8,128)(2,1)S(1)} %get-tuple-element.52), channel_id=1, source_target_pairs={{0,24},{1,97},{2,26},{3,99},{4,28},{5,101},{6,30},{7,103},{8,0},{9... | collective-permute-start | bytes 983048 | tf_op jit(solution)/shard_map/ppermute | solution.py:370
  79.5 10.1 %collective-permute-start.15 = (bf16[2,64,1280]{2,1,0:T(8,128)(2,1)S(1)}, bf16[2,64,1280]{2,1,0:T(8,128)(2,1)S(1)}, u32[]{:S(2)}, u32[]{:S(2)}) collective-permute-start(bf16[2,64,1280]{2,1,0:T(8,128)(2,1)S(1)} %get-tuple-element.55), channel_id=1, source_target_pairs={{0,8},{1,33},{2,10},{3,35},{4,12},{5,37},{6,14},{7,39},{8,16},{9,4... | collective-permute-start | bytes 983048 | tf_op jit(solution)/shard_map/ppermute | solution.py:370
  82.8 7.7 %collective-permute-start.14 = (bf16[2,64,1280]{2,1,0:T(8,128)(2,1)S(1)}, bf16[2,64,1280]{2,1,0:T(8,128)(2,1)S(1)}, u32[]{:S(2)}, u32[]{:S(2)}) collective-permute-start(bf16[2,64,1280]{2,1,0:T(8,128)(2,1)S(1)} %collective-permute-done.13.refs_3_.refs_4_), channel_id=1, source_target_pairs={{0,8},{1,33},{2,10},{3,35},{4,12},{5,37},{6,14},{7,39},{8,16},{9,4... | collective-permute-start | bytes 983048 | tf_op jit(solution)/shard_map/ppermute | solution.py:370
  82.8 9.0 %collective-permute-start.18 = (bf16[2,64,1280]{2,1,0:T(8,128)(2,1)S(1)}, bf16[2,64,1280]{2,1,0:T(8,128)(2,1)S(1)}, u32[]{:S(2)}, u32[]{:S(2)}) collective-permute-start(bf16[2,64,1280]{2,1,0:T(8,128)(2,1)S(1)} %collective-permute-done.17.refs_6_.refs_7_), channel_id=1, source_target_pairs={{0,24},{1,97},{2,26},{3,99},{4,28},{5,101},{6,30},{7,103},{8,0},{9... | collective-permute-start | bytes 983048 | tf_op jit(solution)/shard_map/ppermute | solution.py:370
  85.6 6.2 %collective-permute-start.21 = (bf16[2,64,1280]{2,1,0:T(8,128)(2,1)S(1)}, bf16[2,64,1280]{2,1,0:T(8,128)(2,1)S(1)}, u32[]{:S(2)}, u32[]{:S(2)}) collective-permute-start(bf16[2,64,1280]{2,1,0:T(8,128)(2,1)S(1)} %collective-permute-done.16.refs_5_.refs_6_), channel_id=1, source_target_pairs={{0,1},{1,0},{2,3},{3,2},{4,5},{5,4},{6,7},{7,6},{8,9},{9,8},{10,11... | collective-permute-start | bytes 983048 | tf_op jit(solution)/shard_map/ppermute | solution.py:370
  87.3 6.9 %collective-permute-start.19 = (bf16[2,64,1280]{2,1,0:T(8,128)(2,1)S(1)}, bf16[2,64,1280]{2,1,0:T(8,128)(2,1)S(1)}, u32[]{:S(2)}, u32[]{:S(2)}) collective-permute-start(bf16[2,64,1280]{2,1,0:T(8,128)(2,1)S(1)} %collective-permute-done.13.refs_3_.refs_4_), channel_id=1, source_target_pairs={{0,1},{1,0},{2,3},{3,2},{4,5},{5,4},{6,7},{7,6},{8,9},{9,8},{10,11... | collective-permute-start | bytes 983048 | tf_op jit(solution)/shard_map/ppermute | solution.py:370
  89.7 4.6 %collective-permute-start.22 = (bf16[2,64,1280]{2,1,0:T(8,128)(2,1)S(1)}, bf16[2,64,1280]{2,1,0:T(8,128)(2,1)S(1)}, u32[]{:S(2)}, u32[]{:S(2)}) collective-permute-start(bf16[2,64,1280]{2,1,0:T(8,128)(2,1)S(1)} %collective-permute-done.17.refs_6_.refs_7_), channel_id=1, source_target_pairs={{0,1},{1,0},{2,3},{3,2},{4,5},{5,4},{6,7},{7,6},{8,9},{9,8},{10,11... | collective-permute-start | bytes 983048 | tf_op jit(solution)/shard_map/ppermute | solution.py:370
  90.5 3.8 %collective-permute-start.20 = (bf16[2,64,1280]{2,1,0:T(8,128)(2,1)S(1)}, bf16[2,64,1280]{2,1,0:T(8,128)(2,1)S(1)}, u32[]{:S(2)}, u32[]{:S(2)}) collective-permute-start(bf16[2,64,1280]{2,1,0:T(8,128)(2,1)S(1)} %collective-permute-done.15.refs_4_.refs_5_), channel_id=1, source_target_pairs={{0,1},{1,0},{2,3},{3,2},{4,5},{5,4},{6,7},{7,6},{8,9},{9,8},{10,11... | collective-permute-start | bytes 983048 | tf_op jit(solution)/shard_map/ppermute | solution.py:370
  91.8 2.5 %collective-permute-start.23 = (bf16[2,64,1280]{2,1,0:T(8,128)(2,1)S(1)}, bf16[2,64,1280]{2,1,0:T(8,128)(2,1)S(1)}, u32[]{:S(2)}, u32[]{:S(2)}) collective-permute-start(bf16[2,64,1280]{2,1,0:T(8,128)(2,1)S(1)} %collective-permute-done.14.refs_8_), channel_id=1, source_target_pairs={{0,1},{1,0},{2,3},{3,2},{4,5},{5,4},{6,7},{7,6},{8,9},{9,8},{10,11... | collective-permute-start | bytes 983048 | tf_op jit(solution)/shard_map/ppermute | solution.py:370
  (7 other events, 10.0 us)

commit v8 on v7

--- a/solution.py
+++ b/solution.py
@@ -341,12 +341,10 @@
 
 
 def total_kernel(own, one, two, three, out):
-    parts = [v[...].astype(F32) for v in (own, one, two, three)]
-    out[...] = sum(parts[1:], parts[0]).astype(BF)
-
-
-def pair_kernel(own, other, out):
-    out[...] = (own[...].astype(F32) + other[...].astype(F32)).astype(BF)
+    out[...] = (
+        (own[...].astype(F32) + two[...].astype(F32))
+        + (one[...].astype(F32) + three[...].astype(F32))
+    ).astype(BF)
 
 
 def stack_kernel(own, one, two, three, out, half0, half1):
@@ -382,15 +380,6 @@
     return moved(v, where)
 
 
-def across(v, axes, bits):
-    def where(*at):
-        to = list(at)
-        to[axes[at[3]]] ^= bits
-        return to
-
-    return moved(v, where)
-
-
 def to_partner(v):
     return moved(v, lambda z, x, y, c: (z, x, y, 1 - c))
 
@@ -404,8 +393,7 @@
     turns = (1, 2, 3)
     own, *parts = small(split_kernel, (wide, piece, piece, piece), keep, to_partner(send))
     own = small(total_kernel, piece, own, *[along(p, (CHIP, DP), j) for p, j in zip(parts, turns)])
-    for bits in (1, 3):
-        own = small(pair_kernel, piece, own, across(own, (DP, CHIP), bits))
+    own = small(total_kernel, piece, own, *[along(own, (DP, CHIP), j) for j in turns])
     four = jax.ShapeDtypeStruct((4, OQ, WIDE), BF)
     two = jax.ShapeDtypeStruct((2, OQ, WIDE), BF)
     block, half0, half1 = small(
@@ -417,12 +405,18 @@
     far0, far1 = along(behind0, rings, 1), along(ahead1, rings, -1)
     mine = (block, behind0, behind1, ahead0, ahead1, far0, far1)
     theirs = [to_partner(v) for v in mine[:5]]
-    written, token = write_early(place, ((0, 0), (0, 1)), (block, theirs[0]))
+    written, token = write_early(
+        place, ((0, 0), (0, 1), (1, 0), (4, 0)), (block, theirs[0], behind0, ahead1)
+    )
     far0, token = lax.optimization_barrier((far0, token))
     theirs.append(to_partner(far0))
     theirs.append(to_partner(far1))
     written, token = write_early(
-        place, ((1, 0), (2, 0), (3, 0), (4, 0)), mine[1:5], written, token
+        place,
+        ((2, 0), (3, 0), (1, 1), (4, 1)),
+        (behind1, ahead0, theirs[1], theirs[4]),
+        written,
+        token,
     )
     return mine[:5] + (far0, far1), theirs, (*written, token)
 
@@ -507,7 +501,7 @@
     return written, token
 
 
-LATE = ((1, 1), (2, 1), (3, 1), (4, 1), (5, 0), (6, 0), (5, 1), (6, 1))
+LATE = ((2, 1), (3, 1), (5, 0), (6, 0), (5, 1), (6, 1))
 
 
 def finish_kernel(place, *refs):
@@ -588,14 +582,14 @@
         in_specs=[smem] + [hbm] * 2 + [vmem] * (5 + len(parts)),
         out_specs=(vmem,) * 3 + (hbm,) * 4,
         scratch_shapes=[
-            pltpu.VMEM((16, OQ, WIDE), F32),
+            pltpu.VMEM((12, OQ, WIDE), F32),
             pltpu.VMEM((MIX, 2 * WIDE), BF),
             pltpu.VMEM((MESO, 9 * MESO), F32),
             pltpu.VMEM((TERR, 9 * TERR), F32),
             pltpu.VMEM((MESO, 9 * LEV), BF),
             pltpu.VMEM((MIX, 256), F32),
             pltpu.SemaphoreType.DMA((18,)),
-            pltpu.SemaphoreType.DMA((32,)),
+            pltpu.SemaphoreType.DMA((24,)),
         ],
         input_output_aliases={1: 5, 2: 6},
         compiler_params=params(36),

time: 102 us -> 101 us (level)
  starting transfers between devices: 34.7 us -> 33 us
    ppermute x25 -> x26, starting transfers between devices: 34.7 us -> 33 us  [moved(): return lax.ppermute(v, ('dp', 'segment', 'space'), pairs)]
    ppermute x25 -> x26, waiting for transfers between devices: 24.8 us -> 25.7 us  [moved(): return lax.ppermute(v, ('dp', 'segment', 'space'), pairs)]
  transfers between devices with their start and end apart: 25 -> 26, of which waited for: 13 -> 12; matrix products, arithmetic and copies ran while one was open for 0% -> 0% of each run, Pallas kernels for 4% -> 5%
where the time goes in v8:
time: 101 us
  Pallas kernels  36.1 us (36%)
  starting transfers between devices  33 us (33%)
  waiting for transfers between devices  25.7 us (25%)
  local copies, waits for them, and re-layouts  4.66 us (5%)
    ppermute x26, starting transfers between devices, moved(): return lax.ppermute(v, ('dp', 'segment', 'space'), pairs)  33 us
    ppermute x26, waiting for transfers between devices, moved(): return lax.ppermute(v, ('dp', 'segment', 'space'), pairs)  25.7 us
    pallas_call x1, Pallas kernels, main(): pl.pallas_call(main_kernel, out_shape=(jax.ShapeDtypeStruct((4, OQ, WIDE)...  24.2 us
    pallas_call x1, Pallas kernels, finish(): pl.pallas_call(finish_kernel, out_shape=(jax.ShapeDtypeStruct((8, TERR),...  5.96 us
    pallas_call x2, Pallas kernels, write_early(): pl.pallas_call(functools.partial(early_kernel, which, len(old)), out_shap...  4.82 us
    unnamed x14, local copies, waits for them, and re-layouts  4.55 us
  transfers between devices with their start and end apart: 26, of which 12 were waited for; matrix products, arithmetic and copies ran while one was open for 0% of the time, Pallas kernels for 5%

profile of v8, /device:TPU:1, one launch (start us, length us, event | category | flops | bytes accessed | tf_op | source)
XLA Modules:
  0.0 100.8 jit_solution(3765197606131620002)
XLA Ops:
  2.8 1.5 %collective-permute-start = (bf16[2,4,144,128]{3,2,1,0:T(8,128)(2,1)S(1)}, bf16[2,4,144,128]{3,2,1,0:T(8,128)(2,1)S(1)}, u32[]{:S(2)}, u32[]{:S(2)}) collective-permute-start(bf16[2,4,144,128]{3,2,1,0:T(8,128)(2,1)S(1)} %maximum_maximum_fusion.own), channel_id=1, source_target_pairs={{0,1},{1,0},{2,3},{3,2},{4,5},{5,4},{6,7},{7,6},{8,9},{9,8},{10,11... | collective-permute-start | bytes 884744 | tf_op jit(solution)/shard_map/ppermute | solution.py:368
  7.6 1.5 %collective-permute-start.2 = (bf16[5,144,128]{2,1,0:T(8,128)(2,1)S(1)}, bf16[5,144,128]{2,1,0:T(8,128)(2,1)S(1)}, u32[]{:S(2)}, u32[]{:S(2)}) collective-permute-start(bf16[5,144,128]{2,1,0:T(8,128)(2,1)S(1)} %get-tuple-element.39), channel_id=1, source_target_pairs={{0,6},{1,7},{2,0},{3,1},{4,2},{5,3},{6,4},{7,5},{8,14},{9,15},{10,... | collective-permute-start | bytes 552968 | tf_op jit(solution)/shard_map/ppermute | solution.py:368
  11.5 2.1 %collective-permute-done.1.above = bf16[5,144,128]{2,1,0:T(8,128)(2,1)S(1)} collective-permute-done((bf16[5,144,128]{2,1,0:T(8,128)(2,1)S(1)}, bf16[5,144,128]{2,1,0:T(8,128)(2,1)S(1)}, u32[]{:S(2)}, u32[]{:S(2)}) %collective-permute-start.1) | collective-permute-done | bytes 184352 | tf_op jit(solution)/shard_map/ppermute | solution.py:368
  13.6 24.2 %sections.1 = (bf16[4,64,1280]{2,1,0:T(8,128)(2,1)S(1)}, bf16[4,64,1280]{2,1,0:T(8,128)(2,1)S(1)}) custom-call(s32[3]{0:T(128)S(1)} %pad_add_fusion.place, bf16[5,144,128]{2,1,0:T(8,128)(2,1)S(1)} %collective-permute-done.1.above, bf16[8,144,128]{2,1,0:T(8,128)(2,1)S(1)} %get-tuple-element.38.eight, bf16[5,144,128]{2,1,0:T(8,128)(2,1)S(1)} %collective-permute-done.2.below, ...), custom_call_target="tpu_custom_call" | custom-call | flops 15000000512 | bytes 12000000 | tf_op jit(solution)/shard_map/sections/pallas_call | solution.py:305
  39.0 1.7 %collective-permute-done.3.came = bf16[4,64,1280]{2,1,0:T(8,128)(2,1)S(1)} collective-permute-done((bf16[4,64,1280]{2,1,0:T(8,128)(2,1)S(1)}, bf16[4,64,1280]{2,1,0:T(8,128)(2,1)S(1)}, u32[]{:S(2)}, u32[]{:S(2)}) %collective-permute-start.3) | collective-permute-done | bytes 655392 | tf_op jit(solution)/shard_map/ppermute | solution.py:368
  40.8 1.7 %collective-permute-start.4 = (bf16[64,1280]{1,0:T(8,128)(2,1)S(1)}, bf16[64,1280]{1,0:T(8,128)(2,1)S(1)}, u32[]{:S(2)}, u32[]{:S(2)}) collective-permute-start(bf16[64,1280]{1,0:T(8,128)(2,1)S(1)} %get-tuple-element.46), channel_id=1, source_target_pairs={{0,2},{1,33},{2,4},{3,35},{4,6},{5,37},{6,0},{7,39},{8,10},{9,41},... | collective-permute-start | bytes 491528 | tf_op jit(solution)/shard_map/ppermute | solution.py:368
  42.6 3.3 %collective-permute-start.5 = (bf16[64,1280]{1,0:T(8,128)(2,1)S(1)}, bf16[64,1280]{1,0:T(8,128)(2,1)S(1)}, u32[]{:S(2)}, u32[]{:S(2)}) collective-permute-start(bf16[64,1280]{1,0:T(8,128)(2,1)S(1)} %get-tuple-element.47), channel_id=1, source_target_pairs={{0,4},{1,65},{2,6},{3,67},{4,0},{5,69},{6,2},{7,71},{8,12},{9,73},... | collective-permute-start | bytes 491528 | tf_op jit(solution)/shard_map/ppermute | solution.py:368
  47.4 3.0 %collective-permute-done.5.two = bf16[64,1280]{1,0:T(8,128)(2,1)S(1)} collective-permute-done((bf16[64,1280]{1,0:T(8,128)(2,1)S(1)}, bf16[64,1280]{1,0:T(8,128)(2,1)S(1)}, u32[]{:S(2)}, u32[]{:S(2)}) %collective-permute-start.5) | collective-permute-done | bytes 163872 | tf_op jit(solution)/shard_map/ppermute | solution.py:368
  50.5 2.7 %collective-permute-start.9 = (bf16[64,1280]{1,0:T(8,128)(2,1)S(1)}, bf16[64,1280]{1,0:T(8,128)(2,1)S(1)}, u32[]{:S(2)}, u32[]{:S(2)}) collective-permute-start(bf16[64,1280]{1,0:T(8,128)(2,1)S(1)} %total.2.own), channel_id=1, source_target_pairs={{0,96},{1,7},{2,98},{3,1},{4,100},{5,3},{6,102},{7,5},{8,104},{9,1... | collective-permute-start | bytes 491528 | tf_op jit(solution)/shard_map/ppermute | solution.py:368
  53.9 3.3 %collective-permute-done.9.three = bf16[64,1280]{1,0:T(8,128)(2,1)S(1)} collective-permute-done((bf16[64,1280]{1,0:T(8,128)(2,1)S(1)}, bf16[64,1280]{1,0:T(8,128)(2,1)S(1)}, u32[]{:S(2)}, u32[]{:S(2)}) %collective-permute-start.9) | collective-permute-done | bytes 163872 | tf_op jit(solution)/shard_map/ppermute | solution.py:368
  57.2 1.8 %collective-permute-done.8.two = bf16[64,1280]{1,0:T(8,128)(2,1)S(1)} collective-permute-done((bf16[64,1280]{1,0:T(8,128)(2,1)S(1)}, bf16[64,1280]{1,0:T(8,128)(2,1)S(1)}, u32[]{:S(2)}, u32[]{:S(2)}) %collective-permute-start.8) | collective-permute-done | bytes 163872 | tf_op jit(solution)/shard_map/ppermute | solution.py:368
  59.0 1.9 %collective-permute-done.7.one = bf16[64,1280]{1,0:T(8,128)(2,1)S(1)} collective-permute-done((bf16[64,1280]{1,0:T(8,128)(2,1)S(1)}, bf16[64,1280]{1,0:T(8,128)(2,1)S(1)}, u32[]{:S(2)}, u32[]{:S(2)}) %collective-permute-start.7) | collective-permute-done | bytes 163872 | tf_op jit(solution)/shard_map/ppermute | solution.py:368
  61.0 2.6 %collective-permute-start.12 = (bf16[64,1280]{1,0:T(8,128)(2,1)S(1)}, bf16[64,1280]{1,0:T(8,128)(2,1)S(1)}, u32[]{:S(2)}, u32[]{:S(2)}) collective-permute-start(bf16[64,1280]{1,0:T(8,128)(2,1)S(1)} %total.3.own), channel_id=1, source_target_pairs={{0,6},{1,25},{2,0},{3,27},{4,2},{5,29},{6,4},{7,31},{8,14},{9,1},{... | collective-permute-start | bytes 491528 | tf_op jit(solution)/shard_map/ppermute | solution.py:368
  64.7 2.9 %collective-permute-done.12.three = bf16[64,1280]{1,0:T(8,128)(2,1)S(1)} collective-permute-done((bf16[64,1280]{1,0:T(8,128)(2,1)S(1)}, bf16[64,1280]{1,0:T(8,128)(2,1)S(1)}, u32[]{:S(2)}, u32[]{:S(2)}) %collective-permute-start.12) | collective-permute-done | bytes 163872 | tf_op jit(solution)/shard_map/ppermute | solution.py:368
  67.6 1.8 %collective-permute-done.11.two = bf16[64,1280]{1,0:T(8,128)(2,1)S(1)} collective-permute-done((bf16[64,1280]{1,0:T(8,128)(2,1)S(1)}, bf16[64,1280]{1,0:T(8,128)(2,1)S(1)}, u32[]{:S(2)}, u32[]{:S(2)}) %collective-permute-start.11) | collective-permute-done | bytes 163872 | tf_op jit(solution)/shard_map/ppermute | solution.py:368
  69.3 1.9 %collective-permute-done.10.one = bf16[64,1280]{1,0:T(8,128)(2,1)S(1)} collective-permute-done((bf16[64,1280]{1,0:T(8,128)(2,1)S(1)}, bf16[64,1280]{1,0:T(8,128)(2,1)S(1)}, u32[]{:S(2)}, u32[]{:S(2)}) %collective-permute-start.10) | collective-permute-done | bytes 163872 | tf_op jit(solution)/shard_map/ppermute | solution.py:368
  71.4 3.3 %collective-permute-start.13 = (bf16[4,64,1280]{2,1,0:T(8,128)(2,1)S(1)}, bf16[4,64,1280]{2,1,0:T(8,128)(2,1)S(1)}, u32[]{:S(2)}, u32[]{:S(2)}) collective-permute-start(bf16[4,64,1280]{2,1,0:T(8,128)(2,1)S(1)} %get-tuple-element.49.refs_0_.refs_3_), channel_id=1, source_target_pairs={{0,1},{1,0},{2,3},{3,2},{4,5},{5,4},{6,7},{7,6},{8,9},{9,8},{10,11... | collective-permute-start | bytes 1966088 | tf_op jit(solution)/shard_map/ppermute | solution.py:368
  74.7 2.7 %collective-permute-start.15 = (bf16[2,64,1280]{2,1,0:T(8,128)(2,1)S(1)}, bf16[2,64,1280]{2,1,0:T(8,128)(2,1)S(1)}, u32[]{:S(2)}, u32[]{:S(2)}) collective-permute-start(bf16[2,64,1280]{2,1,0:T(8,128)(2,1)S(1)} %get-tuple-element.51), channel_id=1, source_target_pairs={{0,24},{1,97},{2,26},{3,99},{4,28},{5,101},{6,30},{7,103},{8,0},{9... | collective-permute-start | bytes 983048 | tf_op jit(solution)/shard_map/ppermute | solution.py:368
  78.9 3.3 %collective-permute-done.14.refs_2_.refs_4_ = bf16[2,64,1280]{2,1,0:T(8,128)(2,1)S(1)} collective-permute-done((bf16[2,64,1280]{2,1,0:T(8,128)(2,1)S(1)}, bf16[2,64,1280]{2,1,0:T(8,128)(2,1)S(1)}, u32[]{:S(2)}, u32[]{:S(2)}) %collective-permute-start.14) | collective-permute-done | bytes 327712 | tf_op jit(solution)/shard_map/ppermute | solution.py:368
  82.1 2.7 %collective-permute-start.21 = (bf16[2,64,1280]{2,1,0:T(8,128)(2,1)S(1)}, bf16[2,64,1280]{2,1,0:T(8,128)(2,1)S(1)}, u32[]{:S(2)}, u32[]{:S(2)}) collective-permute-start(bf16[2,64,1280]{2,1,0:T(8,128)(2,1)S(1)} %collective-permute-done.15.refs_3_.refs_7_), channel_id=1, source_target_pairs={{0,24},{1,97},{2,26},{3,99},{4,28},{5,101},{6,30},{7,103},{8,0},{9... | collective-permute-start | bytes 983048 | tf_op jit(solution)/shard_map/ppermute | solution.py:368
  86.3 2.7 %early.2 = (f32[256,5760]{1,0:T(8,128)}, f32[256,2304]{1,0:T(8,128)}, f32[8,128]{1,0:T(8,128)S(1)}) custom-call(s32[3]{0:T(128)S(1)} %pad_add_fusion.place, bf16[4,64,1280]{2,1,0:T(8,128)(2,1)S(1)} %get-tuple-element.49.refs_0_.refs_3_, bf16[4,64,1280]{2,1,0:T(8,128)(2,1)S(1)} %collective-permute-done.13.refs_1_.refs_10_, ...), custom_call_target="tpu_custom_call" | custom-call | bytes 4000000 | tf_op jit(solution)/shard_map/early/pallas_call | solution.py:483
  89.6 1.8 %collective-permute-start.22 = (bf16[2,64,1280]{2,1,0:T(8,128)(2,1)S(1)}, bf16[2,64,1280]{2,1,0:T(8,128)(2,1)S(1)}, u32[]{:S(2)}, u32[]{:S(2)}) collective-permute-start(bf16[2,64,1280]{2,1,0:T(8,128)(2,1)S(1)} %collective-permute-done.17.refs_3_.refs_5_), channel_id=1, source_target_pairs={{0,1},{1,0},{2,3},{3,2},{4,5},{5,4},{6,7},{7,6},{8,9},{9,8},{10,11... | collective-permute-start | bytes 983048 | tf_op jit(solution)/shard_map/ppermute | solution.py:368
  91.9 2.1 %early.3 = (f32[256,5760]{1,0:T(8,128)}, f32[256,2304]{1,0:T(8,128)}, f32[8,128]{1,0:T(8,128)S(1)}) custom-call(s32[3]{0:T(128)S(1)} %pad_add_fusion.place, f32[256,5760]{1,0:T(8,128)} %get-tuple-element.52.refs_0_, f32[256,2304]{1,0:T(8,128)} %get-tuple-element.53.refs_1_, ...), custom_call_target="tpu_custom_call", output_to_operand_aliasing={{0}: (1, {}), {1}: (2, {})} | custom-call | bytes 4000000 | tf_op jit(solution)/shard_map/early/pallas_call | solution.py:483
  94.7 6.0 %finish.1 = (f32[8,256]{1,0:T(8,128)}, f32[384,128]{1,0:T(8,128)}, f32[3,256]{1,0:T(4,128)}, f32[256,2304]{1,0:T(8,128)}, f32[384,3456]{1,0:T(8,128)}, /*index=5*/f32[256,5760]{1,0:T(8,128)}, f32[256,2304]{1,0:T(8,128)}) custom-call(s32[3]{0:T(128)S(1)} %pad_add_fusion.place, ...), custom_call_target="tpu_custom_call", output_to_operand_aliasing={{5}: (1, {}), {6}: (2, {})} | custom-call | tf_op jit(solution)/shard_map/finish/pallas_call | solution.py:571
  (62 shorter events, 17.5 us)
Async XLA Ops:
  2.8 2.7 %collective-permute-start = (bf16[2,4,144,128]{3,2,1,0:T(8,128)(2,1)S(1)}, bf16[2,4,144,128]{3,2,1,0:T(8,128)(2,1)S(1)}, u32[]{:S(2)}, u32[]{:S(2)}) collective-permute-start(bf16[2,4,144,128]{3,2,1,0:T(8,128)(2,1)S(1)} %maximum_maximum_fusion.own), channel_id=1, source_target_pairs={{0,1},{1,0},{2,3},{3,2},{4,5},{5,4},{6,7},{7,6},{8,9},{9,8},{10,11... | collective-permute-start | bytes 884744 | tf_op jit(solution)/shard_map/ppermute | solution.py:368
  6.2 7.4 %collective-permute-start.1 = (bf16[5,144,128]{2,1,0:T(8,128)(2,1)S(1)}, bf16[5,144,128]{2,1,0:T(8,128)(2,1)S(1)}, u32[]{:S(2)}, u32[]{:S(2)}) collective-permute-start(bf16[5,144,128]{2,1,0:T(8,128)(2,1)S(1)} %get-tuple-element.37), channel_id=1, source_target_pairs={{0,2},{1,3},{2,4},{3,5},{4,6},{5,7},{6,0},{7,1},{8,10},{9,11},{10,... | collective-permute-start | bytes 552968 | tf_op jit(solution)/shard_map/ppermute | solution.py:368
  7.6 6.0 %collective-permute-start.2 = (bf16[5,144,128]{2,1,0:T(8,128)(2,1)S(1)}, bf16[5,144,128]{2,1,0:T(8,128)(2,1)S(1)}, u32[]{:S(2)}, u32[]{:S(2)}) collective-permute-start(bf16[5,144,128]{2,1,0:T(8,128)(2,1)S(1)} %get-tuple-element.39), channel_id=1, source_target_pairs={{0,6},{1,7},{2,0},{3,1},{4,2},{5,3},{6,4},{7,5},{8,14},{9,15},{10,... | collective-permute-start | bytes 552968 | tf_op jit(solution)/shard_map/ppermute | solution.py:368
  37.8 2.9 %collective-permute-start.3 = (bf16[4,64,1280]{2,1,0:T(8,128)(2,1)S(1)}, bf16[4,64,1280]{2,1,0:T(8,128)(2,1)S(1)}, u32[]{:S(2)}, u32[]{:S(2)}) collective-permute-start(bf16[4,64,1280]{2,1,0:T(8,128)(2,1)S(1)} %get-tuple-element.44), channel_id=1, source_target_pairs={{0,1},{1,0},{2,3},{3,2},{4,5},{5,4},{6,7},{7,6},{8,9},{9,8},{10,11... | collective-permute-start | bytes 1966088 | tf_op jit(solution)/shard_map/ppermute | solution.py:368
  40.8 6.6 %collective-permute-start.4 = (bf16[64,1280]{1,0:T(8,128)(2,1)S(1)}, bf16[64,1280]{1,0:T(8,128)(2,1)S(1)}, u32[]{:S(2)}, u32[]{:S(2)}) collective-permute-start(bf16[64,1280]{1,0:T(8,128)(2,1)S(1)} %get-tuple-element.46), channel_id=1, source_target_pairs={{0,2},{1,33},{2,4},{3,35},{4,6},{5,37},{6,0},{7,39},{8,10},{9,41},... | collective-permute-start | bytes 491528 | tf_op jit(solution)/shard_map/ppermute | solution.py:368
  42.6 7.9 %collective-permute-start.5 = (bf16[64,1280]{1,0:T(8,128)(2,1)S(1)}, bf16[64,1280]{1,0:T(8,128)(2,1)S(1)}, u32[]{:S(2)}, u32[]{:S(2)}) collective-permute-start(bf16[64,1280]{1,0:T(8,128)(2,1)S(1)} %get-tuple-element.47), channel_id=1, source_target_pairs={{0,4},{1,65},{2,6},{3,67},{4,0},{5,69},{6,2},{7,71},{8,12},{9,73},... | collective-permute-start | bytes 491528 | tf_op jit(solution)/shard_map/ppermute | solution.py:368
  45.8 4.6 %collective-permute-start.6 = (bf16[64,1280]{1,0:T(8,128)(2,1)S(1)}, bf16[64,1280]{1,0:T(8,128)(2,1)S(1)}, u32[]{:S(2)}, u32[]{:S(2)}) collective-permute-start(bf16[64,1280]{1,0:T(8,128)(2,1)S(1)} %get-tuple-element.48), channel_id=1, source_target_pairs={{0,6},{1,97},{2,0},{3,99},{4,2},{5,101},{6,4},{7,103},{8,14},{9,10... | collective-permute-start | bytes 491528 | tf_op jit(solution)/shard_map/ppermute | solution.py:368
  50.5 6.7 %collective-permute-start.9 = (bf16[64,1280]{1,0:T(8,128)(2,1)S(1)}, bf16[64,1280]{1,0:T(8,128)(2,1)S(1)}, u32[]{:S(2)}, u32[]{:S(2)}) collective-permute-start(bf16[64,1280]{1,0:T(8,128)(2,1)S(1)} %total.2.own), channel_id=1, source_target_pairs={{0,96},{1,7},{2,98},{3,1},{4,100},{5,3},{6,102},{7,5},{8,104},{9,1... | collective-permute-start | bytes 491528 | tf_op jit(solution)/shard_map/ppermute | solution.py:368
  53.2 5.8 %collective-permute-start.8 = (bf16[64,1280]{1,0:T(8,128)(2,1)S(1)}, bf16[64,1280]{1,0:T(8,128)(2,1)S(1)}, u32[]{:S(2)}, u32[]{:S(2)}) collective-permute-start(bf16[64,1280]{1,0:T(8,128)(2,1)S(1)} %total.2.own), channel_id=1, source_target_pairs={{0,64},{1,5},{2,66},{3,7},{4,68},{5,1},{6,70},{7,3},{8,72},{9,13},... | collective-permute-start | bytes 491528 | tf_op jit(solution)/shard_map/ppermute | solution.py:368
  53.5 7.4 %collective-permute-start.7 = (bf16[64,1280]{1,0:T(8,128)(2,1)S(1)}, bf16[64,1280]{1,0:T(8,128)(2,1)S(1)}, u32[]{:S(2)}, u32[]{:S(2)}) collective-permute-start(bf16[64,1280]{1,0:T(8,128)(2,1)S(1)} %total.2.own), channel_id=1, source_target_pairs={{0,32},{1,3},{2,34},{3,5},{4,36},{5,7},{6,38},{7,1},{8,40},{9,11},... | collective-permute-start | bytes 491528 | tf_op jit(solution)/shard_map/ppermute | solution.py:368
  61.0 6.6 %collective-permute-start.12 = (bf16[64,1280]{1,0:T(8,128)(2,1)S(1)}, bf16[64,1280]{1,0:T(8,128)(2,1)S(1)}, u32[]{:S(2)}, u32[]{:S(2)}) collective-permute-start(bf16[64,1280]{1,0:T(8,128)(2,1)S(1)} %total.3.own), channel_id=1, source_target_pairs={{0,6},{1,25},{2,0},{3,27},{4,2},{5,29},{6,4},{7,31},{8,14},{9,1},{... | collective-permute-start | bytes 491528 | tf_op jit(solution)/shard_map/ppermute | solution.py:368
  63.6 5.8 %collective-permute-start.11 = (bf16[64,1280]{1,0:T(8,128)(2,1)S(1)}, bf16[64,1280]{1,0:T(8,128)(2,1)S(1)}, u32[]{:S(2)}, u32[]{:S(2)}) collective-permute-start(bf16[64,1280]{1,0:T(8,128)(2,1)S(1)} %total.3.own), channel_id=1, source_target_pairs={{0,4},{1,17},{2,6},{3,19},{4,0},{5,21},{6,2},{7,23},{8,12},{9,25},... | collective-permute-start | bytes 491528 | tf_op jit(solution)/shard_map/ppermute | solution.py:368
  64.1 7.2 %collective-permute-start.10 = (bf16[64,1280]{1,0:T(8,128)(2,1)S(1)}, bf16[64,1280]{1,0:T(8,128)(2,1)S(1)}, u32[]{:S(2)}, u32[]{:S(2)}) collective-permute-start(bf16[64,1280]{1,0:T(8,128)(2,1)S(1)} %total.3.own), channel_id=1, source_target_pairs={{0,2},{1,9},{2,4},{3,11},{4,6},{5,13},{6,0},{7,15},{8,10},{9,17},{... | collective-permute-start | bytes 491528 | tf_op jit(solution)/shard_map/ppermute | solution.py:368
  71.4 13.5 %collective-permute-start.13 = (bf16[4,64,1280]{2,1,0:T(8,128)(2,1)S(1)}, bf16[4,64,1280]{2,1,0:T(8,128)(2,1)S(1)}, u32[]{:S(2)}, u32[]{:S(2)}) collective-permute-start(bf16[4,64,1280]{2,1,0:T(8,128)(2,1)S(1)} %get-tuple-element.49.refs_0_.refs_3_), channel_id=1, source_target_pairs={{0,1},{1,0},{2,3},{3,2},{4,5},{5,4},{6,7},{7,6},{8,9},{9,8},{10,11... | collective-permute-start | bytes 1966088 | tf_op jit(solution)/shard_map/ppermute | solution.py:368
  74.7 7.4 %collective-permute-start.14 = (bf16[2,64,1280]{2,1,0:T(8,128)(2,1)S(1)}, bf16[2,64,1280]{2,1,0:T(8,128)(2,1)S(1)}, u32[]{:S(2)}, u32[]{:S(2)}) collective-permute-start(bf16[2,64,1280]{2,1,0:T(8,128)(2,1)S(1)} %get-tuple-element.50), channel_id=1, source_target_pairs={{0,8},{1,33},{2,10},{3,35},{4,12},{5,37},{6,14},{7,39},{8,16},{9,4... | collective-permute-start | bytes 983048 | tf_op jit(solution)/shard_map/ppermute | solution.py:368
  74.7 7.4 %collective-permute-start.15 = (bf16[2,64,1280]{2,1,0:T(8,128)(2,1)S(1)}, bf16[2,64,1280]{2,1,0:T(8,128)(2,1)S(1)}, u32[]{:S(2)}, u32[]{:S(2)}) collective-permute-start(bf16[2,64,1280]{2,1,0:T(8,128)(2,1)S(1)} %get-tuple-element.51), channel_id=1, source_target_pairs={{0,24},{1,97},{2,26},{3,99},{4,28},{5,101},{6,30},{7,103},{8,0},{9... | collective-permute-start | bytes 983048 | tf_op jit(solution)/shard_map/ppermute | solution.py:368
  77.4 11.6 %collective-permute-start.18 = (bf16[2,64,1280]{2,1,0:T(8,128)(2,1)S(1)}, bf16[2,64,1280]{2,1,0:T(8,128)(2,1)S(1)}, u32[]{:S(2)}, u32[]{:S(2)}) collective-permute-start(bf16[2,64,1280]{2,1,0:T(8,128)(2,1)S(1)} %get-tuple-element.50), channel_id=1, source_target_pairs={{0,24},{1,97},{2,26},{3,99},{4,28},{5,101},{6,30},{7,103},{8,0},{9... | collective-permute-start | bytes 983048 | tf_op jit(solution)/shard_map/ppermute | solution.py:368
  77.4 11.9 %collective-permute-start.17 = (bf16[2,64,1280]{2,1,0:T(8,128)(2,1)S(1)}, bf16[2,64,1280]{2,1,0:T(8,128)(2,1)S(1)}, u32[]{:S(2)}, u32[]{:S(2)}) collective-permute-start(bf16[2,64,1280]{2,1,0:T(8,128)(2,1)S(1)} %get-tuple-element.51), channel_id=1, source_target_pairs={{0,8},{1,33},{2,10},{3,35},{4,12},{5,37},{6,14},{7,39},{8,16},{9,4... | collective-permute-start | bytes 983048 | tf_op jit(solution)/shard_map/ppermute | solution.py:368
  82.1 7.5 %collective-permute-start.16 = (bf16[2,64,1280]{2,1,0:T(8,128)(2,1)S(1)}, bf16[2,64,1280]{2,1,0:T(8,128)(2,1)S(1)}, u32[]{:S(2)}, u32[]{:S(2)}) collective-permute-start(bf16[2,64,1280]{2,1,0:T(8,128)(2,1)S(1)} %collective-permute-done.14.refs_2_.refs_4_), channel_id=1, source_target_pairs={{0,8},{1,33},{2,10},{3,35},{4,12},{5,37},{6,14},{7,39},{8,16},{9,4... | collective-permute-start | bytes 983048 | tf_op jit(solution)/shard_map/ppermute | solution.py:368
  82.1 9.2 %collective-permute-start.21 = (bf16[2,64,1280]{2,1,0:T(8,128)(2,1)S(1)}, bf16[2,64,1280]{2,1,0:T(8,128)(2,1)S(1)}, u32[]{:S(2)}, u32[]{:S(2)}) collective-permute-start(bf16[2,64,1280]{2,1,0:T(8,128)(2,1)S(1)} %collective-permute-done.15.refs_3_.refs_7_), channel_id=1, source_target_pairs={{0,24},{1,97},{2,26},{3,99},{4,28},{5,101},{6,30},{7,103},{8,0},{9... | collective-permute-start | bytes 983048 | tf_op jit(solution)/shard_map/ppermute | solution.py:368
  84.8 6.6 %collective-permute-start.19 = (bf16[2,64,1280]{2,1,0:T(8,128)(2,1)S(1)}, bf16[2,64,1280]{2,1,0:T(8,128)(2,1)S(1)}, u32[]{:S(2)}, u32[]{:S(2)}) collective-permute-start(bf16[2,64,1280]{2,1,0:T(8,128)(2,1)S(1)} %collective-permute-done.14.refs_2_.refs_4_), channel_id=1, source_target_pairs={{0,1},{1,0},{2,3},{3,2},{4,5},{5,4},{6,7},{7,6},{8,9},{9,8},{10,11... | collective-permute-start | bytes 983048 | tf_op jit(solution)/shard_map/ppermute | solution.py:368
  89.0 2.9 %collective-permute-start.20 = (bf16[2,64,1280]{2,1,0:T(8,128)(2,1)S(1)}, bf16[2,64,1280]{2,1,0:T(8,128)(2,1)S(1)}, u32[]{:S(2)}, u32[]{:S(2)}) collective-permute-start(bf16[2,64,1280]{2,1,0:T(8,128)(2,1)S(1)} %collective-permute-done.15.refs_3_.refs_7_), channel_id=1, source_target_pairs={{0,1},{1,0},{2,3},{3,2},{4,5},{5,4},{6,7},{7,6},{8,9},{9,8},{10,11... | collective-permute-start | bytes 983048 | tf_op jit(solution)/shard_map/ppermute | solution.py:368
  89.3 4.7 %collective-permute-start.23 = (bf16[2,64,1280]{2,1,0:T(8,128)(2,1)S(1)}, bf16[2,64,1280]{2,1,0:T(8,128)(2,1)S(1)}, u32[]{:S(2)}, u32[]{:S(2)}) collective-permute-start(bf16[2,64,1280]{2,1,0:T(8,128)(2,1)S(1)} %collective-permute-done.18.refs_4_.refs_6_), channel_id=1, source_target_pairs={{0,1},{1,0},{2,3},{3,2},{4,5},{5,4},{6,7},{7,6},{8,9},{9,8},{10,11... | collective-permute-start | bytes 983048 | tf_op jit(solution)/shard_map/ppermute | solution.py:368
  89.6 4.4 %collective-permute-start.22 = (bf16[2,64,1280]{2,1,0:T(8,128)(2,1)S(1)}, bf16[2,64,1280]{2,1,0:T(8,128)(2,1)S(1)}, u32[]{:S(2)}, u32[]{:S(2)}) collective-permute-start(bf16[2,64,1280]{2,1,0:T(8,128)(2,1)S(1)} %collective-permute-done.17.refs_3_.refs_5_), channel_id=1, source_target_pairs={{0,1},{1,0},{2,3},{3,2},{4,5},{5,4},{6,7},{7,6},{8,9},{9,8},{10,11... | collective-permute-start | bytes 983048 | tf_op jit(solution)/shard_map/ppermute | solution.py:368
  (8 other events, 13.3 us)
